TPU v7x, 32 devices: a whole 2x2x4 slice. The times are simulated.
32 devices in a mesh: pop: 8 (over z, core), mp: 4 (over y, x).
Axes of the slice: x: 2, y: 2, z: 4, core: 2. Of those that a mesh axis runs over, the one named last changes fastest.
Arguments:
- prompts: bfloat16 [32, 128, 4096], P('pop'), may hold values from -9 to 9
- gate_weight: bfloat16 [4096, 8192], P('pop', 'mp'), may hold values from -0.09375 to 0.09375
- up_weight: bfloat16 [4096, 8192], P('pop', 'mp'), may hold values from -0.09375 to 0.09375
- reward_head: bfloat16 [8192], P('mp'), may hold values from -0.0625 to 0.0625
- member_seeds: int32 [32], P('pop'), may hold values from 0 to 1073741823
- counters: int32 [32], P('pop'), may hold values from 0 to 65535
- member_ranks: int32 [32], P('pop'), may hold values from 0 to 31, each once
Outputs:
- new_gate: bfloat16 [4096, 8192], P('pop', 'mp')
- new_up: bfloat16 [4096, 8192], P('pop', 'mp')
- scores: float32 [32], P('pop')
All inputs are finite; a program needn't handle non-finite values.
Results may differ from a plain program's by a relative error of at most 0.014.
Values may be sent and summed in bfloat16 or wider, within the bound.
No kernel may reach another device: no remote copies, remote signals or barrier semaphores. Data moves between devices by JAX's collectives and lax.ppermute only.
A program may use at most 128 MiB of HBM per device.

v0:
```python
import jax
import jax.numpy as jnp
from jax import lax
from jax.sharding import PartitionSpec as P

sigma_perturb = 0.004
learn_rate = 0.0016


def shift_down(number, amount):
    return lax.shift_right_logical(number, jnp.full_like(number, amount))


def mix_bits(number):
    number = number ^ shift_down(number, 16)
    number = number * 2146121005
    number = number ^ shift_down(number, 15)
    number = number * -2073254261
    return number ^ shift_down(number, 16)


def factor_rows(seed_list, counter_list, slot, positions):
    anchor = mix_bits(
        seed_list * 1103515245 + mix_bits(counter_list * 668265263 + slot * 374761393)
    )
    hashed = mix_bits(anchor[:, None] + positions[None, :] * -1640531535)
    uniform_part = shift_down(hashed, 8).astype(jnp.float32) * (1.0 / 16777216.0)
    return (2.0 * uniform_part - 1.0 + 1.0 / 16777216.0) * 1.7320508075688772


def shards(prompts, gate_weight, up_weight, reward_head, member_seeds, counters, member_ranks):
    members_here, seq_len, width = prompts.shape
    own_rows, own_cols = gate_weight.shape
    pop_index = lax.axis_index("pop")
    mp_index = lax.axis_index("mp")
    row_start = pop_index * own_rows
    column_ids = mp_index * own_cols + jnp.arange(own_cols, dtype=jnp.int32)
    all_seeds, all_counters, all_ranks = (
        lax.all_gather(member_seeds, "pop", axis=0, tiled=True),
        lax.all_gather(counters, "pop", axis=0, tiled=True),
        lax.all_gather(member_ranks, "pop", axis=0, tiled=True),
    )
    members_all = all_seeds.shape[0]
    fitness = (all_ranks.astype(jnp.float32) + 0.5) / members_all - 0.5
    scaling = learn_rate / (members_all * sigma_perturb)
    right_gate = factor_rows(all_seeds, all_counters, 1, column_ids).astype(jnp.bfloat16)
    right_up = factor_rows(all_seeds, all_counters, 3, column_ids).astype(jnp.bfloat16)

    def fresh_rows(weight_rows, first_row, slot, right_factor):
        row_ids = first_row + jnp.arange(weight_rows.shape[0], dtype=jnp.int32)
        left_factor = (
            factor_rows(all_seeds, all_counters, slot, row_ids) * fitness[:, None]
        ).astype(jnp.bfloat16)
        update_term = scaling * jnp.dot(
            left_factor.T, right_factor, preferred_element_type=jnp.float32
        )
        return (weight_rows.astype(jnp.float32) + update_term).astype(jnp.bfloat16)

    new_gate = fresh_rows(gate_weight, row_start, 0, right_gate)
    new_up = fresh_rows(up_weight, row_start, 2, right_up)
    flat_rows = prompts.reshape(members_here * seq_len, width)
    gate_base = jnp.dot(
        flat_rows,
        lax.all_gather(new_gate, "pop", axis=0, tiled=True),
        preferred_element_type=jnp.float32,
    )
    up_base = jnp.dot(
        flat_rows,
        lax.all_gather(new_up, "pop", axis=0, tiled=True),
        preferred_element_type=jnp.float32,
    )
    later = counters + 1
    all_positions = jnp.arange(width, dtype=jnp.int32)
    gate_vec = factor_rows(member_seeds, later, 0, all_positions).astype(jnp.bfloat16)
    gate_col = factor_rows(member_seeds, later, 1, column_ids)
    up_vec = factor_rows(member_seeds, later, 2, all_positions).astype(jnp.bfloat16)
    up_col = factor_rows(member_seeds, later, 3, column_ids)
    gate_proj = jnp.einsum("mld,md->ml", prompts, gate_vec, preferred_element_type=jnp.float32)
    up_proj = jnp.einsum("mld,md->ml", prompts, up_vec, preferred_element_type=jnp.float32)
    gate_value = (
        gate_base.reshape(members_here, seq_len, own_cols)
        + sigma_perturb * gate_proj[:, :, None] * gate_col[:, None, :]
    )
    up_value = (
        up_base.reshape(members_here, seq_len, own_cols)
        + sigma_perturb * up_proj[:, :, None] * up_col[:, None, :]
    )
    hidden = (jax.nn.silu(gate_value) * up_value).astype(jnp.bfloat16)
    partial_reward = jnp.einsum("mlf,f->m", hidden, reward_head, preferred_element_type=jnp.float32)
    summed = lax.psum(partial_reward, "mp")
    all_rewards = lax.all_gather(summed, "pop", axis=0, tiled=True)
    rewards = all_rewards / seq_len
    reward_mean = jnp.mean(rewards)
    reward_var = jnp.mean((rewards - reward_mean) ** 2)
    all_scores = (rewards - reward_mean) / jnp.sqrt(reward_var + 1e-05)
    own_scores = lax.dynamic_slice_in_dim(all_scores, pop_index * members_here, members_here)
    return (new_gate, new_up, own_scores)


def solution(mesh):
    in_specs = (
        P("pop", None, None),
        P("pop", "mp"),
        P("pop", "mp"),
        P("mp"),
        P("pop"),
        P("pop"),
        P("pop"),
    )
    out_specs = (P("pop", "mp"), P("pop", "mp"), P("pop"))
    return jax.shard_map(shards, mesh=mesh, in_specs=in_specs, out_specs=out_specs, check_vma=False)
```

profile of v0, /device:TPU:0, one launch (start us, length us, event | category | flops | bytes accessed | tf_op | source)
XLA Modules:
  0.0 376.3 jit_solution(16224391409295555679)
XLA Ops:
  7.2 0.0 copy-start.4
  7.2 0.0 all-gather.3.cloned.1.call-start
  7.2 1.4 dynamic-slice
  9.3 0.9 dynamic-update-slice
  10.1 0.8 dynamic-update-slice.1
  11.0 0.8 dynamic-update-slice.2
  11.8 10.6 %all-reduce.4 = (s32[32]{0:T(128)S(1)}, s32[32]{0:T(128)S(1)}, s32[32]{0:T(128)S(1)}) all-reduce(s32[32]{0:T(128)S(1)} %dynamic-update-slice, s32[32]{0:T(128)S(1)} %dynamic-update-slice.1, s32[32]{0:T(128)S(1)} %dynamic-update-slice.2), channel_id=1, replica_groups=mesh['pop'=8,'mp'=4] {'pop'}, use_global_device_ids=true, to_apply=%add | all-reduce | flops 96 | bytes 768
  22.5 3.7 add_convert_fusion.1
  26.2 0.0 copy-start.1
  26.2 0.0 copy-start.2
  26.2 0.0 copy-start.3
  26.2 0.0 all-gather.3.cloned.1.call-update
  26.3 0.0 all-gather.5.cloned.1.call-start
  26.3 0.0 copy-done.4
  26.3 2.2 add_convert_fusion
  28.5 0.0 all-gather.5.cloned.1.call-update
  28.5 0.0 copy-done.1
  28.5 0.0 copy-start
  28.6 0.0 copy-done.2
  28.6 0.0 copy-done.3
  28.6 0.2 fusion.76
  28.8 3.5 fusion.68
  32.3 0.0 copy-done
  32.3 1.2 fusion.70
  33.5 0.1 fusion.84
  33.7 142.4 %all-gather.3.cloned.1.call-done = bf16[4096,2048]{1,0:T(8,128)(2,1)} async-done(((bf16[512,2048]{1,0:T(8,128)(2,1)}), bf16[4096,2048]{1,0:T(8,128)(2,1)}) %all-gather.3.cloned.1.call-update) | async-done | bytes 16777232 | tf_op jit(solution)/shard_map/all_gather | solution.py:64
  176.1 15.0 %fusion.169 = f32[2048,512]{0,1:T(8,128)} fusion(bf16[512,4096]{1,0:T(8,128)(2,1)} %bitcast.28, bf16[4096,2048]{1,0:T(8,128)(2,1)} %all-gather.3.cloned.1.call-done), kind=kOutput, calls=%fused_computation.255 | convolution fusion | flops 8589934592 | bytes 25165824 | tf_op jit(solution)/shard_map/dot_general | solution.py:62
  191.0 136.6 %all-gather.5.cloned.1.call-done = bf16[4096,2048]{1,0:T(8,128)(2,1)} async-done(((bf16[512,2048]{1,0:T(8,128)(2,1)}), bf16[4096,2048]{1,0:T(8,128)(2,1)}) %all-gather.5.cloned.1.call-update) | async-done | bytes 16777232 | tf_op jit(solution)/shard_map/all_gather | solution.py:69
  327.6 15.0 %convert_reduce_fusion = bf16[4,2048]{1,0:T(4,128)(2,1)S(1)} fusion(f32[4,2048]{1,0:T(4,128)S(1)} %get-tuple-element.9, f32[4,128]{1,0:T(4,128)S(1)} %get-tuple-element.18, f32[4,2048]{1,0:T(4,128)S(1)} %get-tuple-element.8, f32[4,128]{1,0:T(4,128)S(1)} %get-tuple-element.19, f32[2048,512]{0,1:T(8,128)} %fusion.169, bf16[512,4096]{1,0:T(8,128)(2,1)} %bitcast.29, ...), kind=kOutput, calls=%fused_computation | convolution fusion | flops 8602509312 | bytes 25251840 | tf_op jit(solution)/shard_map/dot_general | solution.py:67
  342.6 0.1 convolution_bitcast_fusion
  342.7 9.8 %psum.7 = f32[4]{0:T(128)S(1)} all-reduce(f32[4]{0:T(128)S(1)} %convolution_bitcast_fusion), channel_id=1, replica_groups=mesh['pop'=8,'mp'=4] {'mp'}, use_global_device_ids=true, to_apply=%region_1.2 | all-reduce | flops 4 | bytes 32 | tf_op jit(solution)/shard_map/psum | solution.py:90
  352.5 0.2 dynamic-update-slice.3
  352.7 13.6 %all-reduce.3 = f32[32]{0:T(128)S(1)} all-reduce(f32[32]{0:T(128)S(1)} %dynamic-update-slice.3), channel_id=1, replica_groups=mesh['pop'=8,'mp'=4] {'pop'}, use_global_device_ids=true, to_apply=%add.3 | all-reduce | flops 32 | bytes 256
  366.3 0.6 fusion.152
  367.6 0.6 multiply_reduce_fusion
  368.9 0.6 dynamic_slice.3
  (13 shorter events, 0.1 us)
Async XLA Ops:
  7.2 19.2 %copy-start.4 = (bf16[512,2048]{1,0:T(8,128)(2,1)S(1)}, bf16[512,2048]{1,0:T(8,128)(2,1)}, u32[]{:S(2)}) copy-start(bf16[512,2048]{1,0:T(8,128)(2,1)} %param.9) | copy-start | bytes 6291460
  7.2 168.9 %all-gather.3.cloned.1.call-start = ((), (), s32[]{:S(2)}) async-start(), calls=%async_computation | async-start | bytes 18874368 | tf_op jit(solution)/shard_map/all_gather | solution.py:64
  26.2 2.3 copy-start.1
  26.2 2.3 copy-start.2
  26.2 2.3 copy-start.3
  26.3 301.3 %all-gather.5.cloned.1.call-start = ((), (), s32[]{:S(2)}) async-start(), calls=%async_computation.1 | async-start | bytes 18874368 | tf_op jit(solution)/shard_map/all_gather | solution.py:69
  28.5 3.8 %copy-start = (bf16[4,128,4096]{2,1,0:T(8,128)(2,1)S(1)}, bf16[4,128,4096]{2,1,0:T(8,128)(2,1)}, u32[]{:S(2)}) copy-start(bf16[4,128,4096]{2,1,0:T(8,128)(2,1)} %param.7) | copy-start | bytes 12582916
Sparse Core Ops, SparseCore 0:
  26.4 149.6 all-gather.2
  178.2 149.3 all-gather.4
where the time goes:
time: 377 us; the launch traced here: 376 us
  waiting for transfers between devices  279 us (74%)
  matrix products  40.7 us (11%)
  blocking collectives  34 us (9%)
  between operations  16.2 us (4%)
  local copies, waits for them, and re-layouts  4.76 us (1%)
    all_gather x1, waiting for transfers between devices, shards(): lax.all_gather(new_gate, 'pop', axis=0, tiled=True)  142 us
    all_gather x1, waiting for transfers between devices, shards(): lax.all_gather(new_up, 'pop', axis=0, tiled=True)  137 us
    unnamed x2, blocking collectives  24.2 us
    dot_general x1, matrix products, shards(): jnp.dot(flat_rows, lax.all_gather(new_gate, 'pop', axis=0, tiled=True), p...  15 us
    dot_general x1, matrix products, shards(): jnp.dot(flat_rows, lax.all_gather(new_up, 'pop', axis=0, tiled=True), pre...  15 us
    psum x1, blocking collectives, shards(): summed = lax.psum(partial_reward, 'mp')  9.82 us
  transfers between devices with their start and end apart: 2, of which 2 were waited for; matrix products, arithmetic and copies ran while one was open for 6% of the time, Pallas kernels for 0%

commit v1 on v0

v1 whole, which is shorter than its diff:
```python
import jax
import jax.numpy as jnp
from jax import lax
from jax.experimental import pallas as pl
from jax.experimental.pallas import tpu as pltpu
from jax.sharding import PartitionSpec as P

sigma_perturb = 0.004
learn_rate = 0.0016
AXES = ("pop", "mp")
CORES = 2


def shift_down(number, amount):
    return lax.shift_right_logical(number, jnp.full_like(number, amount))


def mix_bits(number):
    number = number ^ shift_down(number, 16)
    number = number * 2146121005
    number = number ^ shift_down(number, 15)
    number = number * -2073254261
    return number ^ shift_down(number, 16)


def factor_rows(seed_list, counter_list, slot, positions):
    anchor = mix_bits(
        seed_list * 1103515245 + mix_bits(counter_list * 668265263 + slot * 374761393)
    )
    hashed = mix_bits(anchor[:, None] + positions[None, :] * -1640531535)
    uniform_part = shift_down(hashed, 8).astype(jnp.float32) * (1.0 / 16777216.0)
    return (2.0 * uniform_part - 1.0 + 1.0 / 16777216.0) * 1.7320508075688772


def fresh_weights(gate_weight, up_weight, seeds, counters, ranks, row_start, column_ids):
    members_all = seeds.shape[0]
    fitness = (ranks.astype(jnp.float32) + 0.5) / members_all - 0.5
    scaling = learn_rate / (members_all * sigma_perturb)
    row_ids = row_start + jnp.arange(gate_weight.shape[0], dtype=jnp.int32)

    def fresh(weight, slot):
        right = factor_rows(seeds, counters, slot + 1, column_ids).astype(jnp.bfloat16)
        left = (factor_rows(seeds, counters, slot, row_ids) * fitness[:, None]).astype(jnp.bfloat16)
        update = scaling * jnp.dot(left.T, right, preferred_element_type=jnp.float32)
        return (weight.astype(jnp.float32) + update).astype(jnp.bfloat16)

    return fresh(gate_weight, 0), fresh(up_weight, 2)


def normalized(rewards):
    reward_mean = jnp.mean(rewards)
    reward_var = jnp.mean((rewards - reward_mean) ** 2)
    return (rewards - reward_mean) / jnp.sqrt(reward_var + 1e-05)


def gathered_plan(
    prompts, gate_weight, up_weight, reward_head, member_seeds, counters, member_ranks
):
    members_here, seq_len, width = prompts.shape
    own_rows, own_cols = gate_weight.shape
    pop_index = lax.axis_index("pop")
    column_ids = lax.axis_index("mp") * own_cols + jnp.arange(own_cols, dtype=jnp.int32)
    small = lax.all_gather(
        jnp.stack([member_seeds, counters, member_ranks]), "pop", axis=1, tiled=True
    )
    new_gate, new_up = fresh_weights(
        gate_weight, up_weight, small[0], small[1], small[2], pop_index * own_rows, column_ids
    )
    flat_rows = prompts.reshape(members_here * seq_len, width)
    later = counters + 1
    positions = jnp.arange(width, dtype=jnp.int32)

    def projected(weight, slot):
        base = jnp.dot(
            flat_rows,
            lax.all_gather(weight, "pop", axis=0, tiled=True),
            preferred_element_type=jnp.float32,
        ).reshape(members_here, seq_len, own_cols)
        vector = factor_rows(member_seeds, later, slot, positions).astype(jnp.bfloat16)
        column = factor_rows(member_seeds, later, slot + 1, column_ids)
        proj = jnp.einsum("mld,md->ml", prompts, vector, preferred_element_type=jnp.float32)
        return base + sigma_perturb * proj[:, :, None] * column[:, None, :]

    hidden = (jax.nn.silu(projected(new_gate, 0)) * projected(new_up, 2)).astype(jnp.bfloat16)
    partial = jnp.einsum("mlf,f->m", hidden, reward_head, preferred_element_type=jnp.float32)
    rewards = lax.all_gather(lax.psum(partial, "mp"), "pop", axis=0, tiled=True) / seq_len
    own = lax.dynamic_slice_in_dim(normalized(rewards), pop_index * members_here, members_here)
    return new_gate, new_up, own


def partial_kernel(count, index_ref, *refs):
    x_refs, w_refs, out_ref = refs[:count], refs[count : 2 * count], refs[2 * count]
    columns = w_refs[0].shape[2]
    rows = jnp.concatenate([r[...] for r in x_refs], axis=1)
    for part in range(2):
        weights = jnp.concatenate([w[part] for w in w_refs], axis=0)
        out_ref[:, part * columns : (part + 1) * columns] = jnp.dot(
            rows, weights, preferred_element_type=jnp.float32
        )


def partial_product(rows, index, chunks):
    count = len(chunks)
    tokens = rows.shape[0]
    _, depth, columns = chunks[0].shape
    tile = min(512, tokens)
    return pl.pallas_call(
        lambda *refs: partial_kernel(count, *refs),
        out_shape=jax.ShapeDtypeStruct((tokens, 2 * columns), jnp.float32),
        grid_spec=pltpu.PrefetchScalarGridSpec(
            num_scalar_prefetch=1,
            grid=(tokens // tile,),
            in_specs=[
                pl.BlockSpec((tile, depth), lambda i, idx, k=k: (i, idx[k])) for k in range(count)
            ]
            + [pl.BlockSpec((2, depth, columns), lambda i, idx: (0, 0, 0))] * count,
            out_specs=pl.BlockSpec((tile, 2 * columns), lambda i, idx: (i, 0)),
        ),
        compiler_params=pltpu.CompilerParams(vmem_limit_bytes=48 * 1024 * 1024),
        cost_estimate=pl.CostEstimate(
            flops=4 * tokens * depth * count * columns,
            bytes_accessed=2 * tokens * depth * count + 8 * tokens * columns + 4 * count * depth * columns,
            transcendentals=0,
        ),
    )(index, *([rows] * count), *chunks)


def final_kernel(count, seq, index_ref, *refs):
    x_refs, w_refs = refs[:count], refs[count : 2 * count]
    base_ref, proj_ref, col_ref, head_ref, out_ref = refs[2 * count :]
    columns = w_refs[0].shape[2]
    rows = jnp.concatenate([r[...] for r in x_refs], axis=1)
    values = []
    for part in range(2):
        weights = jnp.concatenate([w[part] for w in w_refs], axis=0)
        value = base_ref[:, part * columns : (part + 1) * columns] + jnp.dot(
            rows, weights, preferred_element_type=jnp.float32
        )
        members = []
        for i in range(rows.shape[0] // seq):
            members.append(
                value[i * seq : (i + 1) * seq]
                + sigma_perturb
                * proj_ref[i * seq : (i + 1) * seq, part : part + 1]
                * col_ref[0, part, i : i + 1, :]
            )
        values.append(members)
    for i, (gate, up) in enumerate(zip(*values)):
        hidden = (gate / (1.0 + jnp.exp(-gate)) * up).astype(jnp.bfloat16)
        terms = hidden.astype(jnp.float32) * head_ref[...].astype(jnp.float32)
        out_ref[i] = jnp.sum(terms.reshape(seq // 8, 8, columns), axis=0)


def final_rewards(rows, index, chunks, base, proj, cols, head, seq):
    count = len(chunks)
    tokens = rows.shape[0]
    _, depth, columns = chunks[0].shape
    group = cols.shape[2]
    tile = group * seq
    return pl.pallas_call(
        lambda *refs: final_kernel(count, seq, *refs),
        out_shape=jax.ShapeDtypeStruct((tokens // seq, 8, columns), jnp.float32),
        grid_spec=pltpu.PrefetchScalarGridSpec(
            num_scalar_prefetch=1,
            grid=(tokens // tile,),
            in_specs=[
                pl.BlockSpec((tile, depth), lambda i, idx, k=k: (i, idx[k])) for k in range(count)
            ]
            + [pl.BlockSpec((2, depth, columns), lambda i, idx: (0, 0, 0))] * count
            + [
                pl.BlockSpec((tile, 2 * columns), lambda i, idx: (i, 0)),
                pl.BlockSpec((tile, 2), lambda i, idx: (i, 0)),
                pl.BlockSpec((1, 2, group, columns), lambda i, idx: (i, 0, 0, 0)),
                pl.BlockSpec((1, columns), lambda i, idx: (0, 0)),
            ],
            out_specs=pl.BlockSpec((group, 8, columns), lambda i, idx: (i, 0, 0)),
        ),
        compiler_params=pltpu.CompilerParams(vmem_limit_bytes=48 * 1024 * 1024),
        cost_estimate=pl.CostEstimate(
            flops=4 * tokens * depth * count * columns,
            bytes_accessed=2 * tokens * depth * count + 8 * tokens * columns + 4 * count * depth * columns,
            transcendentals=tokens * columns,
        ),
    )(index, *([rows] * count), *chunks, base, proj, cols, head)


def tree_sum(terms):
    while len(terms) > 1:
        half = len(terms) // 2
        terms = [terms[i] + terms[i + half] for i in range(half)]
    return terms[0]


def spread_plan(planes, prompts, gate_weight, up_weight, reward_head, member_seeds, counters, member_ranks):
    members_here, seq, width = prompts.shape
    own_rows, own_cols = gate_weight.shape
    n_mp = members_here
    pop_index = lax.axis_index("pop")
    mp_index = lax.axis_index("mp")
    z, core = pop_index // CORES, pop_index % CORES
    block = own_cols // planes

    def pairs(move, keep=lambda z: True):
        out = []
        for a in range(planes):
            for c in range(CORES):
                for m in range(n_mp):
                    target = move(a, c, m)
                    if keep(a) and 0 <= target[0] < planes:
                        source = (a * CORES + c) * n_mp + m
                        out.append((source, (target[0] * CORES + target[1]) * n_mp + target[2]))
        return out

    def send(value, move, keep=lambda z: True):
        return lax.ppermute(value, AXES, pairs(move, keep))

    def swap_core(value):
        return send(value, lambda a, c, m: (a, 1 - c, m))

    def swap_in_plane(value, bit):
        return send(value, lambda a, c, m: (a, c, m ^ bit))

    def turn(value, s):
        return send(value, lambda a, c, m: ((a + s) % planes, c, m))

    own_member = lax.dynamic_index_in_dim(prompts, mp_index, 0, keepdims=False)
    up_hops, down_hops = [own_member], [own_member]
    for s in range(1, planes):
        up_hops.append(send(up_hops[-1], lambda a, c, m: (a + 1, c, m), lambda a: a >= s - 1))
        down_hops.append(
            send(down_hops[-1], lambda a, c, m: (a - 1, c, m), lambda a: a <= planes - s)
        )

    small = jnp.stack([member_seeds, counters, member_ranks])
    small_here = jnp.stack([small] + [turn(small, s) for s in range(1, planes)])
    small_other = swap_core(small_here)
    every = jnp.concatenate([small_here, small_other]).transpose(1, 0, 2).reshape(3, -1)

    arrivals = []
    for a in range(planes):
        order = []
        for s in range(1, planes):
            if a - s >= 0:
                order.append((0, s, a - s))
            if a + s < planes:
                order.append((1, s, a + s))
        arrivals.append(order)

    groups = [prompts.reshape(members_here * seq, width)]
    group_seeds = [(member_seeds, counters)]
    group_ids = [pop_index * members_here + jnp.arange(members_here, dtype=jnp.int32)]
    half = seq // 2
    for r in range(planes - 1):
        picks = {}
        for a in range(planes):
            picks.setdefault(arrivals[a][r][:2], []).append(a)
        block_here = None
        for (way, s), where in picks.items():
            value = (up_hops, down_hops)[way][s]
            if block_here is None:
                block_here = value
            else:
                here = (z == where[0])
                for a in where[1:]:
                    here = here | (z == a)
                block_here = jnp.where(here, value, block_here)
        across_x = swap_in_plane(block_here, 1)
        across_y = swap_in_plane(block_here, 2)
        corner_top = swap_in_plane(across_y[:half], 1)
        corner_low = swap_in_plane(across_x[half:], 2)
        groups.append(
            jnp.concatenate([block_here, across_x, across_y, corner_top, corner_low], axis=0)
        )
        source = jnp.int32(0)
        for a in range(planes):
            source = jnp.where(z == a, arrivals[a][r][2], source)
        back = (z - source) % planes
        rel = mp_index ^ jnp.arange(members_here, dtype=jnp.int32)
        chosen = jnp.int32(0)
        for s in range(1, planes):
            chosen = jnp.where(back == s, small_here[s], chosen)
        order = (rel[:, None] == jnp.arange(members_here, dtype=jnp.int32)[None, :]).astype(jnp.int32)
        picked = jnp.sum(order[None] * chosen[:, None, :], axis=2)
        group_seeds.append((picked[0], picked[1]))
        group_ids.append((source * CORES + core) * members_here + rel)

    column_ids = mp_index * own_cols + jnp.arange(own_cols, dtype=jnp.int32)
    new_gate, new_up = fresh_weights(
        gate_weight, up_weight, every[0], every[1], every[2], pop_index * own_rows, column_ids
    )

    def for_plane(target):
        start = target * block
        return jnp.stack(
            [
                lax.dynamic_slice_in_dim(new_gate, start, block, axis=1),
                lax.dynamic_slice_in_dim(new_up, start, block, axis=1),
            ]
        )

    order_of = [0] + sorted(range(1, planes), key=lambda s: (-min(s, planes - s), s))
    chunks, places = [], []
    for s in order_of:
        mine = for_plane((z + s) % planes)
        if s:
            mine = turn(mine, s)
        chunks.append((mine, swap_core(mine)))
        source = (z - s) % planes
        places.append((source * CORES + core, source * CORES + 1 - core))

    my_columns = mp_index * own_cols + z * block + jnp.arange(block, dtype=jnp.int32)
    positions = jnp.arange(width, dtype=jnp.int32)
    projs, cols = [], []
    for rows, (seeds, counts) in zip(groups, group_seeds):
        both_p, both_c = [], []
        for slot in (0, 2):
            vector = factor_rows(seeds, counts + 1, slot, positions).astype(jnp.bfloat16)
            both_c.append(factor_rows(seeds, counts + 1, slot + 1, my_columns))
            both_p.append(
                jnp.einsum(
                    "mld,md->ml",
                    rows.reshape(members_here, seq, width),
                    vector,
                    preferred_element_type=jnp.float32,
                ).reshape(-1)
            )
        projs.append(jnp.stack(both_p, axis=1))
        cols.append(jnp.stack(both_c))

    early = [c for pair in chunks[:-1] for c in pair]
    early_index = jnp.stack([p for pair in places[:-1] for p in pair])
    head = lax.dynamic_slice_in_dim(reward_head, z * block, block).reshape(1, block)
    sums = []
    for rows, proj, col in zip(groups, projs, cols):
        base = partial_product(rows, early_index, early)
        out = final_rewards(
            rows, jnp.stack(places[-1]), list(chunks[-1]), base, proj, col[None], head, seq
        )
        sums.append(out)
    sums = jnp.concatenate(sums).reshape(planes * members_here, -1).sum(axis=1)

    ids = jnp.concatenate(group_ids)
    total = planes * CORES * members_here
    rewards = jnp.sum(
        jnp.where(ids[:, None] == jnp.arange(total, dtype=jnp.int32)[None, :], sums[:, None], 0.0),
        axis=0,
    ).reshape(1, total)
    rewards = (rewards + swap_in_plane(rewards, 1)) + (
        swap_in_plane(rewards, 2) + swap_in_plane(rewards, 3)
    )
    rewards = tree_sum([rewards] + [turn(rewards, s) for s in range(1, planes)])
    rewards = (rewards + swap_core(rewards)).reshape(total) / seq
    own = lax.dynamic_slice_in_dim(normalized(rewards), pop_index * members_here, members_here)
    return new_gate, new_up, own


def solution(mesh):
    n_pop, n_mp = mesh.shape["pop"], mesh.shape["mp"]
    planes = n_pop // CORES

    def shards(prompts, gate_weight, *rest):
        members_here, seq, width = prompts.shape
        own_cols = gate_weight.shape[1]
        gathered = 2 * width * own_cols + members_here * seq * width
        spread = 2 * width * own_cols // planes + planes * members_here * seq * width
        square = n_mp == 4 and members_here == n_mp and planes & (planes - 1) == 0
        if square and own_cols % (128 * planes) == 0 and spread < gathered:
            return spread_plan(planes, prompts, gate_weight, *rest)
        return gathered_plan(prompts, gate_weight, *rest)

    in_specs = (
        P("pop", None, None),
        P("pop", "mp"),
        P("pop", "mp"),
        P("mp"),
        P("pop"),
        P("pop"),
        P("pop"),
    )
    out_specs = (P("pop", "mp"), P("pop", "mp"), P("pop"))
    return jax.shard_map(shards, mesh=mesh, in_specs=in_specs, out_specs=out_specs, check_vma=False)
```

time: 377 us -> 337 us (0.89)
  waiting for transfers between devices: 279 us -> 179 us
  starting transfers between devices: 0.08 us -> 44.7 us
  Pallas kernels: 0 us -> 44.6 us
  blocking collectives: 34 us -> 0 us
  local copies, waits for them, and re-layouts: 4.76 us -> 33.2 us
  matrix products: 40.7 us -> 17.5 us
  between operations: 16.2 us -> 2.9 us
  other arithmetic: 1.64 us -> 14.4 us
    all_gather x2 -> x0, waiting for transfers between devices: 279 us -> none  [the longest x1 142 us: shards(): lax.all_gather(new_gate, 'pop', axis=0, tiled=True)]
    ppermute x0 -> x36, waiting for transfers between devices: none -> 179 us  [send(): return lax.ppermute(value, AXES, pairs(move, keep))]
    ppermute x0 -> x36, starting transfers between devices: none -> 44.7 us  [send(): return lax.ppermute(value, AXES, pairs(move, keep))]
    pallas_call x0 -> x8, Pallas kernels: none -> 44.6 us  [the longest x4 30.1 us: partial_product(): pl.pallas_call(lambda *refs: partial_kernel(count, *refs), out_shape=jax....]
    unnamed x2 -> x0, blocking collectives: 24.2 us -> none
    dot_general x7 -> x10, matrix products: 40.7 us -> 17.5 us  [the longest x8 14.2 us: spread_plan(): jnp.einsum('mld,md->ml', rows.reshape(members_here, seq, width), vector,...]
    unnamed x20 -> x63, local copies, waits for them, and re-layouts: 4.17 us -> 16.7 us
    psum x1 -> x0, blocking collectives: 9.82 us -> none  [shards(): summed = lax.psum(partial_reward, 'mp')]
  transfers between devices with their start and end apart: 2 -> 36, of which waited for: 2 -> 20; matrix products, arithmetic and copies ran while one was open for 6% -> 15% of each run, Pallas kernels for 0% -> 3%
where the time goes in v1:
time: 337 us; the launch traced here: 336 us
  waiting for transfers between devices  179 us (53%)
  starting transfers between devices  44.7 us (13%)
  Pallas kernels  44.6 us (13%)
  local copies, waits for them, and re-layouts  33.2 us (10%)
  matrix products  17.5 us (5%)
  other arithmetic  14.4 us (4%)
    ppermute x36, waiting for transfers between devices, send(): return lax.ppermute(value, AXES, pairs(move, keep))  179 us
    ppermute x36, starting transfers between devices, send(): return lax.ppermute(value, AXES, pairs(move, keep))  44.7 us
    pallas_call x4, Pallas kernels, partial_product(): pl.pallas_call(lambda *refs: partial_kernel(count, *refs), out_shape=jax....  30.1 us
    unnamed x63, local copies, waits for them, and re-layouts  16.7 us
    pallas_call x4, Pallas kernels, final_rewards(): pl.pallas_call(lambda *refs: final_kernel(count, seq, *refs), out_shape=j...  14.5 us
    dot_general x8, matrix products, spread_plan(): jnp.einsum('mld,md->ml', rows.reshape(members_here, seq, width), vector,...  14.2 us
  transfers between devices with their start and end apart: 36, of which 20 were waited for; matrix products, arithmetic and copies ran while one was open for 15% of the time, Pallas kernels for 3%

profile of v1, /device:TPU:0, one launch (start us, length us, event | category | flops | bytes accessed | tf_op | source)
XLA Modules:
  0.0 336.3 jit_solution(7143537508926050289)
XLA Ops:
  1.3 3.1 collective-permute-start
  4.4 2.6 collective-permute-start.1
  9.6 2.6 collective-permute-start.11
  17.9 15.9 %collective-permute-done.11 = bf16[128,4096]{1,0:T(8,128)(2,1)S(1)} collective-permute-done((bf16[128,4096]{1,0:T(8,128)(2,1)S(1)}, bf16[128,4096]{1,0:T(8,128)(2,1)S(1)}, u32[]{:S(2)}, u32[]{:S(2)}) %collective-permute-start.11) | collective-permute-done | bytes 1048608 | tf_op jit(solution)/shard_map/ppermute | solution.py:215
  33.8 1.7 collective-permute-start.17
  35.5 2.6 collective-permute-done.12
  39.4 2.4 add_convert_fusion.1
  42.7 1.6 dynamic-slice_bitcast_fusion.1
  46.5 4.5 %collective-permute-start.7 = (bf16[2,512,512]{2,1,0:T(8,128)(2,1)}, bf16[2,512,512]{2,1,0:T(8,128)(2,1)S(1)}, u32[]{:S(2)}, u32[]{:S(2)}) collective-permute-start(bf16[2,512,512]{2,1,0:T(8,128)(2,1)} %pad_maximum_fusion.2), channel_id=1, source_target_pairs={{0,16},{1,17},{2,18},{3,19},{4,20},{5,21},{6,22},{7,23},{8,24},{9,... | collective-permute-start | bytes 3145736 | tf_op jit(solution)/shard_map/ppermute | solution.py:215
  52.1 2.0 collective-permute-start.9
  54.1 1.6 collective-permute-start.23
  55.8 10.6 %collective-permute-done.18 = bf16[128,4096]{1,0:T(8,128)(2,1)} collective-permute-done((bf16[128,4096]{1,0:T(8,128)(2,1)}, bf16[128,4096]{1,0:T(8,128)(2,1)}, u32[]{:S(2)}, u32[]{:S(2)}) %collective-permute-start.18) | collective-permute-done | bytes 1048608 | tf_op jit(solution)/shard_map/ppermute | solution.py:215
  66.4 1.5 collective-permute-start.24
  73.0 12.7 %collective-permute-done.4.refs_3_ = bf16[2,512,512]{2,1,0:T(8,128)(2,1)} collective-permute-done((bf16[2,512,512]{2,1,0:T(8,128)(2,1)}, bf16[2,512,512]{2,1,0:T(8,128)(2,1)}, u32[]{:S(2)}, u32[]{:S(2)}) %collective-permute-start.4) | collective-permute-done | bytes 1048608 | tf_op jit(solution)/shard_map/ppermute | solution.py:215
  85.7 68.6 %collective-permute-done.7.refs_9_ = bf16[2,512,512]{2,1,0:T(8,128)(2,1)S(1)} collective-permute-done((bf16[2,512,512]{2,1,0:T(8,128)(2,1)}, bf16[2,512,512]{2,1,0:T(8,128)(2,1)S(1)}, u32[]{:S(2)}, u32[]{:S(2)}) %collective-permute-start.7) | collective-permute-done | bytes 1048608 | tf_op jit(solution)/shard_map/ppermute | solution.py:215
  154.9 7.7 %collective-permute-done.24 = bf16[128,4096]{1,0:T(8,128)(2,1)} collective-permute-done((bf16[128,4096]{1,0:T(8,128)(2,1)}, bf16[128,4096]{1,0:T(8,128)(2,1)}, u32[]{:S(2)}, u32[]{:S(2)}) %collective-permute-start.24) | collective-permute-done | bytes 1048608 | tf_op jit(solution)/shard_map/ppermute | solution.py:215
  162.6 4.9 %constant_dynamic-update-slice_fusion.4 = (bf16[512,4096]{1,0:T(8,128)(2,1)S(1)}, bf16[128,4096]{1,0:T(8,128)(2,1)}, bf16[512,4096]{1,0:T(8,128)(2,1)}, bf16[128...) fusion(bf16[128,4096]{1,0:T(8,128)(2,1)} %copy-done.21, ...), kind=kLoop, calls=%fused_computation.199 | loop fusion | flops 3145725 | bytes 12582917
  168.8 1.5 collective-permute-start.26
  171.6 7.5 %shard_map.94.refs_5_ = f32[512,1024]{1,0:T(8,128)} custom-call(s32[6]{0:T(128)S(1)} %stack.155.refs_0_, bf16[512,4096]{1,0:T(8,128)(2,1)} %bitcast.217, bf16[512,4096]{1,0:T(8,128)(2,1)} %bitcast.218, bf16[512,4096]{1,0:T(8,128)(2,1)} %bitcast.219, bf16[512,4096]{1,0:T(8,128)(2,1)} %bitcast.220, bf16[512,4096]{1,0:T(8,128)(2,1)} %bitcast.221, ...), custom_call_target="tpu_custom_call" | custom-call | flops 3221225472 | bytes 11534336 | tf_op jit(solution)/shard_map/pallas_call | solution.py:107
  181.6 1.6 copy-done.7
  183.2 3.5 %shard_map.95 = f32[4,8,512]{2,1,0:T(8,128)S(1)} custom-call(s32[2]{0:T(128)S(1)} %pad_add_fusion.3.refs_0_, bf16[512,4096]{1,0:T(8,128)(2,1)} %bitcast.223, bf16[512,4096]{1,0:T(8,128)(2,1)} %bitcast.224, bf16[2,512,512]{2,1,0:T(8,128)(2,1)} %collective-permute-done.4.refs_3_, bf16[2,512,512]{2,1,0:T(8,128)(2,1)S(1)} %collective-permute-done.5.refs_4_, ...), custom_call_target="tpu_custom_call" | custom-call | flops 1073741824 | bytes 5242880 | tf_op jit(solution)/shard_map/pallas_call | solution.py:160
  186.8 8.4 %collective-permute-done.26 = bf16[128,4096]{1,0:T(8,128)(2,1)} collective-permute-done((bf16[128,4096]{1,0:T(8,128)(2,1)}, bf16[128,4096]{1,0:T(8,128)(2,1)}, u32[]{:S(2)}, u32[]{:S(2)}) %collective-permute-start.26) | collective-permute-done | bytes 1048608 | tf_op jit(solution)/shard_map/ppermute | solution.py:215
  198.4 2.3 constant_dynamic-update-slice_fusion.13
  200.7 2.3 constant_dynamic-update-slice_fusion.12
  204.1 13.6 %collective-permute-done.20 = bf16[128,4096]{1,0:T(8,128)(2,1)} collective-permute-done((bf16[128,4096]{1,0:T(8,128)(2,1)}, bf16[128,4096]{1,0:T(8,128)(2,1)}, u32[]{:S(2)}, u32[]{:S(2)}) %collective-permute-start.20) | collective-permute-done | bytes 1048608 | tf_op jit(solution)/shard_map/ppermute | solution.py:215
  217.7 1.5 collective-permute-start.28
  222.0 18.2 %collective-permute-done.14 = bf16[128,4096]{1,0:T(8,128)(2,1)} collective-permute-done((bf16[128,4096]{1,0:T(8,128)(2,1)}, bf16[128,4096]{1,0:T(8,128)(2,1)}, u32[]{:S(2)}, u32[]{:S(2)}) %collective-permute-start.14) | collective-permute-done | bytes 1048608 | tf_op jit(solution)/shard_map/ppermute | solution.py:215
  240.1 1.5 collective-permute-start.22
  241.7 1.9 slice.66
  244.8 1.5 constant_dynamic-update-slice_fusion.7
  253.8 7.4 %collective-permute-done.21 = bf16[64,4096]{1,0:T(8,128)(2,1)S(1)} collective-permute-done((bf16[64,4096]{1,0:T(8,128)(2,1)S(1)}, bf16[64,4096]{1,0:T(8,128)(2,1)S(1)}, u32[]{:S(2)}, u32[]{:S(2)}) %collective-permute-start.21) | collective-permute-done | bytes 524320 | tf_op jit(solution)/shard_map/ppermute | solution.py:215
  264.7 3.6 %convolution_bitcast_fusion.3 = f32[512,1]{0,1:T(1,128)S(1)} fusion(bf16[4,128,4096]{2,1,0:T(8,128)(2,1)} %bitcast.214, bf16[4,4096,1]{1,0,2:T(4,128)(2,1)} %get-tuple-element.30), kind=kOutput, calls=%fused_computation.5 | convolution fusion | flops 4194304 | bytes 4229120 | tf_op jit(solution)/shard_map/mld,md->ml/dot_general | solution.py:320
  269.2 2.3 collective-permute-done.15
  271.5 1.9 constant_dynamic-update-slice_fusion.1
  273.4 1.9 constant_dynamic-update-slice_fusion.refs_1_.refs_2_.refs_3_.refs_4_.refs_5_.refs_6_
  275.3 3.5 %convolution_bitcast_fusion.4 = f32[512,1]{0,1:T(1,128)S(1)} fusion(bf16[4,128,4096]{2,1,0:T(8,128)(2,1)} %bitcast.211, bf16[4,4096,1]{1,0,2:T(4,128)(2,1)} %get-tuple-element.29), kind=kOutput, calls=%fused_computation.6 | convolution fusion | flops 4194304 | bytes 4229120 | tf_op jit(solution)/shard_map/mld,md->ml/dot_general | solution.py:320
  283.4 7.5 %shard_map.100.refs_5_ = f32[512,1024]{1,0:T(8,128)} custom-call(s32[6]{0:T(128)S(1)} %stack.155.refs_0_, bf16[512,4096]{1,0:T(8,128)(2,1)} %copy-done.16, bf16[512,4096]{1,0:T(8,128)(2,1)} %copy-done.16, bf16[512,4096]{1,0:T(8,128)(2,1)} %copy-done.16, bf16[512,4096]{1,0:T(8,128)(2,1)} %copy-done.16, bf16[512,4096]{1,0:T(8,128)(2,1)} %copy-done.16, ...), custom_call_target="tpu_custom_call" | custom-call | flops 3221225472 | bytes 11534336 | tf_op jit(solution)/shard_map/pallas_call | solution.py:107
  290.9 7.4 %shard_map.98.refs_5_ = f32[512,1024]{1,0:T(8,128)} custom-call(s32[6]{0:T(128)S(1)} %stack.155.refs_0_, bf16[512,4096]{1,0:T(8,128)(2,1)} %copy-done.14, bf16[512,4096]{1,0:T(8,128)(2,1)} %copy-done.14, bf16[512,4096]{1,0:T(8,128)(2,1)} %copy-done.14, bf16[512,4096]{1,0:T(8,128)(2,1)} %copy-done.14, bf16[512,4096]{1,0:T(8,128)(2,1)} %copy-done.14, ...), custom_call_target="tpu_custom_call" | custom-call | flops 3221225472 | bytes 11534336 | tf_op jit(solution)/shard_map/pallas_call | solution.py:107
  298.3 7.7 %shard_map.96.refs_5_ = f32[512,1024]{1,0:T(8,128)} custom-call(s32[6]{0:T(128)S(1)} %stack.155.refs_0_, bf16[512,4096]{1,0:T(8,128)(2,1)} %constant_dynamic-update-slice_fusion.refs_1_.refs_2_.refs_3_.refs_4_.refs_5_.refs_6_, bf16[512,4096]{1,0:T(8,128)(2,1)} %constant_dynamic-update-slice_fusion.refs_1_.refs_2_.refs_3_.refs_4_.refs_5_.refs_6_, ...), custom_call_target="tpu_custom_call" | custom-call | flops 3221225472 | bytes 11534336 | tf_op jit(solution)/shard_map/pallas_call | solution.py:107
  306.0 3.7 %shard_map.101 = f32[4,8,512]{2,1,0:T(8,128)S(1)} custom-call(s32[2]{0:T(128)S(1)} %pad_add_fusion.3.refs_0_, bf16[512,4096]{1,0:T(8,128)(2,1)} %copy-done.16, bf16[512,4096]{1,0:T(8,128)(2,1)} %copy-done.16, bf16[2,512,512]{2,1,0:T(8,128)(2,1)} %collective-permute-done.4.refs_3_, bf16[2,512,512]{2,1,0:T(8,128)(2,1)S(1)} %copy-done.5, ...), custom_call_target="tpu_custom_call" | custom-call | flops 1073741824 | bytes 5242880 | tf_op jit(solution)/shard_map/pallas_call | solution.py:160
  309.7 3.7 %shard_map.99 = f32[4,8,512]{2,1,0:T(8,128)S(1)} custom-call(s32[2]{0:T(128)S(1)} %pad_add_fusion.3.refs_0_, bf16[512,4096]{1,0:T(8,128)(2,1)} %copy-done.14, bf16[512,4096]{1,0:T(8,128)(2,1)} %copy-done.14, bf16[2,512,512]{2,1,0:T(8,128)(2,1)} %collective-permute-done.4.refs_3_, bf16[2,512,512]{2,1,0:T(8,128)(2,1)S(1)} %copy-done.5, ...), custom_call_target="tpu_custom_call" | custom-call | flops 1073741824 | bytes 5242880 | tf_op jit(solution)/shard_map/pallas_call | solution.py:160
  313.4 3.6 %shard_map.97 = f32[4,8,512]{2,1,0:T(8,128)S(1)} custom-call(s32[2]{0:T(128)S(1)} %pad_add_fusion.3.refs_0_, bf16[512,4096]{1,0:T(8,128)(2,1)} %constant_dynamic-update-slice_fusion.refs_1_.refs_2_.refs_3_.refs_4_.refs_5_.refs_6_, bf16[512,4096]{1,0:T(8,128)(2,1)} %constant_dynamic-update-slice_fusion.refs_1_.refs_2_.refs_3_.refs_4_.refs_5_.refs_6_, ...), custom_call_target="tpu_custom_call" | custom-call | flops 1073741824 | bytes 5242880 | tf_op jit(solution)/shard_map/pallas_call | solution.py:160
  317.4 1.4 collective-permute-start.30
  318.8 1.4 collective-permute-start.31
  321.0 2.3 collective-permute-done.31
  323.8 3.8 %collective-permute-start.34 = (f32[1,32]{1,0:T(1,128)S(1)}, f32[1,32]{1,0:T(1,128)S(1)}, u32[]{:S(2)}, u32[]{:S(2)}) collective-permute-start(f32[1,32]{1,0:T(1,128)S(1)} %add_add_fusion.1), channel_id=1, source_target_pairs={{0,24},{1,25},{2,26},{3,27},{4,28},{5,29},{6,30},{7,31},{8,0},{9,1... | collective-permute-start | bytes 392 | tf_op jit(solution)/shard_map/ppermute | solution.py:215
  327.6 1.5 collective-permute-done.33
  329.1 2.9 collective-permute-done.32
  (178 shorter events, 53.9 us)
Async XLA Ops:
  1.3 14.5 %collective-permute-start = (s32[3,4]{1,0:T(4,128)S(1)}, s32[3,4]{1,0:T(4,128)S(1)}, u32[]{:S(2)}, u32[]{:S(2)}) collective-permute-start(s32[3,4]{1,0:T(4,128)S(1)} %get-tuple-element.59), channel_id=1, source_target_pairs={{0,8},{1,9},{2,10},{3,11},{4,12},{5,13},{6,14},{7,15},{8,16},{9,17... | collective-permute-start | bytes 152 | tf_op jit(solution)/shard_map/ppermute | solution.py:215
  4.4 11.4 %collective-permute-start.1 = (s32[3,4]{1,0:T(4,128)S(1)}, s32[3,4]{1,0:T(4,128)S(1)}, u32[]{:S(2)}, u32[]{:S(2)}) collective-permute-start(s32[3,4]{1,0:T(4,128)S(1)} %get-tuple-element.59), channel_id=1, source_target_pairs={{0,16},{1,17},{2,18},{3,19},{4,20},{5,21},{6,22},{7,23},{8,24},{9,... | collective-permute-start | bytes 152 | tf_op jit(solution)/shard_map/ppermute | solution.py:215
  7.0 8.9 %collective-permute-start.2 = (s32[3,4]{1,0:T(4,128)S(1)}, s32[3,4]{1,0:T(4,128)S(1)}, u32[]{:S(2)}, u32[]{:S(2)}) collective-permute-start(s32[3,4]{1,0:T(4,128)S(1)} %get-tuple-element.59), channel_id=1, source_target_pairs={{0,24},{1,25},{2,26},{3,27},{4,28},{5,29},{6,30},{7,31},{8,0},{9,1... | collective-permute-start | bytes 152 | tf_op jit(solution)/shard_map/ppermute | solution.py:215
  9.6 24.1 %collective-permute-start.11 = (bf16[128,4096]{1,0:T(8,128)(2,1)S(1)}, bf16[128,4096]{1,0:T(8,128)(2,1)S(1)}, u32[]{:S(2)}, u32[]{:S(2)}) collective-permute-start(bf16[128,4096]{1,0:T(8,128)(2,1)S(1)} %dynamic-slice_bitcast_fusion), channel_id=1, source_target_pairs={{0,8},{1,9},{2,10},{3,11},{4,12},{5,13},{6,14},{7,15},{8,16},{9,17... | collective-permute-start | bytes 3145736 | tf_op jit(solution)/shard_map/ppermute | solution.py:215
  12.3 25.8 %collective-permute-start.12 = (bf16[128,4096]{1,0:T(8,128)(2,1)S(1)}, bf16[128,4096]{1,0:T(8,128)(2,1)}, u32[]{:S(2)}, u32[]{:S(2)}) collective-permute-start(bf16[128,4096]{1,0:T(8,128)(2,1)S(1)} %dynamic-slice_bitcast_fusion), channel_id=1, source_target_pairs={{8,0},{9,1},{10,2},{11,3},{12,4},{13,5},{14,6},{15,7},{16,8},{17,9... | collective-permute-start | bytes 3145736 | tf_op jit(solution)/shard_map/ppermute | solution.py:215
  15.9 1.2 collective-permute-start.3
  17.8 24.0 %copy-start.26 = (bf16[512,2048]{1,0:T(8,128)(2,1)S(1)}, bf16[512,2048]{1,0:T(8,128)(2,1)}, u32[]{:S(2)}) copy-start(bf16[512,2048]{1,0:T(8,128)(2,1)} %param.9) | copy-start | bytes 6291460
  33.8 8.9 %copy-start.21 = (bf16[128,4096]{1,0:T(8,128)(2,1)}, bf16[128,4096]{1,0:T(8,128)(2,1)S(1)}, u32[]{:S(2)}) copy-start(bf16[128,4096]{1,0:T(8,128)(2,1)S(1)} %collective-permute-done.11) | copy-start | bytes 3145732
  33.8 20.3 %collective-permute-start.17 = (bf16[128,4096]{1,0:T(8,128)(2,1)S(1)}, bf16[128,4096]{1,0:T(8,128)(2,1)}, u32[]{:S(2)}, u32[]{:S(2)}) collective-permute-start(bf16[128,4096]{1,0:T(8,128)(2,1)S(1)} %collective-permute-done.11), channel_id=1, source_target_pairs={{8,16},{9,17},{10,18},{11,19},{12,20},{13,21},{14,22},{15,23},{16,... | collective-permute-start | bytes 3145736 | tf_op jit(solution)/shard_map/ppermute | solution.py:215
  38.1 28.3 %collective-permute-start.18 = (bf16[128,4096]{1,0:T(8,128)(2,1)}, bf16[128,4096]{1,0:T(8,128)(2,1)}, u32[]{:S(2)}, u32[]{:S(2)}) collective-permute-start(bf16[128,4096]{1,0:T(8,128)(2,1)} %collective-permute-done.12), channel_id=1, source_target_pairs={{8,0},{9,1},{10,2},{11,3},{12,4},{13,5},{14,6},{15,7},{16,8},{17,9... | collective-permute-start | bytes 3145736 | tf_op jit(solution)/shard_map/ppermute | solution.py:215
  44.3 24.8 %copy-start.17 = (bf16[4,128,4096]{2,1,0:T(8,128)(2,1)S(1)}, bf16[4,128,4096]{2,1,0:T(8,128)(2,1)}, u32[]{:S(2)}) copy-start(bf16[4,128,4096]{2,1,0:T(8,128)(2,1)} %param.7) | copy-start | bytes 12582916
  45.4 40.3 %collective-permute-start.4 = (bf16[2,512,512]{2,1,0:T(8,128)(2,1)}, bf16[2,512,512]{2,1,0:T(8,128)(2,1)}, u32[]{:S(2)}, u32[]{:S(2)}) collective-permute-start(bf16[2,512,512]{2,1,0:T(8,128)(2,1)} %pad_maximum_fusion), channel_id=1, source_target_pairs={{0,24},{1,25},{2,26},{3,27},{4,28},{5,29},{6,30},{7,31},{8,0},{9,1... | collective-permute-start | bytes 3145736 | tf_op jit(solution)/shard_map/ppermute | solution.py:215
  46.5 107.8 %collective-permute-start.7 = (bf16[2,512,512]{2,1,0:T(8,128)(2,1)}, bf16[2,512,512]{2,1,0:T(8,128)(2,1)S(1)}, u32[]{:S(2)}, u32[]{:S(2)}) collective-permute-start(bf16[2,512,512]{2,1,0:T(8,128)(2,1)} %pad_maximum_fusion.2), channel_id=1, source_target_pairs={{0,16},{1,17},{2,18},{3,19},{4,20},{5,21},{6,22},{7,23},{8,24},{9,... | collective-permute-start | bytes 3145736 | tf_op jit(solution)/shard_map/ppermute | solution.py:215
  52.1 102.2 %collective-permute-start.9 = (bf16[2,512,512]{2,1,0:T(8,128)(2,1)}, bf16[2,512,512]{2,1,0:T(8,128)(2,1)S(1)}, u32[]{:S(2)}, u32[]{:S(2)}) collective-permute-start(bf16[2,512,512]{2,1,0:T(8,128)(2,1)} %pad_maximum_fusion.3), channel_id=1, source_target_pairs={{0,8},{1,9},{2,10},{3,11},{4,12},{5,13},{6,14},{7,15},{8,16},{9,17... | collective-permute-start | bytes 3145736 | tf_op jit(solution)/shard_map/ppermute | solution.py:215
  54.1 100.7 %collective-permute-start.23 = (bf16[128,4096]{1,0:T(8,128)(2,1)}, bf16[128,4096]{1,0:T(8,128)(2,1)}, u32[]{:S(2)}, u32[]{:S(2)}) collective-permute-start(bf16[128,4096]{1,0:T(8,128)(2,1)} %collective-permute-done.17), channel_id=1, source_target_pairs={{16,24},{17,25},{18,26},{19,27},{20,28},{21,29},{22,30},{23,31}} | collective-permute-start | bytes 3145736 | tf_op jit(solution)/shard_map/ppermute | solution.py:215
  66.4 96.2 %collective-permute-start.24 = (bf16[128,4096]{1,0:T(8,128)(2,1)}, bf16[128,4096]{1,0:T(8,128)(2,1)}, u32[]{:S(2)}, u32[]{:S(2)}) collective-permute-start(bf16[128,4096]{1,0:T(8,128)(2,1)} %collective-permute-done.18), channel_id=1, source_target_pairs={{8,0},{9,1},{10,2},{11,3},{12,4},{13,5},{14,6},{15,7}} | collective-permute-start | bytes 3145736 | tf_op jit(solution)/shard_map/ppermute | solution.py:215
  85.7 83.1 %collective-permute-start.6 = (bf16[2,512,512]{2,1,0:T(8,128)(2,1)S(1)}, bf16[2,512,512]{2,1,0:T(8,128)(2,1)S(1)}, u32[]{:S(2)}, u32[]{:S(2)}) collective-permute-start(bf16[2,512,512]{2,1,0:T(8,128)(2,1)S(1)} %pad_maximum_fusion.1.refs_7_), channel_id=1, source_target_pairs={{0,4},{1,5},{2,6},{3,7},{4,0},{5,1},{6,2},{7,3},{8,12},{9,13},{10,... | collective-permute-start | bytes 3145736 | tf_op jit(solution)/shard_map/ppermute | solution.py:215
  154.3 26.0 %collective-permute-start.5 = (bf16[2,512,512]{2,1,0:T(8,128)(2,1)}, bf16[2,512,512]{2,1,0:T(8,128)(2,1)S(1)}, u32[]{:S(2)}, u32[]{:S(2)}) collective-permute-start(bf16[2,512,512]{2,1,0:T(8,128)(2,1)} %collective-permute-done.4.refs_3_), channel_id=1, source_target_pairs={{0,4},{1,5},{2,6},{3,7},{4,0},{5,1},{6,2},{7,3},{8,12},{9,13},{10,... | collective-permute-start | bytes 3145736 | tf_op jit(solution)/shard_map/ppermute | solution.py:215
  154.3 16.2 %collective-permute-start.8 = (bf16[2,512,512]{2,1,0:T(8,128)(2,1)S(1)}, bf16[2,512,512]{2,1,0:T(8,128)(2,1)S(1)}, u32[]{:S(2)}, u32[]{:S(2)}) collective-permute-start(bf16[2,512,512]{2,1,0:T(8,128)(2,1)S(1)} %collective-permute-done.7.refs_9_), channel_id=1, source_target_pairs={{0,4},{1,5},{2,6},{3,7},{4,0},{5,1},{6,2},{7,3},{8,12},{9,13},{10,... | collective-permute-start | bytes 3145736 | tf_op jit(solution)/shard_map/ppermute | solution.py:215
  154.8 15.7 %collective-permute-start.10 = (bf16[2,512,512]{2,1,0:T(8,128)(2,1)S(1)}, bf16[2,512,512]{2,1,0:T(8,128)(2,1)S(1)}, u32[]{:S(2)}, u32[]{:S(2)}) collective-permute-start(bf16[2,512,512]{2,1,0:T(8,128)(2,1)S(1)} %collective-permute-done.9.refs_11_), channel_id=1, source_target_pairs={{0,4},{1,5},{2,6},{3,7},{4,0},{5,1},{6,2},{7,3},{8,12},{9,13},{10,... | collective-permute-start | bytes 3145736 | tf_op jit(solution)/shard_map/ppermute | solution.py:215
  167.5 29.5 %collective-permute-start.25 = (bf16[128,4096]{1,0:T(8,128)(2,1)}, bf16[128,4096]{1,0:T(8,128)(2,1)}, u32[]{:S(2)}, u32[]{:S(2)}) collective-permute-start(bf16[128,4096]{1,0:T(8,128)(2,1)} %get-tuple-element.23), channel_id=1, source_target_pairs={{0,1},{1,0},{2,3},{3,2},{4,5},{5,4},{6,7},{7,6},{8,9},{9,8},{10,11... | collective-permute-start | bytes 3145736 | tf_op jit(solution)/shard_map/ppermute | solution.py:215
  168.8 10.2 %copy-start = (bf16[2,512,512]{2,1,0:T(8,128)(2,1)}, bf16[2,512,512]{2,1,0:T(8,128)(2,1)S(1)}, u32[]{:S(2)}) copy-start(bf16[2,512,512]{2,1,0:T(8,128)(2,1)S(1)} %collective-permute-done.6.refs_8_) | copy-start | bytes 3145732
  168.8 26.4 %collective-permute-start.26 = (bf16[128,4096]{1,0:T(8,128)(2,1)}, bf16[128,4096]{1,0:T(8,128)(2,1)}, u32[]{:S(2)}, u32[]{:S(2)}) collective-permute-start(bf16[128,4096]{1,0:T(8,128)(2,1)} %get-tuple-element.23), channel_id=1, source_target_pairs={{0,2},{1,3},{2,0},{3,1},{4,6},{5,7},{6,4},{7,5},{8,10},{9,11},{10,... | collective-permute-start | bytes 3145736 | tf_op jit(solution)/shard_map/ppermute | solution.py:215
  170.5 8.5 %copy-start.2 = (bf16[2,512,512]{2,1,0:T(8,128)(2,1)}, bf16[2,512,512]{2,1,0:T(8,128)(2,1)S(1)}, u32[]{:S(2)}) copy-start(bf16[2,512,512]{2,1,0:T(8,128)(2,1)S(1)} %collective-permute-done.8.refs_10_) | copy-start | bytes 3145732
  179.1 41.2 %collective-permute-start.19 = (bf16[128,4096]{1,0:T(8,128)(2,1)}, bf16[128,4096]{1,0:T(8,128)(2,1)}, u32[]{:S(2)}, u32[]{:S(2)}) collective-permute-start(bf16[128,4096]{1,0:T(8,128)(2,1)} %get-tuple-element.25), channel_id=1, source_target_pairs={{0,1},{1,0},{2,3},{3,2},{4,5},{5,4},{6,7},{7,6},{8,9},{9,8},{10,11... | collective-permute-start | bytes 3145736 | tf_op jit(solution)/shard_map/ppermute | solution.py:215
  179.6 38.1 %collective-permute-start.20 = (bf16[128,4096]{1,0:T(8,128)(2,1)}, bf16[128,4096]{1,0:T(8,128)(2,1)}, u32[]{:S(2)}, u32[]{:S(2)}) collective-permute-start(bf16[128,4096]{1,0:T(8,128)(2,1)} %get-tuple-element.25), channel_id=1, source_target_pairs={{0,2},{1,3},{2,0},{3,1},{4,6},{5,7},{6,4},{7,5},{8,10},{9,11},{10,... | collective-permute-start | bytes 3145736 | tf_op jit(solution)/shard_map/ppermute | solution.py:215
  180.3 6.5 %copy-start.4 = (bf16[2,512,512]{2,1,0:T(8,128)(2,1)}, bf16[2,512,512]{2,1,0:T(8,128)(2,1)S(1)}, u32[]{:S(2)}) copy-start(bf16[2,512,512]{2,1,0:T(8,128)(2,1)S(1)} %collective-permute-done.5.refs_4_) | copy-start | bytes 3145732
  180.3 59.9 %collective-permute-start.14 = (bf16[128,4096]{1,0:T(8,128)(2,1)}, bf16[128,4096]{1,0:T(8,128)(2,1)}, u32[]{:S(2)}, u32[]{:S(2)}) collective-permute-start(bf16[128,4096]{1,0:T(8,128)(2,1)} %get-tuple-element.7), channel_id=1, source_target_pairs={{0,2},{1,3},{2,0},{3,1},{4,6},{5,7},{6,4},{7,5},{8,10},{9,11},{10,... | collective-permute-start | bytes 3145736 | tf_op jit(solution)/shard_map/ppermute | solution.py:215
  195.2 51.1 %collective-permute-start.13 = (bf16[128,4096]{1,0:T(8,128)(2,1)}, bf16[128,4096]{1,0:T(8,128)(2,1)S(1)}, u32[]{:S(2)}, u32[]{:S(2)}) collective-permute-start(bf16[128,4096]{1,0:T(8,128)(2,1)} %get-tuple-element.7), channel_id=1, source_target_pairs={{0,1},{1,0},{2,3},{3,2},{4,5},{5,4},{6,7},{7,6},{8,9},{9,8},{10,11... | collective-permute-start | bytes 3145736 | tf_op jit(solution)/shard_map/ppermute | solution.py:215
  197.0 52.9 %collective-permute-start.27 = (bf16[64,4096]{1,0:T(8,128)(2,1)S(1)}, bf16[64,4096]{1,0:T(8,128)(2,1)S(1)}, u32[]{:S(2)}, u32[]{:S(2)}) collective-permute-start(bf16[64,4096]{1,0:T(8,128)(2,1)S(1)} %slice.70), channel_id=1, source_target_pairs={{0,1},{1,0},{2,3},{3,2},{4,5},{5,4},{6,7},{7,6},{8,9},{9,8},{10,11... | collective-permute-start | bytes 1572872 | tf_op jit(solution)/shard_map/ppermute | solution.py:215
  217.7 33.6 %collective-permute-start.28 = (bf16[64,4096]{1,0:T(8,128)(2,1)S(1)}, bf16[64,4096]{1,0:T(8,128)(2,1)S(1)}, u32[]{:S(2)}, u32[]{:S(2)}) collective-permute-start(bf16[64,4096]{1,0:T(8,128)(2,1)S(1)} %slice.71), channel_id=1, source_target_pairs={{0,2},{1,3},{2,0},{3,1},{4,6},{5,7},{6,4},{7,5},{8,10},{9,11},{10,... | collective-permute-start | bytes 1572872 | tf_op jit(solution)/shard_map/ppermute | solution.py:215
  220.3 40.8 %collective-permute-start.21 = (bf16[64,4096]{1,0:T(8,128)(2,1)S(1)}, bf16[64,4096]{1,0:T(8,128)(2,1)S(1)}, u32[]{:S(2)}, u32[]{:S(2)}) collective-permute-start(bf16[64,4096]{1,0:T(8,128)(2,1)S(1)} %slice.68), channel_id=1, source_target_pairs={{0,1},{1,0},{2,3},{3,2},{4,5},{5,4},{6,7},{7,6},{8,9},{9,8},{10,11... | collective-permute-start | bytes 1572872 | tf_op jit(solution)/shard_map/ppermute | solution.py:215
  240.1 22.4 %collective-permute-start.22 = (bf16[64,4096]{1,0:T(8,128)(2,1)S(1)}, bf16[64,4096]{1,0:T(8,128)(2,1)S(1)}, u32[]{:S(2)}, u32[]{:S(2)}) collective-permute-start(bf16[64,4096]{1,0:T(8,128)(2,1)S(1)} %slice.69), channel_id=1, source_target_pairs={{0,2},{1,3},{2,0},{3,1},{4,6},{5,7},{6,4},{7,5},{8,10},{9,11},{10,... | collective-permute-start | bytes 1572872 | tf_op jit(solution)/shard_map/ppermute | solution.py:215
  244.8 6.4 %copy-start.15 = (bf16[512,4096]{1,0:T(8,128)(2,1)S(1)}, bf16[512,4096]{1,0:T(8,128)(2,1)}, u32[]{:S(2)}) copy-start(bf16[512,4096]{1,0:T(8,128)(2,1)} %constant_dynamic-update-slice_fusion.12) | copy-start | bytes 12582916
  246.3 25.2 %collective-permute-start.15 = (bf16[64,4096]{1,0:T(8,128)(2,1)}, bf16[64,4096]{1,0:T(8,128)(2,1)}, u32[]{:S(2)}, u32[]{:S(2)}) collective-permute-start(bf16[64,4096]{1,0:T(8,128)(2,1)} %slice.66), channel_id=1, source_target_pairs={{0,1},{1,0},{2,3},{3,2},{4,5},{5,4},{6,7},{7,6},{8,9},{9,8},{10,11... | collective-permute-start | bytes 1572872 | tf_op jit(solution)/shard_map/ppermute | solution.py:215
  248.3 5.4 %copy-start.12 = (bf16[512,4096]{1,0:T(8,128)(2,1)}, bf16[512,4096]{1,0:T(8,128)(2,1)S(1)}, u32[]{:S(2)}) copy-start(bf16[512,4096]{1,0:T(8,128)(2,1)S(1)} %constant_dynamic-update-slice_fusion.2) | copy-start | bytes 12582916
  249.9 23.5 %collective-permute-start.16 = (bf16[64,4096]{1,0:T(8,128)(2,1)}, bf16[64,4096]{1,0:T(8,128)(2,1)}, u32[]{:S(2)}, u32[]{:S(2)}) collective-permute-start(bf16[64,4096]{1,0:T(8,128)(2,1)} %slice.67), channel_id=1, source_target_pairs={{0,2},{1,3},{2,0},{3,1},{4,6},{5,7},{6,4},{7,5},{8,10},{9,11},{10,... | collective-permute-start | bytes 1572872 | tf_op jit(solution)/shard_map/ppermute | solution.py:215
  252.5 10.0 %copy-start.23 = (bf16[4,4096,1]{1,0,2:T(4,128)(2,1)S(1)}, bf16[4,4096,1]{1,0,2:T(4,128)(2,1)}, u32[]{:S(2)}) copy-start(bf16[4,4096,1]{1,0,2:T(4,128)(2,1)} %get-tuple-element.31) | copy-start | bytes 98308
  269.2 9.7 %copy-start.22 = (bf16[4,4096,1]{1,0,2:T(4,128)(2,1)S(1)}, bf16[4,4096,1]{1,0,2:T(4,128)(2,1)}, u32[]{:S(2)}) copy-start(bf16[4,4096,1]{1,0,2:T(4,128)(2,1)} %get-tuple-element.28) | copy-start | bytes 98308
  298.3 7.7 %copy-start.5 = (bf16[2,512,512]{2,1,0:T(8,128)(2,1)S(1)}, bf16[2,512,512]{2,1,0:T(8,128)(2,1)}, u32[]{:S(2)}) copy-start(bf16[2,512,512]{2,1,0:T(8,128)(2,1)} %copy-done.4) | copy-start | bytes 3145732
  298.3 7.7 %copy-start.9 = (f32[512,1024]{1,0:T(8,128)S(1)}, f32[512,1024]{1,0:T(8,128)}, u32[]{:S(2)}) copy-start(f32[512,1024]{1,0:T(8,128)} %shard_map.100.refs_5_) | copy-start | bytes 6291460
  317.4 3.6 %collective-permute-start.30 = (f32[1,32]{1,0:T(1,128)S(1)}, f32[1,32]{1,0:T(1,128)S(1)}, u32[]{:S(2)}, u32[]{:S(2)}) collective-permute-start(f32[1,32]{1,0:T(1,128)S(1)} %bitcast.235), channel_id=1, source_target_pairs={{0,2},{1,3},{2,0},{3,1},{4,6},{5,7},{6,4},{7,5},{8,10},{9,11},{10,... | collective-permute-start | bytes 392 | tf_op jit(solution)/shard_map/ppermute | solution.py:215
  318.8 4.4 %collective-permute-start.31 = (f32[1,32]{1,0:T(1,128)S(1)}, f32[1,32]{1,0:T(1,128)S(1)}, u32[]{:S(2)}, u32[]{:S(2)}) collective-permute-start(f32[1,32]{1,0:T(1,128)S(1)} %bitcast.236), channel_id=1, source_target_pairs={{0,3},{1,2},{2,1},{3,0},{4,7},{5,6},{6,5},{7,4},{8,11},{9,10},{10,... | collective-permute-start | bytes 392 | tf_op jit(solution)/shard_map/ppermute | solution.py:215
  320.2 3.5 %collective-permute-start.29 = (f32[1,32]{1,0:T(1,128)S(1)}, f32[1,32]{1,0:T(1,128)S(1)}, u32[]{:S(2)}, u32[]{:S(2)}) collective-permute-start(f32[1,32]{1,0:T(1,128)S(1)} %bitcast.237), channel_id=1, source_target_pairs={{0,1},{1,0},{2,3},{3,2},{4,5},{5,4},{6,7},{7,6},{8,9},{9,8},{10,11... | collective-permute-start | bytes 392 | tf_op jit(solution)/shard_map/ppermute | solution.py:215
  323.8 5.3 %collective-permute-start.33 = (f32[1,32]{1,0:T(1,128)S(1)}, f32[1,32]{1,0:T(1,128)S(1)}, u32[]{:S(2)}, u32[]{:S(2)}) collective-permute-start(f32[1,32]{1,0:T(1,128)S(1)} %add_add_fusion.1), channel_id=1, source_target_pairs={{0,8},{1,9},{2,10},{3,11},{4,12},{5,13},{6,14},{7,15},{8,16},{9,17... | collective-permute-start | bytes 392 | tf_op jit(solution)/shard_map/ppermute | solution.py:215
  323.8 5.3 %collective-permute-start.34 = (f32[1,32]{1,0:T(1,128)S(1)}, f32[1,32]{1,0:T(1,128)S(1)}, u32[]{:S(2)}, u32[]{:S(2)}) collective-permute-start(f32[1,32]{1,0:T(1,128)S(1)} %add_add_fusion.1), channel_id=1, source_target_pairs={{0,24},{1,25},{2,26},{3,27},{4,28},{5,29},{6,30},{7,31},{8,0},{9,1... | collective-permute-start | bytes 392 | tf_op jit(solution)/shard_map/ppermute | solution.py:215
  327.6 4.4 %collective-permute-start.32 = (f32[1,32]{1,0:T(1,128)S(1)}, f32[1,32]{1,0:T(1,128)S(1)}, u32[]{:S(2)}, u32[]{:S(2)}) collective-permute-start(f32[1,32]{1,0:T(1,128)S(1)} %add_add_fusion.1), channel_id=1, source_target_pairs={{0,16},{1,17},{2,18},{3,19},{4,20},{5,21},{6,22},{7,23},{8,24},{9,... | collective-permute-start | bytes 392 | tf_op jit(solution)/shard_map/ppermute | solution.py:215
  332.1 1.1 collective-permute-start.35
  (15 other events, 41.3 us)

commit v2 on v1

v2 whole, which is shorter than its diff:
```python
import jax
import jax.numpy as jnp
from jax import lax
from jax.experimental import pallas as pl
from jax.experimental.pallas import tpu as pltpu
from jax.sharding import PartitionSpec as P

sigma_perturb = 0.004
learn_rate = 0.0016
AXES = ("pop", "mp")
CORES = 2


def shift_down(number, amount):
    return lax.shift_right_logical(number, jnp.full_like(number, amount))


def mix_bits(number):
    number = number ^ shift_down(number, 16)
    number = number * 2146121005
    number = number ^ shift_down(number, 15)
    number = number * -2073254261
    return number ^ shift_down(number, 16)


def factor_rows(seed_list, counter_list, slot, positions):
    anchor = mix_bits(
        seed_list * 1103515245 + mix_bits(counter_list * 668265263 + slot * 374761393)
    )
    hashed = mix_bits(anchor[:, None] + positions[None, :] * -1640531535)
    uniform_part = shift_down(hashed, 8).astype(jnp.float32) * (1.0 / 16777216.0)
    return (2.0 * uniform_part - 1.0 + 1.0 / 16777216.0) * 1.7320508075688772


def fresh_weights(gate_weight, up_weight, seeds, counters, ranks, row_start, column_ids):
    members_all = seeds.shape[0]
    fitness = (ranks.astype(jnp.float32) + 0.5) / members_all - 0.5
    scaling = learn_rate / (members_all * sigma_perturb)
    row_ids = row_start + jnp.arange(gate_weight.shape[0], dtype=jnp.int32)

    def fresh(weight, slot):
        right = factor_rows(seeds, counters, slot + 1, column_ids).astype(jnp.bfloat16)
        left = (factor_rows(seeds, counters, slot, row_ids) * fitness[:, None]).astype(jnp.bfloat16)
        update = scaling * jnp.dot(left.T, right, preferred_element_type=jnp.float32)
        return (weight.astype(jnp.float32) + update).astype(jnp.bfloat16)

    return fresh(gate_weight, 0), fresh(up_weight, 2)


def normalized(rewards):
    reward_mean = jnp.mean(rewards)
    reward_var = jnp.mean((rewards - reward_mean) ** 2)
    return (rewards - reward_mean) / jnp.sqrt(reward_var + 1e-05)


def gathered_plan(
    prompts, gate_weight, up_weight, reward_head, member_seeds, counters, member_ranks
):
    members_here, seq_len, width = prompts.shape
    own_rows, own_cols = gate_weight.shape
    pop_index = lax.axis_index("pop")
    column_ids = lax.axis_index("mp") * own_cols + jnp.arange(own_cols, dtype=jnp.int32)
    small = lax.all_gather(
        jnp.stack([member_seeds, counters, member_ranks]), "pop", axis=1, tiled=True
    )
    new_gate, new_up = fresh_weights(
        gate_weight, up_weight, small[0], small[1], small[2], pop_index * own_rows, column_ids
    )
    flat_rows = prompts.reshape(members_here * seq_len, width)
    later = counters + 1
    positions = jnp.arange(width, dtype=jnp.int32)

    def projected(weight, slot):
        base = jnp.dot(
            flat_rows,
            lax.all_gather(weight, "pop", axis=0, tiled=True),
            preferred_element_type=jnp.float32,
        ).reshape(members_here, seq_len, own_cols)
        vector = factor_rows(member_seeds, later, slot, positions).astype(jnp.bfloat16)
        column = factor_rows(member_seeds, later, slot + 1, column_ids)
        proj = jnp.einsum("mld,md->ml", prompts, vector, preferred_element_type=jnp.float32)
        return base + sigma_perturb * proj[:, :, None] * column[:, None, :]

    hidden = (jax.nn.silu(projected(new_gate, 0)) * projected(new_up, 2)).astype(jnp.bfloat16)
    partial = jnp.einsum("mlf,f->m", hidden, reward_head, preferred_element_type=jnp.float32)
    rewards = lax.all_gather(lax.psum(partial, "mp"), "pop", axis=0, tiled=True) / seq_len
    own = lax.dynamic_slice_in_dim(normalized(rewards), pop_index * members_here, members_here)
    return new_gate, new_up, own


def product_kernel(plan, counts, finish, starts_ref, *refs):
    refs = list(refs)
    x_refs, w_refs, base_refs = [[refs.pop(0) for _ in range(count)] for count in counts]
    if finish:
        proj_ref, col_ref, head_ref = [refs.pop(0) for _ in range(3)]
        head = head_ref[...].astype(jnp.float32)
    out_ref = refs.pop(0)
    columns = w_refs[0].shape[2]
    for i, (segments, first_chunk, base) in enumerate(plan):
        values = [None, None]
        for k in range(first_chunk, len(w_refs)):
            depth = w_refs[k].shape[1]
            at = pl.ds(pl.multiple_of(starts_ref[k], depth), depth)
            rows = [x_refs[x][pl.ds(first, count), at] for x, first, count in segments]
            rows = rows[0] if len(rows) == 1 else jnp.concatenate(rows)
            for part in range(2):
                term = jnp.dot(rows, w_refs[k][part], preferred_element_type=jnp.float32)
                values[part] = term if values[part] is None else values[part] + term
        seq = values[0].shape[0]
        for part in range(2):
            if base is not None:
                at = pl.ds(base[1], seq)
                values[part] += base_refs[base[0]][at, part * columns : (part + 1) * columns]
            if not finish:
                out_ref[i * seq : (i + 1) * seq, part * columns : (part + 1) * columns] = values[part]
        if finish:
            gate, up = [
                values[part]
                + sigma_perturb
                * proj_ref[i * seq : (i + 1) * seq, part : part + 1]
                * col_ref[part, i : i + 1, :]
                for part in range(2)
            ]
            hidden = (gate / (1.0 + jnp.exp(-gate)) * up).astype(jnp.bfloat16)
            terms = hidden.astype(jnp.float32) * head
            out_ref[i] = jnp.sum(terms.reshape(seq // 8, 8, columns), axis=0)


def product(members, chunks, finish=None):
    depths = [chunk.shape[1] for _, chunk in chunks]
    columns = chunks[0][1].shape[2]
    arrays, base_arrays, plan = [], [], []

    def number(array, known):
        for i, other in enumerate(known):
            if other is array:
                return i
        known.append(array)
        return len(known) - 1

    for segments, first_chunk, base in members:
        placed = [(number(a, arrays), first, rows) for a, first, rows in segments]
        plan.append((placed, first_chunk, base and (number(base[0], base_arrays), base[1])))
    seq = sum(rows for _, _, rows in members[0][0])
    total = seq * len(members)
    work = sum(seq * sum(depths[first:]) for _, first, _ in members)
    vmem = pl.BlockSpec(memory_space=pltpu.VMEM)
    operands = [
        *arrays,
        *[chunk for _, chunk in chunks],
        *base_arrays,
        *(finish or ()),
    ]
    shape = (len(members), 8, columns) if finish else (total, 2 * columns)
    held = sum(a.size * a.dtype.itemsize for a in operands) + 4 * total * 2 * columns
    counts = [len(arrays), len(chunks), len(base_arrays)]
    return pl.pallas_call(
        lambda *refs: product_kernel(plan, counts, finish, *refs),
        out_shape=jax.ShapeDtypeStruct(shape, jnp.float32),
        in_specs=[pl.BlockSpec(memory_space=pltpu.SMEM)] + [vmem] * len(operands),
        out_specs=vmem,
        compiler_params=pltpu.CompilerParams(vmem_limit_bytes=held + 4 * 1024 * 1024),
        cost_estimate=pl.CostEstimate(
            flops=4 * work * columns,
            bytes_accessed=2 * work + 16 * total * columns + 4 * sum(depths) * columns,
            transcendentals=total * columns if finish else 0,
        ),
    )(jnp.stack([start for start, _ in chunks]), *operands)


def tree_sum(terms):
    while len(terms) > 1:
        half = len(terms) // 2
        terms = [terms[i] + terms[i + half] for i in range(half)]
    return terms[0]


def spread_plan(planes, prompts, gate_weight, up_weight, reward_head, member_seeds, counters, member_ranks):
    members_here, seq, width = prompts.shape
    own_rows, own_cols = gate_weight.shape
    n_mp = members_here
    pop_index = lax.axis_index("pop")
    mp_index = lax.axis_index("mp")
    z, core = pop_index // CORES, pop_index % CORES
    block = own_cols // planes

    def pairs(move, keep=lambda z: True):
        out = []
        for a in range(planes):
            for c in range(CORES):
                for m in range(n_mp):
                    target = move(a, c, m)
                    if keep(a) and 0 <= target[0] < planes:
                        source = (a * CORES + c) * n_mp + m
                        out.append((source, (target[0] * CORES + target[1]) * n_mp + target[2]))
        return out

    def send(value, move, keep=lambda z: True):
        return lax.ppermute(value, AXES, pairs(move, keep))

    def swap_core(value):
        return send(value, lambda a, c, m: (a, 1 - c, m))

    def swap_in_plane(value, bit):
        return send(value, lambda a, c, m: (a, c, m ^ bit))

    def turn(value, s):
        return send(value, lambda a, c, m: ((a + s) % planes, c, m))

    def tie(*values):
        return lax.optimization_barrier(values)

    def up(value, s):
        return send(value, lambda a, c, m: (a + 1, c, m), lambda a: a >= s - 1)

    def down(value, s):
        return send(value, lambda a, c, m: (a - 1, c, m), lambda a: a <= planes - s)

    arrivals = []
    for a in range(planes):
        order = []
        for s in range(1, planes):
            if a - s >= 0:
                order.append((0, s, a - s))
            if a + s < planes:
                order.append((1, s, a + s))
        arrivals.append(order)

    def by_plane(numbers):
        value = jnp.int32(numbers[0])
        for a in range(1, planes):
            value = jnp.where(z == a, numbers[a], value)
        return value

    def round_block(r):
        picks = {}
        for a in range(planes):
            picks.setdefault(arrivals[a][r - 1][:2], []).append(a)
        chosen = None
        for (way, s), where in picks.items():
            here = z == where[0]
            for a in where[1:]:
                here = here | (z == a)
            value = hops[way][s]
            chosen = value if chosen is None else jnp.where(here, value, chosen)
        return chosen

    def piece(weights, s, first, count):
        corner = (first, (z + s) % planes * block)
        return jnp.stack([lax.dynamic_slice(w, corner, (count, block)) for w in weights])

    small = jnp.stack([member_seeds, counters, member_ranks])
    own_member = lax.dynamic_index_in_dim(prompts, mp_index, 0, keepdims=False)
    hops = [[own_member, up(own_member, 1)], [own_member, down(own_member, 1)]]
    small_here = jnp.stack([small] + [turn(small, s) for s in range(1, planes)])
    small_other = swap_core(small_here)
    every = jnp.concatenate([small_here, small_other]).transpose(1, 0, 2).reshape(3, -1)
    head = lax.dynamic_slice_in_dim(reward_head, z * block, block).reshape(1, block)
    my_columns = mp_index * own_cols + z * block + jnp.arange(block, dtype=jnp.int32)
    positions = jnp.arange(width, dtype=jnp.int32)
    lanes = jnp.arange(members_here, dtype=jnp.int32)

    rel = mp_index ^ lanes
    rel_hot = (rel[:, None] == lanes[None, :]).astype(jnp.int32)
    flat = prompts.reshape(members_here * seq, width)
    members = [[(flat, i * seq, seq)] for i in range(members_here)]
    group_ids = [pop_index * members_here + lanes]
    picked = [(member_seeds, counters)]
    for r in range(1, planes):
        source = by_plane([arrivals[a][r - 1][2] for a in range(planes)])
        back = (z - source) % planes
        chosen = jnp.int32(0)
        for s in range(1, planes):
            chosen = jnp.where(back == s, small_here[s], chosen)
        chosen = jnp.sum(rel_hot[None] * chosen[:, None, :], axis=2)
        picked.append((chosen[0], chosen[1]))
        group_ids.append((source * CORES + core) * members_here + rel)

    def perturbed(r):
        seeds, counts = picked[r]
        vectors = jnp.stack(
            [factor_rows(seeds, counts + 1, slot, positions).astype(jnp.bfloat16) for slot in (0, 2)],
            axis=1,
        )
        found = [
            lax.dot_general(
                array[first : first + rows],
                vectors[i],
                (((1,), (1,)), ((), ())),
                preferred_element_type=jnp.float32,
            )
            for i in range(members_here)
            for array, first, rows in members[r * members_here + i]
        ]
        columns = [factor_rows(seeds, counts + 1, slot + 1, my_columns) for slot in (0, 2)]
        return jnp.concatenate(found), jnp.stack(columns)

    projs, cols = map(lambda v: [v], perturbed(0))

    column_ids = mp_index * own_cols + jnp.arange(own_cols, dtype=jnp.int32)
    weights = fresh_weights(
        gate_weight, up_weight, every[0], every[1], every[2], pop_index * own_rows, column_ids
    )
    new_gate, new_up = weights
    far_first = sorted(range(1, planes), key=lambda s: (-min(s, planes - s), s))
    half_rows = own_rows // 2
    queue = [(s, 0, own_rows) for s in far_first[:-1]]
    queue += [(far_first[-1], first, half_rows) for first in (0, half_rows)]
    leave = {planes - 2: queue[:1], planes - 1: queue[1:-1], planes: queue[-1:]}
    outgoing = {key: piece(weights, *key) for key in queue}
    landed = {(0, 0, own_rows): piece(weights, 0, 0, own_rows)}
    chunks = []

    def add_chunks(key):
        s, first, _ = key
        plane = (z - s) % planes * CORES
        return [
            ((plane + core) * own_rows + first, landed[key]),
            ((plane + 1 - core) * own_rows + first, swap_core(landed[key])),
        ]

    half = seq // 2
    fresh = [(0, 0, own_rows)]
    across_x = across_y = corner_x = corner_y = None
    bases, held_back, early = [], 0, 0

    def on(some, first_chunk, base=None):
        return [
            (m, first_chunk, base if base is None else (base, i * seq)) for i, m in enumerate(some)
        ]

    hops[0][1], hops[1][1] = tie(hops[0][1], hops[1][1])
    for phase in range(1, planes + 1):
        if phase < planes - 1:
            hops[0].append(up(hops[0][phase], phase + 1))
            hops[1].append(down(hops[1][phase], phase + 1))
        to_x, to_y = [], []
        if phase < planes:
            here = round_block(phase)
            to_x.append(here)
            to_y.append(here)
        if phase > 1:
            to_x.append(across_y[:half])
            to_y.append(across_x[half:seq])
        new_x = swap_in_plane(jnp.concatenate(to_x), 1)
        new_y = swap_in_plane(jnp.concatenate(to_y), 2)
        for key in leave.get(phase, ()):
            landed[key] = turn(outgoing[key], key[0])
        new_chunks = [c for key in fresh for c in add_chunks(key)]
        fresh = leave.get(phase, ())
        known = chunks + new_chunks
        if phase == planes - 1:
            early = len(members)
            bases = [product(on(members, 0), known)]
            held_back = len(known)
        elif phase == planes:
            bases.append(product(on(members[:early], 0, bases[0]), known[held_back:]))
            bases.append(product(on(members[early:], 0), known))
        parts = (hops, new_x, new_y, landed, new_chunks, outgoing, bases)
        hops, new_x, new_y, landed, new_chunks, outgoing, bases = tie(*parts)
        chunks += new_chunks
        if phase > 1:
            first = seq if phase < planes else 0
            members.append([(new_x, first, half), (new_y, first, half)])
            proj, col = perturbed(phase - 1)
            projs.append(proj)
            cols.append(col)
        if phase < planes:
            members += [[(here, 0, seq)], [(new_x, 0, seq)], [(new_y, 0, seq)]]
        across_x, across_y = new_x, new_y

    last = [c for key in fresh for c in add_chunks(key)]
    plan = on(members[:early], len(chunks), bases[1])
    plan += on(members[early:-1], len(chunks), bases[2]) + on(members[-1:], 0)
    finish = (jnp.concatenate(projs), jnp.concatenate(cols, axis=1), head)
    sums = product(plan, chunks + last, finish).reshape(len(members), -1).sum(axis=1)

    ids = jnp.concatenate(group_ids)
    total = planes * CORES * members_here
    rewards = jnp.sum(
        jnp.where(ids[:, None] == jnp.arange(total, dtype=jnp.int32)[None, :], sums[:, None], 0.0),
        axis=0,
    ).reshape(1, total)
    rewards = (rewards + swap_in_plane(rewards, 1)) + (
        swap_in_plane(rewards, 2) + swap_in_plane(rewards, 3)
    )
    rewards = tree_sum([rewards] + [turn(rewards, s) for s in range(1, planes)])
    rewards = (rewards + swap_core(rewards)).reshape(total) / seq
    own = lax.dynamic_slice_in_dim(normalized(rewards), pop_index * members_here, members_here)
    return new_gate, new_up, own


def solution(mesh):
    n_pop, n_mp = mesh.shape["pop"], mesh.shape["mp"]
    planes = n_pop // CORES

    def shards(prompts, gate_weight, *rest):
        members_here, seq, width = prompts.shape
        own_cols = gate_weight.shape[1]
        gathered = 2 * width * own_cols + members_here * seq * width
        spread = 2 * width * own_cols // planes + planes * members_here * seq * width
        square = n_mp == 4 and members_here == n_mp and planes & (planes - 1) == 0
        if square and own_cols % (128 * planes) == 0 and spread < gathered:
            return spread_plan(planes, prompts, gate_weight, *rest)
        return gathered_plan(prompts, gate_weight, *rest)

    in_specs = (
        P("pop", None, None),
        P("pop", "mp"),
        P("pop", "mp"),
        P("mp"),
        P("pop"),
        P("pop"),
        P("pop"),
    )
    out_specs = (P("pop", "mp"), P("pop", "mp"), P("pop"))
    return jax.shard_map(shards, mesh=mesh, in_specs=in_specs, out_specs=out_specs, check_vma=False)
```

time: 337 us -> 235 us (0.70)
  waiting for transfers between devices: 179 us -> 97 us
  Pallas kernels: 44.6 us -> 33.9 us
  local copies, waits for them, and re-layouts: 33.2 us -> 24.9 us
  other arithmetic: 14.4 us -> 10.7 us
  matrix products: 17.5 us -> 21 us
    ppermute x36 -> x34, waiting for transfers between devices: 179 us -> 97 us  [send(): return lax.ppermute(value, AXES, pairs(move, keep))]
    pallas_call x8 -> x4, Pallas kernels: 44.6 us -> 33.9 us  [product(): pl.pallas_call(lambda *refs: product_kernel(plan, counts, finish, *refs),...]
    slice x6, local copies, waits for them, and re-layouts: 7.07 us -> 1.83 us  [the longest x3 0.92 us: spread_plan(): to_x.append(across_y[:half])]
    unnamed x1 -> x0, other arithmetic: 4.85 us -> none
    dot_general x8 -> x19, matrix products: 14.2 us -> 17.6 us  [perturbed(): lax.dot_general(array[first:first + rows], vectors[i], (((1,), (1,)), (()...]
    ppermute x36 -> x34, starting transfers between devices: 44.7 us -> 43.8 us  [send(): return lax.ppermute(value, AXES, pairs(move, keep))]
    unnamed x63 -> x104, local copies, waits for them, and re-layouts: 16.7 us -> 17.2 us
  transfers between devices with their start and end apart: 36 -> 34, of which waited for: 20 -> 13; matrix products, arithmetic and copies ran while one was open for 15% -> 15% of each run, Pallas kernels for 3% -> 9%
where the time goes in v2:
time: 235 us; the launch traced here: 234 us
  waiting for transfers between devices  97 us (41%)
  starting transfers between devices  43.8 us (19%)
  Pallas kernels  33.9 us (14%)
  local copies, waits for them, and re-layouts  24.9 us (11%)
  matrix products  21 us (9%)
  other arithmetic  10.7 us (5%)
  between operations  3.13 us (1%)
    ppermute x34, waiting for transfers between devices, send(): return lax.ppermute(value, AXES, pairs(move, keep))  97 us
    ppermute x34, starting transfers between devices, send(): return lax.ppermute(value, AXES, pairs(move, keep))  43.8 us
    pallas_call x4, Pallas kernels, product(): pl.pallas_call(lambda *refs: product_kernel(plan, counts, finish, *refs),...  33.9 us
    dot_general x19, matrix products, perturbed(): lax.dot_general(array[first:first + rows], vectors[i], (((1,), (1,)), (()...  17.6 us
    unnamed x104, local copies, waits for them, and re-layouts  17.2 us
  transfers between devices with their start and end apart: 34, of which 13 were waited for; matrix products, arithmetic and copies ran while one was open for 15% of the time, Pallas kernels for 9%

profile of v2, /device:TPU:0, one launch (start us, length us, event | category | flops | bytes accessed | tf_op | source)
XLA Modules:
  0.0 234.4 jit_solution(13143720665428069155)
XLA Ops:
  1.4 3.0 %collective-permute-start = (s32[3,4]{1,0:T(4,128)S(1)}, s32[3,4]{1,0:T(4,128)S(1)}, u32[]{:S(2)}, u32[]{:S(2)}) collective-permute-start(s32[3,4]{1,0:T(4,128)S(1)} %get-tuple-element.165), channel_id=1, source_target_pairs={{0,8},{1,9},{2,10},{3,11},{4,12},{5,13},{6,14},{7,15},{8,16},{9,17... | collective-permute-start | bytes 152 | tf_op jit(solution)/shard_map/ppermute | solution.py:199
  4.4 2.6 %collective-permute-start.1 = (s32[3,4]{1,0:T(4,128)S(1)}, s32[3,4]{1,0:T(4,128)S(1)}, u32[]{:S(2)}, u32[]{:S(2)}) collective-permute-start(s32[3,4]{1,0:T(4,128)S(1)} %get-tuple-element.165), channel_id=1, source_target_pairs={{0,16},{1,17},{2,18},{3,19},{4,20},{5,21},{6,22},{7,23},{8,24},{9,... | collective-permute-start | bytes 152 | tf_op jit(solution)/shard_map/ppermute | solution.py:199
  7.0 1.3 collective-permute-start.2
  8.4 1.3 dynamic-slice_bitcast_fusion
  9.7 3.6 %collective-permute-start.4 = (bf16[128,4096]{1,0:T(8,128)(2,1)S(1)}, bf16[128,4096]{1,0:T(8,128)(2,1)}, u32[]{:S(2)}, u32[]{:S(2)}) collective-permute-start(bf16[128,4096]{1,0:T(8,128)(2,1)S(1)} %dynamic-slice_bitcast_fusion), channel_id=1, source_target_pairs={{0,8},{1,9},{2,10},{3,11},{4,12},{5,13},{6,14},{7,15},{8,16},{9,17... | collective-permute-start | bytes 3145736 | tf_op jit(solution)/shard_map/ppermute | solution.py:199
  13.2 1.3 collective-permute-start.5
  20.0 2.2 convolution_bitcast_fusion.3
  22.2 2.2 convolution_bitcast_fusion.2
  24.4 2.2 convolution_bitcast_fusion.1
  28.4 2.6 %add_convert_fusion.1 = bf16[512,2048]{1,0:T(8,128)(2,1)S(1)} fusion(bf16[512,2048]{1,0:T(8,128)(2,1)} %param.8, s32[2048]{0:T(1024)S(1)} %add_multiply_fusion, s32[32]{0:T(128)S(1)} %get-tuple-element.173, f32[32]{0:T(128)S(1)} %reshape.1830, s32[512]{0:T(512)S(1)} %add_multiply_fusion.2, s32[32]{0:T(128)S(1)} %get-tuple-element.174), kind=kOutput, calls=%fused_computation.1 | convolution fusion | flops 72531968 | bytes 4204928 | tf_op jit(solution)/shard_map/dot_general | solution.py:44
  33.8 5.1 %collective-permute-done.5 = bf16[128,4096]{1,0:T(8,128)(2,1)S(1)} collective-permute-done((bf16[128,4096]{1,0:T(8,128)(2,1)S(1)}, bf16[128,4096]{1,0:T(8,128)(2,1)S(1)}, u32[]{:S(2)}, u32[]{:S(2)}) %collective-permute-start.5) | collective-permute-done | bytes 1048608 | tf_op jit(solution)/shard_map/ppermute | solution.py:199
  39.6 1.3 collective-permute-start.7
  41.0 1.6 collective-permute-start.8
  42.6 1.5 collective-permute-start.9
  45.5 18.8 %collective-permute-done.7 = bf16[128,4096]{1,0:T(8,128)(2,1)S(1)} collective-permute-done((bf16[128,4096]{1,0:T(8,128)(2,1)S(1)}, bf16[128,4096]{1,0:T(8,128)(2,1)S(1)}, u32[]{:S(2)}, u32[]{:S(2)}) %collective-permute-start.7) | collective-permute-done | bytes 1048608 | tf_op jit(solution)/shard_map/ppermute | solution.py:199
  66.7 1.5 collective-permute-start.14
  69.8 1.3 collective-permute-start.12
  71.1 4.0 %collective-permute-start.15 = (bf16[2,512,512]{2,1,0:T(8,128)(2,1)S(1)}, bf16[2,512,512]{2,1,0:T(8,128)(2,1)S(1)}, u32[]{:S(2)}, u32[]{:S(2)}) collective-permute-start(bf16[2,512,512]{2,1,0:T(8,128)(2,1)S(1)} %pad_maximum_fusion.6), channel_id=1, source_target_pairs={{0,16},{1,17},{2,18},{3,19},{4,20},{5,21},{6,22},{7,23},{8,24},{9,... | collective-permute-start | bytes 3145736 | tf_op jit(solution)/shard_map/ppermute | solution.py:199
  76.7 18.6 %collective-permute-done.12 = bf16[128,4096]{1,0:T(8,128)(2,1)S(1)} collective-permute-done((bf16[128,4096]{1,0:T(8,128)(2,1)S(1)}, bf16[128,4096]{1,0:T(8,128)(2,1)S(1)}, u32[]{:S(2)}, u32[]{:S(2)}) %collective-permute-start.12) | collective-permute-done | bytes 1048608 | tf_op jit(solution)/shard_map/ppermute | solution.py:199
  95.4 21.2 %collective-permute-done.15.refs_10_.refs_6_.refs_15_ = bf16[2,512,512]{2,1,0:T(8,128)(2,1)S(1)} collective-permute-done((bf16[2,512,512]{2,1,0:T(8,128)(2,1)S(1)}, bf16[2,512,512]{2,1,0:T(8,128)(2,1)S(1)}, u32[]{:S(2)}, u32[]{:S(2)}) %collective-permute-start.15) | collective-permute-done | bytes 1048608 | tf_op jit(solution)/shard_map/ppermute | solution.py:199
  117.3 1.5 collective-permute-start.16
  119.8 3.8 %collective-permute-start.19 = (bf16[2,256,512]{2,1,0:T(8,128)(2,1)S(1)}, bf16[2,256,512]{2,1,0:T(8,128)(2,1)}, u32[]{:S(2)}, u32[]{:S(2)}) collective-permute-start(bf16[2,256,512]{2,1,0:T(8,128)(2,1)S(1)} %pad_maximum_fusion.7), channel_id=1, source_target_pairs={{0,24},{1,25},{2,26},{3,27},{4,28},{5,29},{6,30},{7,31},{8,0},{9,1... | collective-permute-start | bytes 1572872 | tf_op jit(solution)/shard_map/ppermute | solution.py:199
  124.7 6.7 %shard_map.94.refs_12_ = f32[1408,1024]{1,0:T(8,128)S(1)} custom-call(s32[4]{0:T(128)S(1)} %pad_add_fusion.3.refs_0_, bf16[512,4096]{1,0:T(8,128)(2,1)S(1)} %bitcast.230, bf16[128,4096]{1,0:T(8,128)(2,1)S(1)} %broadcast_select_fusion.refs_2_, bf16[128,4096]{1,0:T(8,128)(2,1)S(1)} %collective-permute-done.8.refs_3_, ...), custom_call_target="tpu_custom_call" | custom-call | flops 5905580032 | bytes 21495808 | tf_op jit(solution)/shard_map/pallas_call | solution.py:157
  131.4 2.5 %copy-done.13 = f32[1408,1024]{1,0:T(8,128)} copy-done((f32[1408,1024]{1,0:T(8,128)}, f32[1408,1024]{1,0:T(8,128)S(1)}, u32[]{:S(2)}) %copy-start.13) | copy-done | bytes 5767192
  133.9 23.0 %collective-permute-done.19.refs_10_.refs_19_ = bf16[2,256,512]{2,1,0:T(8,128)(2,1)} collective-permute-done((bf16[2,256,512]{2,1,0:T(8,128)(2,1)S(1)}, bf16[2,256,512]{2,1,0:T(8,128)(2,1)}, u32[]{:S(2)}, u32[]{:S(2)}) %collective-permute-start.19) | collective-permute-done | bytes 524320 | tf_op jit(solution)/shard_map/ppermute | solution.py:199
  159.9 1.5 collective-permute-start.22
  161.4 1.9 collective-permute-start.23
  163.7 1.7 fusion.6
  165.4 1.6 fusion.4
  167.1 1.5 copy-done.20
  168.7 1.7 copy-done.23
  170.3 1.2 copy-done.26
  171.5 1.2 copy-done.28
  172.8 5.9 %shard_map.96.refs_24_ = f32[512,1024]{1,0:T(8,128)S(1)} custom-call(s32[8]{0:T(128)S(1)} %stack.218.refs_0_, bf16[192,4096]{1,0:T(8,128)(2,1)S(1)} %copy-done.18, bf16[192,4096]{1,0:T(8,128)(2,1)S(1)} %copy-done.20, bf16[128,4096]{1,0:T(8,128)(2,1)S(1)} %select_select_fusion.refs_3_.refs_10_, bf16[2,512,512]{2,1,0:T(8,128)(2,1)S(1)} %copy-done.15, ...), custom_call_target="tpu_custom_call" | custom-call | flops 3758096384 | bytes 15204352 | tf_op jit(solution)/shard_map/pallas_call | solution.py:157
  178.7 1.4 copy-done.21
  180.2 8.3 %shard_map.95.refs_23_ = f32[1408,1024]{1,0:T(8,128)S(1)} custom-call(s32[4]{0:T(128)S(1)} %pad_add_fusion.4.refs_0_, bf16[512,4096]{1,0:T(8,128)(2,1)S(1)} %bitcast.231, bf16[128,4096]{1,0:T(8,128)(2,1)S(1)} %broadcast_select_fusion.refs_2_, bf16[128,4096]{1,0:T(8,128)(2,1)S(1)} %copy-done.4, bf16[128,4096]{1,0:T(8,128)(2,1)S(1)} %copy-done.7, ...), custom_call_target="tpu_custom_call" | custom-call | flops 4429185024 | bytes 19005440 | tf_op jit(solution)/shard_map/pallas_call | solution.py:157
  188.4 2.5 %copy-done = f32[1408,1024]{1,0:T(8,128)} copy-done((f32[1408,1024]{1,0:T(8,128)}, f32[1408,1024]{1,0:T(8,128)S(1)}, u32[]{:S(2)}) %copy-start) | copy-done | bytes 5767192
  191.6 1.3 fusion.16
  192.8 1.3 fusion.178
  194.1 1.3 fusion.176
  195.6 1.4 copy.83.refs_25_
  201.9 13.1 %shard_map.97 = f32[16,8,512]{2,1,0:T(8,128)S(1)} custom-call(s32[10]{0:T(128)S(1)} %stack.225.refs_0_, bf16[512,4096]{1,0:T(8,128)(2,1)} %bitcast.229, bf16[128,4096]{1,0:T(8,128)(2,1)S(1)} %broadcast_select_fusion.refs_2_, bf16[128,4096]{1,0:T(8,128)(2,1)S(1)} %copy-done.5, bf16[128,4096]{1,0:T(8,128)(2,1)S(1)} %copy-done.8, bf16[192,4096]{1,0:T(8,128)(2,1)} %copy-done.9, ...), custom_call_target="tpu_custom_call" | custom-call | flops 3087007744 | bytes 28180480 | tf_op jit(solution)/shard_map/pallas_call | solution.py:157
  215.9 2.4 %collective-permute-start.29 = (f32[1,32]{1,0:T(1,128)S(1)}, f32[1,32]{1,0:T(1,128)S(1)}, u32[]{:S(2)}, u32[]{:S(2)}) collective-permute-start(f32[1,32]{1,0:T(1,128)S(1)} %bitcast.243), channel_id=1, source_target_pairs={{0,3},{1,2},{2,1},{3,0},{4,7},{5,6},{6,5},{7,4},{8,11},{9,10},{10,... | collective-permute-start | bytes 392 | tf_op jit(solution)/shard_map/ppermute | solution.py:199
  218.9 1.4 collective-permute-done.29
  220.3 1.5 collective-permute-done.27
  222.0 3.7 %collective-permute-start.32 = (f32[1,32]{1,0:T(1,128)S(1)}, f32[1,32]{1,0:T(1,128)S(1)}, u32[]{:S(2)}, u32[]{:S(2)}) collective-permute-start(f32[1,32]{1,0:T(1,128)S(1)} %add_add_fusion.1), channel_id=1, source_target_pairs={{0,24},{1,25},{2,26},{3,27},{4,28},{5,29},{6,30},{7,31},{8,0},{9,1... | collective-permute-start | bytes 392 | tf_op jit(solution)/shard_map/ppermute | solution.py:199
  225.7 1.5 collective-permute-done.31
  227.2 2.9 %collective-permute-done.30 = f32[1,32]{1,0:T(1,128)S(1)} collective-permute-done((f32[1,32]{1,0:T(1,128)S(1)}, f32[1,32]{1,0:T(1,128)S(1)}, u32[]{:S(2)}, u32[]{:S(2)}) %collective-permute-start.30) | collective-permute-done | bytes 160 | tf_op jit(solution)/shard_map/ppermute | solution.py:199
  (222 shorter events, 34.2 us)
Async XLA Ops:
  0.6 14.2 %copy-start.45 = (s32[4]{0:T(128)S(1)}, s32[4]{0:T(128)}, u32[]{:S(2)}) copy-start(s32[4]{0:T(128)} %param.12) | copy-start | bytes 52
  0.6 14.2 %copy-start.46 = (s32[4]{0:T(128)S(1)}, s32[4]{0:T(128)}, u32[]{:S(2)}) copy-start(s32[4]{0:T(128)} %param.11) | copy-start | bytes 52
  1.4 15.8 %collective-permute-start = (s32[3,4]{1,0:T(4,128)S(1)}, s32[3,4]{1,0:T(4,128)S(1)}, u32[]{:S(2)}, u32[]{:S(2)}) collective-permute-start(s32[3,4]{1,0:T(4,128)S(1)} %get-tuple-element.165), channel_id=1, source_target_pairs={{0,8},{1,9},{2,10},{3,11},{4,12},{5,13},{6,14},{7,15},{8,16},{9,17... | collective-permute-start | bytes 152 | tf_op jit(solution)/shard_map/ppermute | solution.py:199
  4.4 12.7 %collective-permute-start.1 = (s32[3,4]{1,0:T(4,128)S(1)}, s32[3,4]{1,0:T(4,128)S(1)}, u32[]{:S(2)}, u32[]{:S(2)}) collective-permute-start(s32[3,4]{1,0:T(4,128)S(1)} %get-tuple-element.165), channel_id=1, source_target_pairs={{0,16},{1,17},{2,18},{3,19},{4,20},{5,21},{6,22},{7,23},{8,24},{9,... | collective-permute-start | bytes 152 | tf_op jit(solution)/shard_map/ppermute | solution.py:199
  7.0 10.1 %collective-permute-start.2 = (s32[3,4]{1,0:T(4,128)S(1)}, s32[3,4]{1,0:T(4,128)S(1)}, u32[]{:S(2)}, u32[]{:S(2)}) collective-permute-start(s32[3,4]{1,0:T(4,128)S(1)} %get-tuple-element.165), channel_id=1, source_target_pairs={{0,24},{1,25},{2,26},{3,27},{4,28},{5,29},{6,30},{7,31},{8,0},{9,1... | collective-permute-start | bytes 152 | tf_op jit(solution)/shard_map/ppermute | solution.py:199
  9.7 24.1 %collective-permute-start.4 = (bf16[128,4096]{1,0:T(8,128)(2,1)S(1)}, bf16[128,4096]{1,0:T(8,128)(2,1)}, u32[]{:S(2)}, u32[]{:S(2)}) collective-permute-start(bf16[128,4096]{1,0:T(8,128)(2,1)S(1)} %dynamic-slice_bitcast_fusion), channel_id=1, source_target_pairs={{0,8},{1,9},{2,10},{3,11},{4,12},{5,13},{6,14},{7,15},{8,16},{9,17... | collective-permute-start | bytes 3145736 | tf_op jit(solution)/shard_map/ppermute | solution.py:199
  13.2 25.7 %collective-permute-start.5 = (bf16[128,4096]{1,0:T(8,128)(2,1)S(1)}, bf16[128,4096]{1,0:T(8,128)(2,1)S(1)}, u32[]{:S(2)}, u32[]{:S(2)}) collective-permute-start(bf16[128,4096]{1,0:T(8,128)(2,1)S(1)} %dynamic-slice_bitcast_fusion), channel_id=1, source_target_pairs={{8,0},{9,1},{10,2},{11,3},{12,4},{13,5},{14,6},{15,7},{16,8},{17,9... | collective-permute-start | bytes 3145736 | tf_op jit(solution)/shard_map/ppermute | solution.py:199
  17.2 10.5 %collective-permute-start.3 = (s32[4,3,4]{2,1,0:T(4,128)S(1)}, s32[4,3,4]{2,1,0:T(4,128)S(1)}, u32[]{:S(2)}, u32[]{:S(2)}) collective-permute-start(s32[4,3,4]{2,1,0:T(4,128)S(1)} %pad_add_fusion), channel_id=1, source_target_pairs={{0,4},{1,5},{2,6},{3,7},{4,0},{5,1},{6,2},{7,3},{8,12},{9,13},{10,... | collective-permute-start | bytes 584 | tf_op jit(solution)/shard_map/ppermute | solution.py:199
  31.0 13.3 %copy-start.29 = (bf16[512,2048]{1,0:T(8,128)(2,1)}, bf16[512,2048]{1,0:T(8,128)(2,1)S(1)}, u32[]{:S(2)}) copy-start(bf16[512,2048]{1,0:T(8,128)(2,1)S(1)} %add_convert_fusion.1) | copy-start | bytes 6291460
  32.3 92.3 %copy-start.14 = (bf16[2,512,512]{2,1,0:T(8,128)(2,1)}, bf16[2,512,512]{2,1,0:T(8,128)(2,1)S(1)}, u32[]{:S(2)}) copy-start(bf16[2,512,512]{2,1,0:T(8,128)(2,1)S(1)} %pad_maximum_fusion.4.refs_8_.refs_4_.refs_13_) | copy-start | bytes 3145732
  32.4 13.2 %collective-permute-start.10 = (bf16[2,512,512]{2,1,0:T(8,128)(2,1)S(1)}, bf16[2,512,512]{2,1,0:T(8,128)(2,1)S(1)}, u32[]{:S(2)}, u32[]{:S(2)}) collective-permute-start(bf16[2,512,512]{2,1,0:T(8,128)(2,1)S(1)} %pad_maximum_fusion.4.refs_8_.refs_4_.refs_13_), channel_id=1, source_target_pairs={{0,4},{1,5},{2,6},{3,7},{4,0},{5,1},{6,2},{7,3},{8,12},{9,13},{10,... | collective-permute-start | bytes 3145736 | tf_op jit(solution)/shard_map/ppermute | solution.py:199
  38.9 6.6 %collective-permute-start.6 = (bf16[128,4096]{1,0:T(8,128)(2,1)}, bf16[128,4096]{1,0:T(8,128)(2,1)S(1)}, u32[]{:S(2)}, u32[]{:S(2)}) collective-permute-start(bf16[128,4096]{1,0:T(8,128)(2,1)} %collective-permute-done.4), channel_id=1, source_target_pairs={{8,16},{9,17},{10,18},{11,19},{12,20},{13,21},{14,22},{15,23},{16,... | collective-permute-start | bytes 3145736 | tf_op jit(solution)/shard_map/ppermute | solution.py:199
  39.6 24.7 %collective-permute-start.7 = (bf16[128,4096]{1,0:T(8,128)(2,1)S(1)}, bf16[128,4096]{1,0:T(8,128)(2,1)S(1)}, u32[]{:S(2)}, u32[]{:S(2)}) collective-permute-start(bf16[128,4096]{1,0:T(8,128)(2,1)S(1)} %collective-permute-done.5), channel_id=1, source_target_pairs={{8,0},{9,1},{10,2},{11,3},{12,4},{13,5},{14,6},{15,7},{16,8},{17,9... | collective-permute-start | bytes 3145736 | tf_op jit(solution)/shard_map/ppermute | solution.py:199
  41.0 23.3 %collective-permute-start.8 = (bf16[128,4096]{1,0:T(8,128)(2,1)S(1)}, bf16[128,4096]{1,0:T(8,128)(2,1)S(1)}, u32[]{:S(2)}, u32[]{:S(2)}) collective-permute-start(bf16[128,4096]{1,0:T(8,128)(2,1)S(1)} %broadcast_select_fusion.refs_2_), channel_id=1, source_target_pairs={{0,1},{1,0},{2,3},{3,2},{4,5},{5,4},{6,7},{7,6},{8,9},{9,8},{10,11... | collective-permute-start | bytes 3145736 | tf_op jit(solution)/shard_map/ppermute | solution.py:199
  42.6 22.6 %collective-permute-start.9 = (bf16[128,4096]{1,0:T(8,128)(2,1)S(1)}, bf16[128,4096]{1,0:T(8,128)(2,1)S(1)}, u32[]{:S(2)}, u32[]{:S(2)}) collective-permute-start(bf16[128,4096]{1,0:T(8,128)(2,1)S(1)} %broadcast_select_fusion.refs_2_), channel_id=1, source_target_pairs={{0,2},{1,3},{2,0},{3,1},{4,6},{5,7},{6,4},{7,5},{8,10},{9,11},{10,... | collective-permute-start | bytes 3145736 | tf_op jit(solution)/shard_map/ppermute | solution.py:199
  44.3 119.1 %copy-start.34 = (bf16[1,2,4096]{2,0,1:T(2,128)(2,1)}, bf16[1,2,4096]{2,0,1:T(2,128)(2,1)S(1)}, u32[]{:S(2)}) copy-start(bf16[1,2,4096]{2,0,1:T(2,128)(2,1)S(1)} %get-tuple-element.120) | copy-start | bytes 49156
  45.5 79.1 %copy-start.22 = (bf16[2,512,512]{2,1,0:T(8,128)(2,1)}, bf16[2,512,512]{2,1,0:T(8,128)(2,1)S(1)}, u32[]{:S(2)}) copy-start(bf16[2,512,512]{2,1,0:T(8,128)(2,1)S(1)} %collective-permute-done.10.refs_9_.refs_5_.refs_14_) | copy-start | bytes 3145732
  64.4 60.3 %copy-start.3 = (bf16[128,4096]{1,0:T(8,128)(2,1)}, bf16[128,4096]{1,0:T(8,128)(2,1)S(1)}, u32[]{:S(2)}) copy-start(bf16[128,4096]{1,0:T(8,128)(2,1)S(1)} %collective-permute-done.8.refs_3_) | copy-start | bytes 3145732
  65.2 59.5 %copy-start.6 = (bf16[128,4096]{1,0:T(8,128)(2,1)}, bf16[128,4096]{1,0:T(8,128)(2,1)S(1)}, u32[]{:S(2)}) copy-start(bf16[128,4096]{1,0:T(8,128)(2,1)S(1)} %collective-permute-done.9.refs_4_) | copy-start | bytes 3145732
  65.9 50.7 %collective-permute-start.13 = (bf16[192,4096]{1,0:T(8,128)(2,1)S(1)}, bf16[192,4096]{1,0:T(8,128)(2,1)S(1)}, u32[]{:S(2)}, u32[]{:S(2)}) collective-permute-start(bf16[192,4096]{1,0:T(8,128)(2,1)S(1)} %get-tuple-element.115), channel_id=1, source_target_pairs={{0,1},{1,0},{2,3},{3,2},{4,5},{5,4},{6,7},{7,6},{8,9},{9,8},{10,11... | collective-permute-start | bytes 4718600 | tf_op jit(solution)/shard_map/ppermute | solution.py:199
  66.7 49.9 %collective-permute-start.14 = (bf16[192,4096]{1,0:T(8,128)(2,1)S(1)}, bf16[192,4096]{1,0:T(8,128)(2,1)S(1)}, u32[]{:S(2)}, u32[]{:S(2)}) collective-permute-start(bf16[192,4096]{1,0:T(8,128)(2,1)S(1)} %get-tuple-element.114), channel_id=1, source_target_pairs={{0,2},{1,3},{2,0},{3,1},{4,6},{5,7},{6,4},{7,5},{8,10},{9,11},{10,... | collective-permute-start | bytes 4718600 | tf_op jit(solution)/shard_map/ppermute | solution.py:199
  69.1 7.7 %collective-permute-start.11 = (bf16[128,4096]{1,0:T(8,128)(2,1)S(1)}, bf16[128,4096]{1,0:T(8,128)(2,1)S(1)}, u32[]{:S(2)}, u32[]{:S(2)}) collective-permute-start(bf16[128,4096]{1,0:T(8,128)(2,1)S(1)} %collective-permute-done.6), channel_id=1, source_target_pairs={{16,24},{17,25},{18,26},{19,27},{20,28},{21,29},{22,30},{23,31}} | collective-permute-start | bytes 3145736 | tf_op jit(solution)/shard_map/ppermute | solution.py:199
  69.8 25.6 %collective-permute-start.12 = (bf16[128,4096]{1,0:T(8,128)(2,1)S(1)}, bf16[128,4096]{1,0:T(8,128)(2,1)S(1)}, u32[]{:S(2)}, u32[]{:S(2)}) collective-permute-start(bf16[128,4096]{1,0:T(8,128)(2,1)S(1)} %collective-permute-done.7), channel_id=1, source_target_pairs={{8,0},{9,1},{10,2},{11,3},{12,4},{13,5},{14,6},{15,7}} | collective-permute-start | bytes 3145736 | tf_op jit(solution)/shard_map/ppermute | solution.py:199
  71.1 45.5 %collective-permute-start.15 = (bf16[2,512,512]{2,1,0:T(8,128)(2,1)S(1)}, bf16[2,512,512]{2,1,0:T(8,128)(2,1)S(1)}, u32[]{:S(2)}, u32[]{:S(2)}) collective-permute-start(bf16[2,512,512]{2,1,0:T(8,128)(2,1)S(1)} %pad_maximum_fusion.6), channel_id=1, source_target_pairs={{0,16},{1,17},{2,18},{3,19},{4,20},{5,21},{6,22},{7,23},{8,24},{9,... | collective-permute-start | bytes 3145736 | tf_op jit(solution)/shard_map/ppermute | solution.py:199
  116.6 40.4 %copy-start.11 = (bf16[192,4096]{1,0:T(8,128)(2,1)}, bf16[192,4096]{1,0:T(8,128)(2,1)S(1)}, u32[]{:S(2)}) copy-start(bf16[192,4096]{1,0:T(8,128)(2,1)S(1)} %collective-permute-done.14.refs_6_) | copy-start | bytes 4718596
  117.3 39.6 %collective-permute-start.16 = (bf16[192,4096]{1,0:T(8,128)(2,1)S(1)}, bf16[192,4096]{1,0:T(8,128)(2,1)S(1)}, u32[]{:S(2)}, u32[]{:S(2)}) collective-permute-start(bf16[192,4096]{1,0:T(8,128)(2,1)S(1)} %get-tuple-element.113), channel_id=1, source_target_pairs={{0,1},{1,0},{2,3},{3,2},{4,5},{5,4},{6,7},{7,6},{8,9},{9,8},{10,11... | collective-permute-start | bytes 4718600 | tf_op jit(solution)/shard_map/ppermute | solution.py:199
  118.8 38.1 %collective-permute-start.17 = (bf16[192,4096]{1,0:T(8,128)(2,1)S(1)}, bf16[192,4096]{1,0:T(8,128)(2,1)S(1)}, u32[]{:S(2)}, u32[]{:S(2)}) collective-permute-start(bf16[192,4096]{1,0:T(8,128)(2,1)S(1)} %get-tuple-element.112), channel_id=1, source_target_pairs={{0,2},{1,3},{2,0},{3,1},{4,6},{5,7},{6,4},{7,5},{8,10},{9,11},{10,... | collective-permute-start | bytes 4718600 | tf_op jit(solution)/shard_map/ppermute | solution.py:199
  119.3 5.3 %collective-permute-start.20 = (bf16[2,512,512]{2,1,0:T(8,128)(2,1)S(1)}, bf16[2,512,512]{2,1,0:T(8,128)(2,1)S(1)}, u32[]{:S(2)}, u32[]{:S(2)}) collective-permute-start(bf16[2,512,512]{2,1,0:T(8,128)(2,1)S(1)} %collective-permute-done.15.refs_10_.refs_6_.refs_15_), channel_id=1, source_target_pairs={{0,4},{1,5},{2,6},{3,7},{4,0},{5,1},{6,2},{7,3},{8,12},{9,13},{10,... | collective-permute-start | bytes 3145736 | tf_op jit(solution)/shard_map/ppermute | solution.py:199
  119.8 37.1 %collective-permute-start.18 = (bf16[2,512,512]{2,1,0:T(8,128)(2,1)S(1)}, bf16[2,512,512]{2,1,0:T(8,128)(2,1)}, u32[]{:S(2)}, u32[]{:S(2)}) collective-permute-start(bf16[2,512,512]{2,1,0:T(8,128)(2,1)S(1)} %pad_maximum_fusion.5), channel_id=1, source_target_pairs={{0,8},{1,9},{2,10},{3,11},{4,12},{5,13},{6,14},{7,15},{8,16},{9,17... | collective-permute-start | bytes 3145736 | tf_op jit(solution)/shard_map/ppermute | solution.py:199
  119.8 37.1 %collective-permute-start.19 = (bf16[2,256,512]{2,1,0:T(8,128)(2,1)S(1)}, bf16[2,256,512]{2,1,0:T(8,128)(2,1)}, u32[]{:S(2)}, u32[]{:S(2)}) collective-permute-start(bf16[2,256,512]{2,1,0:T(8,128)(2,1)S(1)} %pad_maximum_fusion.7), channel_id=1, source_target_pairs={{0,24},{1,25},{2,26},{3,27},{4,28},{5,29},{6,30},{7,31},{8,0},{9,1... | collective-permute-start | bytes 1572872 | tf_op jit(solution)/shard_map/ppermute | solution.py:199
  156.9 10.2 %collective-permute-start.24 = (bf16[2,512,512]{2,1,0:T(8,128)(2,1)}, bf16[2,512,512]{2,1,0:T(8,128)(2,1)}, u32[]{:S(2)}, u32[]{:S(2)}) collective-permute-start(bf16[2,512,512]{2,1,0:T(8,128)(2,1)} %collective-permute-done.18.refs_8_.refs_17_), channel_id=1, source_target_pairs={{0,4},{1,5},{2,6},{3,7},{4,0},{5,1},{6,2},{7,3},{8,12},{9,13},{10,... | collective-permute-start | bytes 3145736 | tf_op jit(solution)/shard_map/ppermute | solution.py:199
  158.5 32.5 %collective-permute-start.21 = (bf16[64,4096]{1,0:T(8,128)(2,1)}, bf16[64,4096]{1,0:T(8,128)(2,1)}, u32[]{:S(2)}, u32[]{:S(2)}) collective-permute-start(bf16[64,4096]{1,0:T(8,128)(2,1)} %slice.154), channel_id=1, source_target_pairs={{0,1},{1,0},{2,3},{3,2},{4,5},{5,4},{6,7},{7,6},{8,9},{9,8},{10,11... | collective-permute-start | bytes 1572872 | tf_op jit(solution)/shard_map/ppermute | solution.py:199
  159.9 31.1 %collective-permute-start.22 = (bf16[64,4096]{1,0:T(8,128)(2,1)}, bf16[64,4096]{1,0:T(8,128)(2,1)}, u32[]{:S(2)}, u32[]{:S(2)}) collective-permute-start(bf16[64,4096]{1,0:T(8,128)(2,1)} %slice.155), channel_id=1, source_target_pairs={{0,2},{1,3},{2,0},{3,1},{4,6},{5,7},{6,4},{7,5},{8,10},{9,11},{10,... | collective-permute-start | bytes 1572872 | tf_op jit(solution)/shard_map/ppermute | solution.py:199
  161.4 29.6 %collective-permute-start.23 = (bf16[2,256,512]{2,1,0:T(8,128)(2,1)}, bf16[2,256,512]{2,1,0:T(8,128)(2,1)}, u32[]{:S(2)}, u32[]{:S(2)}) collective-permute-start(bf16[2,256,512]{2,1,0:T(8,128)(2,1)} %pad_maximum_fusion.8), channel_id=1, source_target_pairs={{0,24},{1,25},{2,26},{3,27},{4,28},{5,29},{6,30},{7,31},{8,0},{9,1... | collective-permute-start | bytes 1572872 | tf_op jit(solution)/shard_map/ppermute | solution.py:199
  163.3 3.8 %collective-permute-start.25 = (bf16[2,256,512]{2,1,0:T(8,128)(2,1)}, bf16[2,256,512]{2,1,0:T(8,128)(2,1)}, u32[]{:S(2)}, u32[]{:S(2)}) collective-permute-start(bf16[2,256,512]{2,1,0:T(8,128)(2,1)} %collective-permute-done.19.refs_10_.refs_19_), channel_id=1, source_target_pairs={{0,4},{1,5},{2,6},{3,7},{4,0},{5,1},{6,2},{7,3},{8,12},{9,13},{10,... | collective-permute-start | bytes 1572872 | tf_op jit(solution)/shard_map/ppermute | solution.py:199
  167.0 13.1 %copy-start.10 = (bf16[192,4096]{1,0:T(8,128)(2,1)S(1)}, bf16[192,4096]{1,0:T(8,128)(2,1)}, u32[]{:S(2)}) copy-start(bf16[192,4096]{1,0:T(8,128)(2,1)} %copy-done.9) | copy-start | bytes 4718596
  180.1 15.3 %copy-start.47 = (f32[128,2]{0,1:T(2,128)S(1)}, f32[128,2]{0,1:T(2,128)}, u32[]{:S(2)}) copy-start(f32[128,2]{0,1:T(2,128)} %convolution_bitcast_fusion.3) | copy-start | bytes 3076
  180.1 15.3 %copy-start.48 = (f32[128,2]{0,1:T(2,128)S(1)}, f32[128,2]{0,1:T(2,128)}, u32[]{:S(2)}) copy-start(f32[128,2]{0,1:T(2,128)} %convolution_bitcast_fusion.2) | copy-start | bytes 3076
  180.2 15.3 %copy-start.49 = (f32[128,2]{0,1:T(2,128)S(1)}, f32[128,2]{0,1:T(2,128)}, u32[]{:S(2)}) copy-start(f32[128,2]{0,1:T(2,128)} %convolution_bitcast_fusion.1) | copy-start | bytes 3076
  191.0 6.0 %collective-permute-start.26 = (bf16[2,256,512]{2,1,0:T(8,128)(2,1)}, bf16[2,256,512]{2,1,0:T(8,128)(2,1)}, u32[]{:S(2)}, u32[]{:S(2)}) collective-permute-start(bf16[2,256,512]{2,1,0:T(8,128)(2,1)} %collective-permute-done.23.refs_21_), channel_id=1, source_target_pairs={{0,4},{1,5},{2,6},{3,7},{4,0},{5,1},{6,2},{7,3},{8,12},{9,13},{10,... | collective-permute-start | bytes 1572872 | tf_op jit(solution)/shard_map/ppermute | solution.py:199
  201.9 13.3 %copy-start.50 = (s32[16]{0:T(128)S(1)}, s32[16]{0:T(128)}, u32[]{:S(2)}) copy-start(s32[16]{0:T(128)} %pad_add_fusion.2) | copy-start | bytes 196
  215.3 3.6 %collective-permute-start.28 = (f32[1,32]{1,0:T(1,128)S(1)}, f32[1,32]{1,0:T(1,128)S(1)}, u32[]{:S(2)}, u32[]{:S(2)}) collective-permute-start(f32[1,32]{1,0:T(1,128)S(1)} %bitcast.242), channel_id=1, source_target_pairs={{0,2},{1,3},{2,0},{3,1},{4,6},{5,7},{6,4},{7,5},{8,10},{9,11},{10,... | collective-permute-start | bytes 392 | tf_op jit(solution)/shard_map/ppermute | solution.py:199
  215.9 4.4 %collective-permute-start.29 = (f32[1,32]{1,0:T(1,128)S(1)}, f32[1,32]{1,0:T(1,128)S(1)}, u32[]{:S(2)}, u32[]{:S(2)}) collective-permute-start(f32[1,32]{1,0:T(1,128)S(1)} %bitcast.243), channel_id=1, source_target_pairs={{0,3},{1,2},{2,1},{3,0},{4,7},{5,6},{6,5},{7,4},{8,11},{9,10},{10,... | collective-permute-start | bytes 392 | tf_op jit(solution)/shard_map/ppermute | solution.py:199
  218.3 3.5 %collective-permute-start.27 = (f32[1,32]{1,0:T(1,128)S(1)}, f32[1,32]{1,0:T(1,128)S(1)}, u32[]{:S(2)}, u32[]{:S(2)}) collective-permute-start(f32[1,32]{1,0:T(1,128)S(1)} %bitcast.244), channel_id=1, source_target_pairs={{0,1},{1,0},{2,3},{3,2},{4,5},{5,4},{6,7},{7,6},{8,9},{9,8},{10,11... | collective-permute-start | bytes 392 | tf_op jit(solution)/shard_map/ppermute | solution.py:199
  221.8 5.3 %collective-permute-start.31 = (f32[1,32]{1,0:T(1,128)S(1)}, f32[1,32]{1,0:T(1,128)S(1)}, u32[]{:S(2)}, u32[]{:S(2)}) collective-permute-start(f32[1,32]{1,0:T(1,128)S(1)} %add_add_fusion.1), channel_id=1, source_target_pairs={{0,8},{1,9},{2,10},{3,11},{4,12},{5,13},{6,14},{7,15},{8,16},{9,17... | collective-permute-start | bytes 392 | tf_op jit(solution)/shard_map/ppermute | solution.py:199
  222.0 5.2 %collective-permute-start.32 = (f32[1,32]{1,0:T(1,128)S(1)}, f32[1,32]{1,0:T(1,128)S(1)}, u32[]{:S(2)}, u32[]{:S(2)}) collective-permute-start(f32[1,32]{1,0:T(1,128)S(1)} %add_add_fusion.1), channel_id=1, source_target_pairs={{0,24},{1,25},{2,26},{3,27},{4,28},{5,29},{6,30},{7,31},{8,0},{9,1... | collective-permute-start | bytes 392 | tf_op jit(solution)/shard_map/ppermute | solution.py:199
  225.7 4.4 %collective-permute-start.30 = (f32[1,32]{1,0:T(1,128)S(1)}, f32[1,32]{1,0:T(1,128)S(1)}, u32[]{:S(2)}, u32[]{:S(2)}) collective-permute-start(f32[1,32]{1,0:T(1,128)S(1)} %add_add_fusion.1), channel_id=1, source_target_pairs={{0,16},{1,17},{2,18},{3,19},{4,20},{5,21},{6,22},{7,23},{8,24},{9,... | collective-permute-start | bytes 392 | tf_op jit(solution)/shard_map/ppermute | solution.py:199
  230.1 1.1 collective-permute-start.33
  (38 other events, 210.1 us)

commit v3 on v2

--- a/solution.py
+++ b/solution.py
@@ -1,3 +1,5 @@
+import math
+
 import jax
 import jax.numpy as jnp
 from jax import lax
@@ -9,6 +11,7 @@
 learn_rate = 0.0016
 AXES = ("pop", "mp")
 CORES = 2
+SPARE_BYTES = 4 * 1024 * 1024
 
 
 def shift_down(number, amount):
@@ -88,47 +91,113 @@
     return new_gate, new_up, own
 
 
-def product_kernel(plan, counts, finish, starts_ref, *refs):
+def product_kernel(plan, counts, plane_of, seq, ranked, vectored, read_out, starts_ref, *refs):
     refs = list(refs)
     x_refs, w_refs, base_refs = [[refs.pop(0) for _ in range(count)] for count in counts]
-    if finish:
-        proj_ref, col_ref, head_ref = [refs.pop(0) for _ in range(3)]
+    if ranked:
+        proj_ref, col_ref = refs.pop(0), refs.pop(0)
+    if vectored:
+        vector_ref, vector_col_ref = refs.pop(0), refs.pop(0)
+    if read_out:
+        head_ref = refs.pop(0)
         head = head_ref[...].astype(jnp.float32)
-    out_ref = refs.pop(0)
-    columns = w_refs[0].shape[2]
-    for i, (segments, first_chunk, base) in enumerate(plan):
-        values = [None, None]
-        for k in range(first_chunk, len(w_refs)):
-            depth = w_refs[k].shape[1]
-            at = pl.ds(pl.multiple_of(starts_ref[k], depth), depth)
-            rows = [x_refs[x][pl.ds(first, count), at] for x, first, count in segments]
-            rows = rows[0] if len(rows) == 1 else jnp.concatenate(rows)
+    out_ref, weights = refs.pop(0), refs.pop(0)
+    rows, totals = [], []
+    for _, _, base, _ in plan:
+        rows.append(refs.pop(0))
+        totals.append(refs.pop(0) if base is not None or not read_out else None)
+    row_sems, weight_sems, total_sems = refs
+    columns = weights.shape[2]
+    n_planes = 1 + plane_of[-1]
+    plane_rows = weights.shape[1] // n_planes
+    weight_copies = []
+    for k, w_ref in enumerate(w_refs):
+        depth = w_ref.shape[1]
+        at = plane_of[k] * plane_rows + pl.multiple_of(starts_ref[len(w_refs) + k], depth)
+        weight_copies.append(pltpu.make_async_copy(w_ref, weights.at[:, pl.ds(at, depth)], weight_sems.at[k]))
+    group_copies = []
+    for g, (segments, first, base, _) in enumerate(plan):
+        copies = []
+        row = 0
+        for i, (x, start_row, count) in enumerate(segments):
+            for plane in range(first, n_planes):
+                start = pl.multiple_of(starts_ref[plane_of.index(plane)], plane_rows)
+                copies.append(
+                    pltpu.make_async_copy(
+                        x_refs[x].at[pl.ds(start_row, count), pl.ds(start, plane_rows)],
+                        rows[g].at[pl.ds(row, count), pl.ds((plane - first) * plane_rows, plane_rows)],
+                        row_sems.at[g, i, plane],
+                    )
+                )
+            row += count
+        if base is not None:
+            source = base_refs[base[0]].at[pl.ds(base[1], row)]
+            copies.append(pltpu.make_async_copy(source, totals[g], total_sems.at[g]))
+        group_copies.append(copies)
+    started = set()
+    for g, (_, first, _, _) in enumerate(plan):
+        for k, copy in enumerate(weight_copies):
+            if plane_of[k] >= first and k not in started:
+                started.add(k)
+                copy.start()
+        for copy in group_copies[g]:
+            copy.start()
+    done_rows, out_copies = 0, []
+    for g, (_, first, base, own_vectors) in enumerate(plan):
+        for k in sorted(started):
+            if plane_of[k] >= first:
+                started.remove(k)
+                weight_copies[k].wait()
+        for copy in group_copies[g]:
+            copy.wait()
+        count = rows[g].shape[0]
+        values = [
+            jnp.dot(rows[g][...], weights[part, first * plane_rows :], preferred_element_type=jnp.float32)
+            for part in range(2)
+        ]
+        for i in range(count // seq):
+            here = slice(i * seq, (i + 1) * seq)
+            there = slice(done_rows + i * seq, done_rows + (i + 1) * seq)
+            member = done_rows // seq + i
+            found = []
+            vector = None
+            for plane in range(first, n_planes if own_vectors is not None else first):
+                start = pl.multiple_of(starts_ref[plane_of.index(plane)], plane_rows)
+                term = lax.dot_general(
+                    rows[g][here, (plane - first) * plane_rows : (plane + 1 - first) * plane_rows],
+                    vector_ref[own_vectors + i, :, pl.ds(start, plane_rows)],
+                    (((1,), (1,)), ((), ())),
+                    preferred_element_type=jnp.float32,
+                )
+                vector = term if vector is None else vector + term
             for part in range(2):
-                term = jnp.dot(rows, w_refs[k][part], preferred_element_type=jnp.float32)
-                values[part] = term if values[part] is None else values[part] + term
-        seq = values[0].shape[0]
-        for part in range(2):
-            if base is not None:
-                at = pl.ds(base[1], seq)
-                values[part] += base_refs[base[0]][at, part * columns : (part + 1) * columns]
-            if not finish:
-                out_ref[i * seq : (i + 1) * seq, part * columns : (part + 1) * columns] = values[part]
-        if finish:
-            gate, up = [
-                values[part]
-                + sigma_perturb
-                * proj_ref[i * seq : (i + 1) * seq, part : part + 1]
-                * col_ref[part, i : i + 1, :]
-                for part in range(2)
-            ]
-            hidden = (gate / (1.0 + jnp.exp(-gate)) * up).astype(jnp.bfloat16)
-            terms = hidden.astype(jnp.float32) * head
-            out_ref[i] = jnp.sum(terms.reshape(seq // 8, 8, columns), axis=0)
-
-
-def product(members, chunks, finish=None):
-    depths = [chunk.shape[1] for _, chunk in chunks]
-    columns = chunks[0][1].shape[2]
+                at = slice(part * columns, (part + 1) * columns)
+                value = values[part][here]
+                if base is not None:
+                    value += totals[g][here, at].astype(jnp.float32)
+                if ranked and own_vectors is None:
+                    value += sigma_perturb * proj_ref[there, part : part + 1] * col_ref[part, member : member + 1, :]
+                if vector is not None:
+                    value += sigma_perturb * vector[:, part : part + 1] * vector_col_ref[part, own_vectors + i]
+                if not read_out:
+                    totals[g][here, at] = value.astype(jnp.bfloat16)
+                found.append(value)
+            if read_out:
+                gate, up = found
+                hidden = (0.5 * gate * (1.0 + jnp.tanh(0.5 * gate)) * up).astype(jnp.bfloat16)
+                terms = hidden.astype(jnp.float32) * head
+                out_ref[member] = jnp.sum(terms.reshape(seq // 8, 8, columns), axis=0)
+        if not read_out:
+            target = out_ref.at[pl.ds(done_rows, count)]
+            out_copies.append(pltpu.make_async_copy(totals[g], target, total_sems.at[g]))
+            out_copies[-1].start()
+        done_rows += count
+    for copy in out_copies:
+        copy.wait()
+
+
+def product(groups, seq, chunks, ranks=(), vectors=(), read_out=()):
+    columns = chunks[0][3].shape[2]
     arrays, base_arrays, plan = [], [], []
 
     def number(array, known):
@@ -138,34 +207,45 @@
         known.append(array)
         return len(known) - 1
 
-    for segments, first_chunk, base in members:
-        placed = [(number(a, arrays), first, rows) for a, first, rows in segments]
-        plan.append((placed, first_chunk, base and (number(base[0], base_arrays), base[1])))
-    seq = sum(rows for _, _, rows in members[0][0])
-    total = seq * len(members)
-    work = sum(seq * sum(depths[first:]) for _, first, _ in members)
+    for segments, first, base, own_vectors in groups:
+        placed = [(number(a, arrays), row, rows) for a, row, rows in segments]
+        plan.append((placed, first, base and (number(base[0], base_arrays), base[1]), own_vectors))
+    sizes = [sum(rows for _, _, rows in segments) for segments, _, _, _ in groups]
+    total = sum(sizes)
+    keys = list(dict.fromkeys(key for key, _, _, _ in chunks))
+    plane_of = [keys.index(key) for key, _, _, _ in chunks]
+    plane_rows = sum(chunk.shape[1] for key, _, _, chunk in chunks if key == keys[0])
+    counts = [len(arrays), len(chunks), len(base_arrays)]
+    buffers = [pltpu.VMEM((2, len(keys) * plane_rows, columns), jnp.bfloat16)]
+    for (_, first, base, _), size in zip(groups, sizes):
+        buffers.append(pltpu.VMEM((size, (len(keys) - first) * plane_rows), jnp.bfloat16))
+        if base is not None or not read_out:
+            buffers.append(pltpu.VMEM((size, 2 * columns), jnp.bfloat16))
+    given = [*arrays, *[chunk for _, _, _, chunk in chunks], *base_arrays]
+    given = [pltpu.with_memory_space_constraint(a, pltpu.HBM) for a in given]
+    extra = [*ranks, *vectors, *read_out]
+    held = sum(2 * math.prod(b.shape) for b in buffers) + 4 * total * columns
+    held += sum(4 * 128 * a.size // min(128, a.shape[-1]) for a in extra)
     vmem = pl.BlockSpec(memory_space=pltpu.VMEM)
-    operands = [
-        *arrays,
-        *[chunk for _, chunk in chunks],
-        *base_arrays,
-        *(finish or ()),
-    ]
-    shape = (len(members), 8, columns) if finish else (total, 2 * columns)
-    held = sum(a.size * a.dtype.itemsize for a in operands) + 4 * total * 2 * columns
-    counts = [len(arrays), len(chunks), len(base_arrays)]
+    outside = pl.BlockSpec(memory_space=pl.ANY)
+    shape = pltpu.HBM((total, 2 * columns), jnp.bfloat16)
+    if read_out:
+        shape = jax.ShapeDtypeStruct((total // seq, 8, columns), jnp.float32)
+    parts = max(len(segments) for segments, _, _, _ in groups)
     return pl.pallas_call(
-        lambda *refs: product_kernel(plan, counts, finish, *refs),
-        out_shape=jax.ShapeDtypeStruct(shape, jnp.float32),
-        in_specs=[pl.BlockSpec(memory_space=pltpu.SMEM)] + [vmem] * len(operands),
-        out_specs=vmem,
-        compiler_params=pltpu.CompilerParams(vmem_limit_bytes=held + 4 * 1024 * 1024),
-        cost_estimate=pl.CostEstimate(
-            flops=4 * work * columns,
-            bytes_accessed=2 * work + 16 * total * columns + 4 * sum(depths) * columns,
-            transcendentals=total * columns if finish else 0,
-        ),
-    )(jnp.stack([start for start, _ in chunks]), *operands)
+        lambda *refs: product_kernel(plan, counts, plane_of, seq, bool(ranks), bool(vectors), bool(read_out), *refs),
+        out_shape=shape,
+        in_specs=[pl.BlockSpec(memory_space=pltpu.SMEM)] + [outside] * len(given) + [vmem] * len(extra),
+        out_specs=vmem if read_out else outside,
+        scratch_shapes=[
+            *buffers,
+            pltpu.SemaphoreType.DMA((len(groups), parts, len(keys))),
+            pltpu.SemaphoreType.DMA((len(chunks),)),
+            pltpu.SemaphoreType.DMA((len(groups),)),
+        ],
+        compiler_params=pltpu.CompilerParams(vmem_limit_bytes=held + SPARE_BYTES),
+        cost_estimate=pl.CostEstimate(flops=1, bytes_accessed=1, transcendentals=0),
+    )(jnp.stack([c[1] for c in chunks] + [c[2] for c in chunks]), *given, *extra)
 
 
 def tree_sum(terms):
@@ -276,26 +356,38 @@
         picked.append((chosen[0], chosen[1]))
         group_ids.append((source * CORES + core) * members_here + rel)
 
-    def perturbed(r):
+    def new_vectors(r):
         seeds, counts = picked[r]
-        vectors = jnp.stack(
+        return jnp.stack(
             [factor_rows(seeds, counts + 1, slot, positions).astype(jnp.bfloat16) for slot in (0, 2)],
             axis=1,
         )
-        found = [
-            lax.dot_general(
-                array[first : first + rows],
-                vectors[i],
-                (((1,), (1,)), ((), ())),
-                preferred_element_type=jnp.float32,
-            )
-            for i in range(members_here)
-            for array, first, rows in members[r * members_here + i]
-        ]
-        columns = [factor_rows(seeds, counts + 1, slot + 1, my_columns) for slot in (0, 2)]
-        return jnp.concatenate(found), jnp.stack(columns)
-
-    projs, cols = map(lambda v: [v], perturbed(0))
+
+    def projected(r, vectors, some):
+        found = []
+        for i in some:
+            parts = [
+                lax.dot_general(
+                    array[first : first + rows],
+                    vectors[i],
+                    (((1,), (1,)), ((), ())),
+                    preferred_element_type=jnp.float32,
+                )
+                for array, first, rows in members[r * members_here + i]
+            ]
+            found.append(parts[0] if len(parts) == 1 else jnp.concatenate(parts))
+        return found
+
+    cols = [
+        jnp.stack([factor_rows(seeds, counts + 1, slot + 1, my_columns) for slot in (0, 2)])
+        for seeds, counts in picked
+    ]
+    cols = jnp.concatenate(cols, axis=1)
+    vectors = [new_vectors(r) for r in range(planes)]
+    late_vectors = jnp.concatenate([vectors[planes - 2][members_here - 1 :], vectors[planes - 1]])
+    late_vectors = jnp.pad(late_vectors, ((0, 0), (0, 14), (0, 0)))
+    late = (late_vectors, cols[:, (planes - 1) * members_here - 1 :, None])
+    projs = projected(0, vectors[0], range(members_here))
 
     column_ids = mp_index * own_cols + jnp.arange(own_cols, dtype=jnp.int32)
     weights = fresh_weights(
@@ -313,67 +405,89 @@
 
     def add_chunks(key):
         s, first, _ = key
-        plane = (z - s) % planes * CORES
+        start = (z - s) % planes * CORES * own_rows
         return [
-            ((plane + core) * own_rows + first, landed[key]),
-            ((plane + 1 - core) * own_rows + first, swap_core(landed[key])),
+            (s, start, core * own_rows + first, landed[key]),
+            (s, start, (1 - core) * own_rows + first, swap_core(landed[key])),
         ]
 
     half = seq // 2
     fresh = [(0, 0, own_rows)]
-    across_x = across_y = corner_x = corner_y = None
-    bases, held_back, early = [], 0, 0
-
-    def on(some, first_chunk, base=None):
-        return [
-            (m, first_chunk, base if base is None else (base, i * seq)) for i, m in enumerate(some)
-        ]
-
-    hops[0][1], hops[1][1] = tie(hops[0][1], hops[1][1])
+    base, early, early_planes = None, 0, 0
+
+    def on(some, first, base=None, vectors=None):
+        groups = []
+        for i in range(0, len(some), members_here):
+            segments = []
+            for segment in [s for m in some[i : i + members_here] for s in m]:
+                array, row, rows = segments[-1] if segments else (None, 0, 0)
+                if array is segment[0] and row + rows == segment[1]:
+                    segments[-1] = (array, row, rows + segment[2])
+                else:
+                    segments.append(segment)
+            groups.append((segments, first, None if base is None else (base, i * seq), vectors if vectors is None else vectors + i))
+        return groups
+
+    next_here = round_block(1)
+    to_x, to_y, hops[0][1], hops[1][1] = tie(next_here, next_here, hops[0][1], hops[1][1])
+    next_here = to_x
     for phase in range(1, planes + 1):
         if phase < planes - 1:
             hops[0].append(up(hops[0][phase], phase + 1))
             hops[1].append(down(hops[1][phase], phase + 1))
-        to_x, to_y = [], []
         if phase < planes:
-            here = round_block(phase)
-            to_x.append(here)
-            to_y.append(here)
-        if phase > 1:
-            to_x.append(across_y[:half])
-            to_y.append(across_x[half:seq])
-        new_x = swap_in_plane(jnp.concatenate(to_x), 1)
-        new_y = swap_in_plane(jnp.concatenate(to_y), 2)
+            here = next_here
+        new_x = swap_in_plane(to_x, 1)
+        new_y = swap_in_plane(to_y, 2)
         for key in leave.get(phase, ()):
             landed[key] = turn(outgoing[key], key[0])
         new_chunks = [c for key in fresh for c in add_chunks(key)]
         fresh = leave.get(phase, ())
         known = chunks + new_chunks
         if phase == planes - 1:
-            early = len(members)
-            bases = [product(on(members, 0), known)]
-            held_back = len(known)
+            early, early_planes = len(members), len(set(c[0] for c in known))
+            ranks = (jnp.concatenate(projs), cols[:, :early])
+            base = product(on(members, 0), seq, known, ranks)
         elif phase == planes:
-            bases.append(product(on(members[:early], 0, bases[0]), known[held_back:]))
-            bases.append(product(on(members[early:], 0), known))
-        parts = (hops, new_x, new_y, landed, new_chunks, outgoing, bases)
-        hops, new_x, new_y, landed, new_chunks, outgoing, bases = tie(*parts)
-        chunks += new_chunks
+            landed_first = [c for c in chunks + new_chunks if c[0] != far_first[-1]]
+            groups = on(members[:early], early_planes, base) + on(members[early:], 0, None, 0)
+            base = product(groups, seq, landed_first, (), late)
+        def next_sends():
+            to_x, to_y, here = [new_y[:half]], [new_x[half:seq]], None
+            if phase + 1 < planes:
+                here = round_block(phase + 1)
+                to_x, to_y = [here, *to_x], [here, *to_y]
+            return jnp.concatenate(to_x), jnp.concatenate(to_y), here
+
+        ahead = ()
+        if phase in leave and phase < planes:
+            hops, new_x, new_y = tie(hops, new_x, new_y)
+            ahead = next_sends()
+        held = [chunk for _, _, _, chunk in new_chunks]
+        parts = (hops, new_x, new_y, ahead, landed, held, outgoing, base, cols, late, projs, head)
+        hops, new_x, new_y, ahead, landed, held, outgoing, base, cols, late, projs, head = tie(*parts)
+        if phase < planes:
+            to_x, to_y, next_here = ahead or next_sends()
+        chunks += [(*c[:3], chunk) for c, chunk in zip(new_chunks, held)]
         if phase > 1:
             first = seq if phase < planes else 0
             members.append([(new_x, first, half), (new_y, first, half)])
-            proj, col = perturbed(phase - 1)
-            projs.append(proj)
-            cols.append(col)
+        if 1 < phase < planes - 1:
+            projs += projected(phase - 1, vectors[phase - 1], [members_here - 1])
         if phase < planes:
             members += [[(here, 0, seq)], [(new_x, 0, seq)], [(new_y, 0, seq)]]
-        across_x, across_y = new_x, new_y
+        if phase < planes - 1:
+            projs += projected(phase, vectors[phase], range(members_here - 1))
 
     last = [c for key in fresh for c in add_chunks(key)]
-    plan = on(members[:early], len(chunks), bases[1])
-    plan += on(members[early:-1], len(chunks), bases[2]) + on(members[-1:], 0)
-    finish = (jnp.concatenate(projs), jnp.concatenate(cols, axis=1), head)
-    sums = product(plan, chunks + last, finish).reshape(len(members), -1).sum(axis=1)
+    plan = on(members[:early], planes - 1, base)
+    plan += [
+        (segments, first, (base, early * seq + row), here)
+        for segments, first, (_, row), here in on(members[early:-1], planes - 1, base, 0)
+    ]
+    plan += on(members[-1:], 0, None, len(members) - 1 - early)
+    sums = product(plan, seq, chunks + last, (), late, (head,))
+    sums = sums.reshape(len(members), -1).sum(axis=1)
 
     ids = jnp.concatenate(group_ids)
     total = planes * CORES * members_here

time: 235 us -> 218 us (0.928)
  waiting for transfers between devices: 97 us -> 78.3 us
  local copies, waits for them, and re-layouts: 24.9 us -> 15.2 us
  other arithmetic: 10.7 us -> 16.6 us
  Pallas kernels: 33.9 us -> 39 us
  starting transfers between devices: 43.8 us -> 46.5 us
  matrix products: 21 us -> 18.4 us
    ppermute x34, waiting for transfers between devices: 97 us -> 78.3 us  [send(): return lax.ppermute(value, AXES, pairs(move, keep))]
    unnamed x104 -> x40, local copies, waits for them, and re-layouts: 17.2 us -> 3.22 us
    pallas_call x4 -> x3, Pallas kernels: 33.9 us -> 39 us  [product(): pl.pallas_call(lambda *refs: product_kernel(plan, counts, plane_of, seq,...]
    slice x6 -> x7, local copies, waits for them, and re-layouts: 1.83 us -> 6 us  [the longest x6 5.98 us: next_sends(): to_x, to_y, here = ([new_y[:half]], [new_x[half:seq]], None)]
    concatenate x3 -> x5, other arithmetic: 0.76 us -> 4.28 us  [the longest x2 4.03 us: next_sends(): return (jnp.concatenate(to_x), jnp.concatenate(to_y), here)]
    another operation x5, other arithmetic: 1.2 us -> 4.08 us  [piece(): jnp.stack([lax.dynamic_slice(w, corner, (count, block)) for w in weights])]
    ppermute x34, starting transfers between devices: 43.8 us -> 46.5 us  [send(): return lax.ppermute(value, AXES, pairs(move, keep))]
    dot_general x19 -> x12, matrix products: 17.6 us -> 15 us  [projected(): lax.dot_general(array[first:first + rows], vectors[i], (((1,), (1,)), (()...]
  transfers between devices with their start and end apart: 34 -> 34, of which waited for: 13 -> 17; matrix products, arithmetic and copies ran while one was open for 15% -> 19% of each run, Pallas kernels for 9% -> 12%
where the time goes in v3:
time: 218 us; the launch traced here: 217 us
  waiting for transfers between devices  78.3 us (36%)
  starting transfers between devices  46.5 us (21%)
  Pallas kernels  39 us (18%)
  matrix products  18.4 us (8%)
  other arithmetic  16.6 us (8%)
  local copies, waits for them, and re-layouts  15.2 us (7%)
  between operations  2.84 us (1%)
    ppermute x34, waiting for transfers between devices, send(): return lax.ppermute(value, AXES, pairs(move, keep))  78.3 us
    ppermute x34, starting transfers between devices, send(): return lax.ppermute(value, AXES, pairs(move, keep))  46.5 us
    pallas_call x3, Pallas kernels, product(): pl.pallas_call(lambda *refs: product_kernel(plan, counts, plane_of, seq,...  39 us
    dot_general x12, matrix products, projected(): lax.dot_general(array[first:first + rows], vectors[i], (((1,), (1,)), (()...  15 us
    slice x6, local copies, waits for them, and re-layouts, next_sends(): to_x, to_y, here = ([new_y[:half]], [new_x[half:seq]], None)  5.98 us
  transfers between devices with their start and end apart: 34, of which 17 were waited for; matrix products, arithmetic and copies ran while one was open for 19% of the time, Pallas kernels for 12%

profile of v3, /device:TPU:0, one launch (start us, length us, event | category | flops | bytes accessed | tf_op | source)
XLA Modules:
  0.0 216.9 jit_solution(405463015050425055)
XLA Ops:
  1.4 3.0 %collective-permute-start = (s32[3,4]{1,0:T(4,128)S(1)}, s32[3,4]{1,0:T(4,128)S(1)}, u32[]{:S(2)}, u32[]{:S(2)}) collective-permute-start(s32[3,4]{1,0:T(4,128)S(1)} %get-tuple-element.203), channel_id=1, source_target_pairs={{0,8},{1,9},{2,10},{3,11},{4,12},{5,13},{6,14},{7,15},{8,16},{9,17... | collective-permute-start | bytes 152 | tf_op jit(solution)/shard_map/ppermute | solution.py:279
  4.4 2.6 %collective-permute-start.1 = (s32[3,4]{1,0:T(4,128)S(1)}, s32[3,4]{1,0:T(4,128)S(1)}, u32[]{:S(2)}, u32[]{:S(2)}) collective-permute-start(s32[3,4]{1,0:T(4,128)S(1)} %get-tuple-element.203), channel_id=1, source_target_pairs={{0,16},{1,17},{2,18},{3,19},{4,20},{5,21},{6,22},{7,23},{8,24},{9,... | collective-permute-start | bytes 152 | tf_op jit(solution)/shard_map/ppermute | solution.py:279
  7.0 1.3 collective-permute-start.2
  8.4 2.3 %dynamic-slice_bitcast_fusion = bf16[128,4096]{1,0:T(8,128)(2,1)} fusion(bf16[4,128,4096]{2,1,0:T(8,128)(2,1)} %param.7, s32[]{:T(128)S(6)} %select_n.221), kind=kLoop, calls=%fused_computation.31 | loop fusion | bytes 2097156 | tf_op jit(solution)/shard_map/jit(dynamic_index_in_dim)/squeeze | solution.py:333
  10.7 3.6 %collective-permute-start.4 = (bf16[128,4096]{1,0:T(8,128)(2,1)}, bf16[128,4096]{1,0:T(8,128)(2,1)}, u32[]{:S(2)}, u32[]{:S(2)}) collective-permute-start(bf16[128,4096]{1,0:T(8,128)(2,1)} %dynamic-slice_bitcast_fusion), channel_id=1, source_target_pairs={{0,8},{1,9},{2,10},{3,11},{4,12},{5,13},{6,14},{7,15},{8,16},{9,17... | collective-permute-start | bytes 3145736 | tf_op jit(solution)/shard_map/ppermute | solution.py:279
  14.2 1.3 collective-permute-start.5
  17.1 2.1 fusion.130
  19.2 1.6 convolution_bitcast_fusion
  20.8 1.6 convolution_bitcast_fusion.1
  22.5 1.6 convolution_bitcast_fusion.2
  24.1 1.6 convolution_bitcast_fusion.3
  27.8 2.6 %add_convert_fusion = bf16[512,2048]{1,0:T(8,128)(2,1)S(1)} fusion(bf16[512,2048]{1,0:T(8,128)(2,1)} %param.9, s32[32]{0:T(128)S(1)} %get-tuple-element.210, s32[2048]{0:T(1024)S(1)} %add_multiply_fusion, s32[32]{0:T(128)S(1)} %get-tuple-element.209, f32[32]{0:T(128)S(1)} %reshape.1830, s32[512]{0:T(512)S(1)} %add_multiply_fusion.2), kind=kOutput, calls=%fused_computation | convolution fusion | flops 72531968 | bytes 4204928 | tf_op jit(solution)/shard_map/dot_general | solution.py:47
  32.0 3.1 %collective-permute-done.4 = bf16[128,4096]{1,0:T(8,128)(2,1)} collective-permute-done((bf16[128,4096]{1,0:T(8,128)(2,1)}, bf16[128,4096]{1,0:T(8,128)(2,1)}, u32[]{:S(2)}, u32[]{:S(2)}) %collective-permute-start.4) | collective-permute-done | bytes 1048608 | tf_op jit(solution)/shard_map/ppermute | solution.py:279
  35.1 5.0 %collective-permute-done.5 = bf16[128,4096]{1,0:T(8,128)(2,1)S(1)} collective-permute-done((bf16[128,4096]{1,0:T(8,128)(2,1)}, bf16[128,4096]{1,0:T(8,128)(2,1)S(1)}, u32[]{:S(2)}, u32[]{:S(2)}) %collective-permute-start.5) | collective-permute-done | bytes 1048608 | tf_op jit(solution)/shard_map/ppermute | solution.py:279
  40.2 1.6 collective-permute-start.6
  43.2 1.6 collective-permute-start.8
  44.7 1.5 collective-permute-start.9
  50.6 17.0 %collective-permute-done.7 = bf16[128,4096]{1,0:T(8,128)(2,1)} collective-permute-done((bf16[128,4096]{1,0:T(8,128)(2,1)S(1)}, bf16[128,4096]{1,0:T(8,128)(2,1)}, u32[]{:S(2)}, u32[]{:S(2)}) %collective-permute-start.7) | collective-permute-done | bytes 1048608 | tf_op jit(solution)/shard_map/ppermute | solution.py:279
  69.0 1.5 select_select_fusion.1.refs_7_
  70.5 2.0 pad_maximum_fusion
  72.5 1.5 collective-permute-start.13
  74.0 1.5 collective-permute-start.14
  75.5 1.6 collective-permute-start.11
  79.0 3.6 %collective-permute-start.15 = (bf16[2,512,512]{2,1,0:T(8,128)(2,1)}, bf16[2,512,512]{2,1,0:T(8,128)(2,1)}, u32[]{:S(2)}, u32[]{:S(2)}) collective-permute-start(bf16[2,512,512]{2,1,0:T(8,128)(2,1)} %pad_maximum_fusion.6), channel_id=1, source_target_pairs={{0,16},{1,17},{2,18},{3,19},{4,20},{5,21},{6,22},{7,23},{8,24},{9,... | collective-permute-start | bytes 3145736 | tf_op jit(solution)/shard_map/ppermute | solution.py:279
  82.6 1.6 fusion.171
  84.5 18.8 %collective-permute-done.12 = bf16[128,4096]{1,0:T(8,128)(2,1)} collective-permute-done((bf16[128,4096]{1,0:T(8,128)(2,1)}, bf16[128,4096]{1,0:T(8,128)(2,1)}, u32[]{:S(2)}, u32[]{:S(2)}) %collective-permute-start.12) | collective-permute-done | bytes 1048608 | tf_op jit(solution)/shard_map/ppermute | solution.py:279
  103.3 2.8 %collective-permute-done.13.refs_5_ = bf16[192,4096]{1,0:T(8,128)(2,1)} collective-permute-done((bf16[192,4096]{1,0:T(8,128)(2,1)}, bf16[192,4096]{1,0:T(8,128)(2,1)}, u32[]{:S(2)}, u32[]{:S(2)}) %collective-permute-start.13) | collective-permute-done | bytes 1572896 | tf_op jit(solution)/shard_map/ppermute | solution.py:279
  109.5 1.4 select_select_fusion.refs_10_
  110.9 2.0 pad_maximum_fusion.2
  113.0 11.6 %collective-permute-done.15.refs_10_.refs_13_.refs_15_ = bf16[2,512,512]{2,1,0:T(8,128)(2,1)} collective-permute-done((bf16[2,512,512]{2,1,0:T(8,128)(2,1)}, bf16[2,512,512]{2,1,0:T(8,128)(2,1)}, u32[]{:S(2)}, u32[]{:S(2)}) %collective-permute-start.15) | collective-permute-done | bytes 1048608 | tf_op jit(solution)/shard_map/ppermute | solution.py:279
  126.8 3.9 %collective-permute-start.19 = (bf16[2,256,512]{2,1,0:T(8,128)(2,1)}, bf16[2,256,512]{2,1,0:T(8,128)(2,1)S(1)}, u32[]{:S(2)}, u32[]{:S(2)}) collective-permute-start(bf16[2,256,512]{2,1,0:T(8,128)(2,1)} %pad_maximum_fusion.7), channel_id=1, source_target_pairs={{0,24},{1,25},{2,26},{3,27},{4,28},{5,29},{6,30},{7,31},{8,0},{9,1... | collective-permute-start | bytes 1572872 | tf_op jit(solution)/shard_map/ppermute | solution.py:279
  132.0 1.3 fusion.19
  133.3 1.6 fusion.7
  134.9 1.6 fusion.9
  136.9 12.0 %shard_map.94.refs_17_ = bf16[1408,1024]{1,0:T(8,128)(2,1)} custom-call(s32[8]{0:T(128)S(1)} %stack.218.refs_0_, bf16[512,4096]{1,0:T(8,128)(2,1)} %bitcast.203, bf16[128,4096]{1,0:T(8,128)(2,1)} %copy-done.1, bf16[128,4096]{1,0:T(8,128)(2,1)} %copy-done.2, bf16[128,4096]{1,0:T(8,128)(2,1)} %copy-done.4, bf16[192,4096]{1,0:T(8,128)(2,1)} %collective-permute-done.13.refs_5_, ...), custom_call_target="tpu_custom_call" | custom-call | flops 1 | bytes 1 | tf_op jit(solution)/shard_map/pallas_call | solution.py:235
  149.0 9.8 %collective-permute-done.16.refs_8_ = bf16[192,4096]{1,0:T(8,128)(2,1)} collective-permute-done((bf16[192,4096]{1,0:T(8,128)(2,1)}, bf16[192,4096]{1,0:T(8,128)(2,1)}, u32[]{:S(2)}, u32[]{:S(2)}) %collective-permute-start.16) | collective-permute-done | bytes 1572896 | tf_op jit(solution)/shard_map/ppermute | solution.py:279
  158.8 1.5 collective-permute-done.17.refs_9_
  160.2 1.9 slice.158
  162.1 1.9 slice.159
  164.8 1.5 collective-permute-start.22
  166.3 2.7 %collective-permute-start.23 = (bf16[2,256,512]{2,1,0:T(8,128)(2,1)}, bf16[2,256,512]{2,1,0:T(8,128)(2,1)}, u32[]{:S(2)}, u32[]{:S(2)}) collective-permute-start(bf16[2,256,512]{2,1,0:T(8,128)(2,1)} %pad_maximum_fusion.8), channel_id=1, source_target_pairs={{0,24},{1,25},{2,26},{3,27},{4,28},{5,29},{6,30},{7,31},{8,0},{9,1... | collective-permute-start | bytes 1572872 | tf_op jit(solution)/shard_map/ppermute | solution.py:279
  170.2 13.8 %shard_map.95.refs_23_ = bf16[1920,1024]{1,0:T(8,128)(2,1)} custom-call(s32[12]{0:T(128)S(1)} %stack.219.refs_0_, bf16[512,4096]{1,0:T(8,128)(2,1)} %bitcast.204, bf16[128,4096]{1,0:T(8,128)(2,1)} %copy-done.1, bf16[128,4096]{1,0:T(8,128)(2,1)} %copy-done.2, bf16[128,4096]{1,0:T(8,128)(2,1)} %copy-done.4, bf16[192,4096]{1,0:T(8,128)(2,1)} %collective-permute-done.13.refs_5_, ...), custom_call_target="tpu_custom_call" | custom-call | flops 1 | bytes 1 | tf_op jit(solution)/shard_map/pallas_call | solution.py:235
  184.9 1.5 collective-permute-done.26.refs_22_
  187.2 13.2 %shard_map.96 = f32[16,8,512]{2,1,0:T(8,128)S(1)} custom-call(s32[20]{0:T(128)S(1)} %stack.194.refs_0_, bf16[512,4096]{1,0:T(8,128)(2,1)} %bitcast.205, bf16[128,4096]{1,0:T(8,128)(2,1)} %copy-done.1, bf16[128,4096]{1,0:T(8,128)(2,1)} %copy-done.2, bf16[128,4096]{1,0:T(8,128)(2,1)} %copy-done.4, bf16[192,4096]{1,0:T(8,128)(2,1)} %collective-permute-done.13.refs_5_, ...), custom_call_target="tpu_custom_call" | custom-call | flops 1 | bytes 1 | tf_op jit(solution)/shard_map/pallas_call | solution.py:235
  201.1 1.5 collective-permute-start.28
  202.7 1.7 collective-permute-start.29
  204.7 2.4 %collective-permute-done.29 = f32[1,32]{1,0:T(1,128)S(1)} collective-permute-done((f32[1,32]{1,0:T(1,128)S(1)}, f32[1,32]{1,0:T(1,128)S(1)}, u32[]{:S(2)}, u32[]{:S(2)}) %collective-permute-start.29) | collective-permute-done | bytes 160 | tf_op jit(solution)/shard_map/ppermute | solution.py:279
  208.4 2.6 %collective-permute-start.32 = (f32[1,32]{1,0:T(1,128)S(1)}, f32[1,32]{1,0:T(1,128)S(1)}, u32[]{:S(2)}, u32[]{:S(2)}) collective-permute-start(f32[1,32]{1,0:T(1,128)S(1)} %add_add_fusion.1), channel_id=1, source_target_pairs={{0,24},{1,25},{2,26},{3,27},{4,28},{5,29},{6,30},{7,31},{8,0},{9,1... | collective-permute-start | bytes 392 | tf_op jit(solution)/shard_map/ppermute | solution.py:279
  (152 shorter events, 32.5 us)
Async XLA Ops:
  0.6 15.0 %copy-start.18 = (s32[4]{0:T(128)S(1)}, s32[4]{0:T(128)}, u32[]{:S(2)}) copy-start(s32[4]{0:T(128)} %param.11) | copy-start | bytes 52
  0.6 15.0 %copy-start.17 = (s32[4]{0:T(128)S(1)}, s32[4]{0:T(128)}, u32[]{:S(2)}) copy-start(s32[4]{0:T(128)} %param.12) | copy-start | bytes 52
  1.4 15.4 %collective-permute-start = (s32[3,4]{1,0:T(4,128)S(1)}, s32[3,4]{1,0:T(4,128)S(1)}, u32[]{:S(2)}, u32[]{:S(2)}) collective-permute-start(s32[3,4]{1,0:T(4,128)S(1)} %get-tuple-element.203), channel_id=1, source_target_pairs={{0,8},{1,9},{2,10},{3,11},{4,12},{5,13},{6,14},{7,15},{8,16},{9,17... | collective-permute-start | bytes 152 | tf_op jit(solution)/shard_map/ppermute | solution.py:279
  4.4 12.4 %collective-permute-start.1 = (s32[3,4]{1,0:T(4,128)S(1)}, s32[3,4]{1,0:T(4,128)S(1)}, u32[]{:S(2)}, u32[]{:S(2)}) collective-permute-start(s32[3,4]{1,0:T(4,128)S(1)} %get-tuple-element.203), channel_id=1, source_target_pairs={{0,16},{1,17},{2,18},{3,19},{4,20},{5,21},{6,22},{7,23},{8,24},{9,... | collective-permute-start | bytes 152 | tf_op jit(solution)/shard_map/ppermute | solution.py:279
  7.0 9.8 %collective-permute-start.2 = (s32[3,4]{1,0:T(4,128)S(1)}, s32[3,4]{1,0:T(4,128)S(1)}, u32[]{:S(2)}, u32[]{:S(2)}) collective-permute-start(s32[3,4]{1,0:T(4,128)S(1)} %get-tuple-element.203), channel_id=1, source_target_pairs={{0,24},{1,25},{2,26},{3,27},{4,28},{5,29},{6,30},{7,31},{8,0},{9,1... | collective-permute-start | bytes 152 | tf_op jit(solution)/shard_map/ppermute | solution.py:279
  10.7 24.5 %collective-permute-start.4 = (bf16[128,4096]{1,0:T(8,128)(2,1)}, bf16[128,4096]{1,0:T(8,128)(2,1)}, u32[]{:S(2)}, u32[]{:S(2)}) collective-permute-start(bf16[128,4096]{1,0:T(8,128)(2,1)} %dynamic-slice_bitcast_fusion), channel_id=1, source_target_pairs={{0,8},{1,9},{2,10},{3,11},{4,12},{5,13},{6,14},{7,15},{8,16},{9,17... | collective-permute-start | bytes 3145736 | tf_op jit(solution)/shard_map/ppermute | solution.py:279
  14.2 25.9 %collective-permute-start.5 = (bf16[128,4096]{1,0:T(8,128)(2,1)}, bf16[128,4096]{1,0:T(8,128)(2,1)S(1)}, u32[]{:S(2)}, u32[]{:S(2)}) collective-permute-start(bf16[128,4096]{1,0:T(8,128)(2,1)} %dynamic-slice_bitcast_fusion), channel_id=1, source_target_pairs={{8,0},{9,1},{10,2},{11,3},{12,4},{13,5},{14,6},{15,7},{16,8},{17,9... | collective-permute-start | bytes 3145736 | tf_op jit(solution)/shard_map/ppermute | solution.py:279
  25.8 1.2 collective-permute-start.3
  27.8 2.6 %copy-start.19 = (bf16[512,2048]{1,0:T(8,128)(2,1)S(1)}, bf16[512,2048]{1,0:T(8,128)(2,1)}, u32[]{:S(2)}) copy-start(bf16[512,2048]{1,0:T(8,128)(2,1)} %param.8) | copy-start | bytes 6291460
  30.4 16.1 %copy-start.11 = (bf16[512,2048]{1,0:T(8,128)(2,1)}, bf16[512,2048]{1,0:T(8,128)(2,1)S(1)}, u32[]{:S(2)}) copy-start(bf16[512,2048]{1,0:T(8,128)(2,1)S(1)} %add_convert_fusion) | copy-start | bytes 6291460
  31.2 15.2 %copy-start.12 = (bf16[512,2048]{1,0:T(8,128)(2,1)}, bf16[512,2048]{1,0:T(8,128)(2,1)S(1)}, u32[]{:S(2)}) copy-start(bf16[512,2048]{1,0:T(8,128)(2,1)S(1)} %add_convert_fusion.1) | copy-start | bytes 6291460
  31.8 14.9 %copy-start.5 = (bf16[2,512,512]{2,1,0:T(8,128)(2,1)}, bf16[2,512,512]{2,1,0:T(8,128)(2,1)S(1)}, u32[]{:S(2)}) copy-start(bf16[2,512,512]{2,1,0:T(8,128)(2,1)S(1)} %pad_maximum_fusion.4.refs_8_.refs_11_.refs_13_) | copy-start | bytes 3145732
  31.8 18.9 %collective-permute-start.10 = (bf16[2,512,512]{2,1,0:T(8,128)(2,1)S(1)}, bf16[2,512,512]{2,1,0:T(8,128)(2,1)S(1)}, u32[]{:S(2)}, u32[]{:S(2)}) collective-permute-start(bf16[2,512,512]{2,1,0:T(8,128)(2,1)S(1)} %pad_maximum_fusion.4.refs_8_.refs_11_.refs_13_), channel_id=1, source_target_pairs={{0,4},{1,5},{2,6},{3,7},{4,0},{5,1},{6,2},{7,3},{8,12},{9,13},{10,... | collective-permute-start | bytes 3145736 | tf_op jit(solution)/shard_map/ppermute | solution.py:279
  40.1 6.5 %copy-start.9 = (bf16[128,4096]{1,0:T(8,128)(2,1)}, bf16[128,4096]{1,0:T(8,128)(2,1)S(1)}, u32[]{:S(2)}) copy-start(bf16[128,4096]{1,0:T(8,128)(2,1)S(1)} %collective-permute-done.5) | copy-start | bytes 3145732
  40.2 38.4 %copy-start.1 = (bf16[128,4096]{1,0:T(8,128)(2,1)}, bf16[128,4096]{1,0:T(8,128)(2,1)S(1)}, u32[]{:S(2)}) copy-start(bf16[128,4096]{1,0:T(8,128)(2,1)S(1)} %broadcast_select_fusion.refs_2_) | copy-start | bytes 3145732
  40.2 10.4 %collective-permute-start.6 = (bf16[128,4096]{1,0:T(8,128)(2,1)}, bf16[128,4096]{1,0:T(8,128)(2,1)}, u32[]{:S(2)}, u32[]{:S(2)}) collective-permute-start(bf16[128,4096]{1,0:T(8,128)(2,1)} %collective-permute-done.4), channel_id=1, source_target_pairs={{8,16},{9,17},{10,18},{11,19},{12,20},{13,21},{14,22},{15,23},{16,... | collective-permute-start | bytes 3145736 | tf_op jit(solution)/shard_map/ppermute | solution.py:279
  41.9 25.7 %collective-permute-start.7 = (bf16[128,4096]{1,0:T(8,128)(2,1)S(1)}, bf16[128,4096]{1,0:T(8,128)(2,1)}, u32[]{:S(2)}, u32[]{:S(2)}) collective-permute-start(bf16[128,4096]{1,0:T(8,128)(2,1)S(1)} %collective-permute-done.5), channel_id=1, source_target_pairs={{8,0},{9,1},{10,2},{11,3},{12,4},{13,5},{14,6},{15,7},{16,8},{17,9... | collective-permute-start | bytes 3145736 | tf_op jit(solution)/shard_map/ppermute | solution.py:279
  43.2 24.4 %collective-permute-start.8 = (bf16[128,4096]{1,0:T(8,128)(2,1)S(1)}, bf16[128,4096]{1,0:T(8,128)(2,1)S(1)}, u32[]{:S(2)}, u32[]{:S(2)}) collective-permute-start(bf16[128,4096]{1,0:T(8,128)(2,1)S(1)} %broadcast_select_fusion.refs_2_), channel_id=1, source_target_pairs={{0,1},{1,0},{2,3},{3,2},{4,5},{5,4},{6,7},{7,6},{8,9},{9,8},{10,11... | collective-permute-start | bytes 3145736 | tf_op jit(solution)/shard_map/ppermute | solution.py:279
  44.7 22.9 %collective-permute-start.9 = (bf16[128,4096]{1,0:T(8,128)(2,1)S(1)}, bf16[128,4096]{1,0:T(8,128)(2,1)S(1)}, u32[]{:S(2)}, u32[]{:S(2)}) collective-permute-start(bf16[128,4096]{1,0:T(8,128)(2,1)S(1)} %broadcast_select_fusion.refs_2_), channel_id=1, source_target_pairs={{0,2},{1,3},{2,0},{3,1},{4,6},{5,7},{6,4},{7,5},{8,10},{9,11},{10,... | collective-permute-start | bytes 3145736 | tf_op jit(solution)/shard_map/ppermute | solution.py:279
  49.5 19.5 %copy-start.10 = (bf16[128,4096]{1,0:T(8,128)(2,1)S(1)}, bf16[128,4096]{1,0:T(8,128)(2,1)}, u32[]{:S(2)}) copy-start(bf16[128,4096]{1,0:T(8,128)(2,1)} %copy-done.9) | copy-start | bytes 3145732
  50.6 17.0 %copy-start.7 = (bf16[2,512,512]{2,1,0:T(8,128)(2,1)}, bf16[2,512,512]{2,1,0:T(8,128)(2,1)S(1)}, u32[]{:S(2)}) copy-start(bf16[2,512,512]{2,1,0:T(8,128)(2,1)S(1)} %collective-permute-done.10.refs_9_.refs_12_.refs_14_) | copy-start | bytes 3145732
  70.5 55.9 %copy-start = (bf16[128,4096]{1,0:T(8,128)(2,1)}, bf16[128,4096]{1,0:T(8,128)(2,1)S(1)}, u32[]{:S(2)}) copy-start(bf16[128,4096]{1,0:T(8,128)(2,1)S(1)} %select_select_fusion.1.refs_7_) | copy-start | bytes 3145732
  72.5 33.6 %collective-permute-start.13 = (bf16[192,4096]{1,0:T(8,128)(2,1)}, bf16[192,4096]{1,0:T(8,128)(2,1)}, u32[]{:S(2)}, u32[]{:S(2)}) collective-permute-start(bf16[192,4096]{1,0:T(8,128)(2,1)} %get-tuple-element.169), channel_id=1, source_target_pairs={{0,1},{1,0},{2,3},{3,2},{4,5},{5,4},{6,7},{7,6},{8,9},{9,8},{10,11... | collective-permute-start | bytes 4718600 | tf_op jit(solution)/shard_map/ppermute | solution.py:279
  74.0 33.3 %collective-permute-start.14 = (bf16[192,4096]{1,0:T(8,128)(2,1)}, bf16[192,4096]{1,0:T(8,128)(2,1)}, u32[]{:S(2)}, u32[]{:S(2)}) collective-permute-start(bf16[192,4096]{1,0:T(8,128)(2,1)} %get-tuple-element.168), channel_id=1, source_target_pairs={{0,2},{1,3},{2,0},{3,1},{4,6},{5,7},{6,4},{7,5},{8,10},{9,11},{10,... | collective-permute-start | bytes 4718600 | tf_op jit(solution)/shard_map/ppermute | solution.py:279
  75.5 9.0 %collective-permute-start.11 = (bf16[128,4096]{1,0:T(8,128)(2,1)}, bf16[128,4096]{1,0:T(8,128)(2,1)}, u32[]{:S(2)}, u32[]{:S(2)}) collective-permute-start(bf16[128,4096]{1,0:T(8,128)(2,1)} %collective-permute-done.6), channel_id=1, source_target_pairs={{16,24},{17,25},{18,26},{19,27},{20,28},{21,29},{22,30},{23,31}} | collective-permute-start | bytes 3145736 | tf_op jit(solution)/shard_map/ppermute | solution.py:279
  77.2 26.1 %collective-permute-start.12 = (bf16[128,4096]{1,0:T(8,128)(2,1)}, bf16[128,4096]{1,0:T(8,128)(2,1)}, u32[]{:S(2)}, u32[]{:S(2)}) collective-permute-start(bf16[128,4096]{1,0:T(8,128)(2,1)} %collective-permute-done.7), channel_id=1, source_target_pairs={{8,0},{9,1},{10,2},{11,3},{12,4},{13,5},{14,6},{15,7}} | collective-permute-start | bytes 3145736 | tf_op jit(solution)/shard_map/ppermute | solution.py:279
  78.6 5.6 %copy-start.3 = (bf16[128,4096]{1,0:T(8,128)(2,1)S(1)}, bf16[128,4096]{1,0:T(8,128)(2,1)}, u32[]{:S(2)}) copy-start(bf16[128,4096]{1,0:T(8,128)(2,1)} %copy-done.2) | copy-start | bytes 3145732
  79.0 45.6 %collective-permute-start.15 = (bf16[2,512,512]{2,1,0:T(8,128)(2,1)}, bf16[2,512,512]{2,1,0:T(8,128)(2,1)}, u32[]{:S(2)}, u32[]{:S(2)}) collective-permute-start(bf16[2,512,512]{2,1,0:T(8,128)(2,1)} %pad_maximum_fusion.6), channel_id=1, source_target_pairs={{0,16},{1,17},{2,18},{3,19},{4,20},{5,21},{6,22},{7,23},{8,24},{9,... | collective-permute-start | bytes 3145736 | tf_op jit(solution)/shard_map/ppermute | solution.py:279
  124.6 34.2 %collective-permute-start.16 = (bf16[192,4096]{1,0:T(8,128)(2,1)}, bf16[192,4096]{1,0:T(8,128)(2,1)}, u32[]{:S(2)}, u32[]{:S(2)}) collective-permute-start(bf16[192,4096]{1,0:T(8,128)(2,1)} %get-tuple-element.107), channel_id=1, source_target_pairs={{0,1},{1,0},{2,3},{3,2},{4,5},{5,4},{6,7},{7,6},{8,9},{9,8},{10,11... | collective-permute-start | bytes 4718600 | tf_op jit(solution)/shard_map/ppermute | solution.py:279
  125.7 34.5 %collective-permute-start.17 = (bf16[192,4096]{1,0:T(8,128)(2,1)}, bf16[192,4096]{1,0:T(8,128)(2,1)}, u32[]{:S(2)}, u32[]{:S(2)}) collective-permute-start(bf16[192,4096]{1,0:T(8,128)(2,1)} %get-tuple-element.108), channel_id=1, source_target_pairs={{0,2},{1,3},{2,0},{3,1},{4,6},{5,7},{6,4},{7,5},{8,10},{9,11},{10,... | collective-permute-start | bytes 4718600 | tf_op jit(solution)/shard_map/ppermute | solution.py:279
  126.2 10.7 %collective-permute-start.20 = (bf16[2,512,512]{2,1,0:T(8,128)(2,1)}, bf16[2,512,512]{2,1,0:T(8,128)(2,1)}, u32[]{:S(2)}, u32[]{:S(2)}) collective-permute-start(bf16[2,512,512]{2,1,0:T(8,128)(2,1)} %collective-permute-done.15.refs_10_.refs_13_.refs_15_), channel_id=1, source_target_pairs={{0,4},{1,5},{2,6},{3,7},{4,0},{5,1},{6,2},{7,3},{8,12},{9,13},{10,... | collective-permute-start | bytes 3145736 | tf_op jit(solution)/shard_map/ppermute | solution.py:279
  126.3 37.7 %collective-permute-start.18 = (bf16[2,512,512]{2,1,0:T(8,128)(2,1)}, bf16[2,512,512]{2,1,0:T(8,128)(2,1)}, u32[]{:S(2)}, u32[]{:S(2)}) collective-permute-start(bf16[2,512,512]{2,1,0:T(8,128)(2,1)} %pad_maximum_fusion.5), channel_id=1, source_target_pairs={{0,8},{1,9},{2,10},{3,11},{4,12},{5,13},{6,14},{7,15},{8,16},{9,17... | collective-permute-start | bytes 3145736 | tf_op jit(solution)/shard_map/ppermute | solution.py:279
  126.8 37.2 %collective-permute-start.19 = (bf16[2,256,512]{2,1,0:T(8,128)(2,1)}, bf16[2,256,512]{2,1,0:T(8,128)(2,1)S(1)}, u32[]{:S(2)}, u32[]{:S(2)}) collective-permute-start(bf16[2,256,512]{2,1,0:T(8,128)(2,1)} %pad_maximum_fusion.7), channel_id=1, source_target_pairs={{0,24},{1,25},{2,26},{3,27},{4,28},{5,29},{6,30},{7,31},{8,0},{9,1... | collective-permute-start | bytes 1572872 | tf_op jit(solution)/shard_map/ppermute | solution.py:279
  164.0 20.0 %copy-start.13 = (bf16[2,256,512]{2,1,0:T(8,128)(2,1)}, bf16[2,256,512]{2,1,0:T(8,128)(2,1)S(1)}, u32[]{:S(2)}) copy-start(bf16[2,256,512]{2,1,0:T(8,128)(2,1)S(1)} %collective-permute-done.19.refs_19_) | copy-start | bytes 1572868
  164.0 5.2 %collective-permute-start.24 = (bf16[2,512,512]{2,1,0:T(8,128)(2,1)}, bf16[2,512,512]{2,1,0:T(8,128)(2,1)S(1)}, u32[]{:S(2)}, u32[]{:S(2)}) collective-permute-start(bf16[2,512,512]{2,1,0:T(8,128)(2,1)} %collective-permute-done.18.refs_15_.refs_17_), channel_id=1, source_target_pairs={{0,4},{1,5},{2,6},{3,7},{4,0},{5,1},{6,2},{7,3},{8,12},{9,13},{10,... | collective-permute-start | bytes 3145736 | tf_op jit(solution)/shard_map/ppermute | solution.py:279
  164.1 19.9 %collective-permute-start.21 = (bf16[64,4096]{1,0:T(8,128)(2,1)}, bf16[64,4096]{1,0:T(8,128)(2,1)S(1)}, u32[]{:S(2)}, u32[]{:S(2)}) collective-permute-start(bf16[64,4096]{1,0:T(8,128)(2,1)} %slice.158), channel_id=1, source_target_pairs={{0,1},{1,0},{2,3},{3,2},{4,5},{5,4},{6,7},{7,6},{8,9},{9,8},{10,11... | collective-permute-start | bytes 1572872 | tf_op jit(solution)/shard_map/ppermute | solution.py:279
  164.8 19.2 %collective-permute-start.22 = (bf16[64,4096]{1,0:T(8,128)(2,1)}, bf16[64,4096]{1,0:T(8,128)(2,1)S(1)}, u32[]{:S(2)}, u32[]{:S(2)}) collective-permute-start(bf16[64,4096]{1,0:T(8,128)(2,1)} %slice.159), channel_id=1, source_target_pairs={{0,2},{1,3},{2,0},{3,1},{4,6},{5,7},{6,4},{7,5},{8,10},{9,11},{10,... | collective-permute-start | bytes 1572872 | tf_op jit(solution)/shard_map/ppermute | solution.py:279
  166.3 17.7 %collective-permute-start.23 = (bf16[2,256,512]{2,1,0:T(8,128)(2,1)}, bf16[2,256,512]{2,1,0:T(8,128)(2,1)}, u32[]{:S(2)}, u32[]{:S(2)}) collective-permute-start(bf16[2,256,512]{2,1,0:T(8,128)(2,1)} %pad_maximum_fusion.8), channel_id=1, source_target_pairs={{0,24},{1,25},{2,26},{3,27},{4,28},{5,29},{6,30},{7,31},{8,0},{9,1... | collective-permute-start | bytes 1572872 | tf_op jit(solution)/shard_map/ppermute | solution.py:279
  169.1 15.0 %collective-permute-start.25 = (bf16[2,256,512]{2,1,0:T(8,128)(2,1)S(1)}, bf16[2,256,512]{2,1,0:T(8,128)(2,1)}, u32[]{:S(2)}, u32[]{:S(2)}) collective-permute-start(bf16[2,256,512]{2,1,0:T(8,128)(2,1)S(1)} %collective-permute-done.19.refs_19_), channel_id=1, source_target_pairs={{0,4},{1,5},{2,6},{3,7},{4,0},{5,1},{6,2},{7,3},{8,12},{9,13},{10,... | collective-permute-start | bytes 1572872 | tf_op jit(solution)/shard_map/ppermute | solution.py:279
  184.0 2.4 %copy-start.14 = (bf16[64,4096]{1,0:T(8,128)(2,1)}, bf16[64,4096]{1,0:T(8,128)(2,1)S(1)}, u32[]{:S(2)}) copy-start(bf16[64,4096]{1,0:T(8,128)(2,1)S(1)} %collective-permute-done.21.refs_11_) | copy-start | bytes 1572868
  184.1 2.3 %collective-permute-start.26 = (bf16[2,256,512]{2,1,0:T(8,128)(2,1)}, bf16[2,256,512]{2,1,0:T(8,128)(2,1)S(1)}, u32[]{:S(2)}, u32[]{:S(2)}) collective-permute-start(bf16[2,256,512]{2,1,0:T(8,128)(2,1)} %collective-permute-done.23.refs_21_), channel_id=1, source_target_pairs={{0,4},{1,5},{2,6},{3,7},{4,0},{5,1},{6,2},{7,3},{8,12},{9,13},{10,... | collective-permute-start | bytes 1572872 | tf_op jit(solution)/shard_map/ppermute | solution.py:279
  200.8 3.6 %collective-permute-start.27 = (f32[1,32]{1,0:T(1,128)S(1)}, f32[1,32]{1,0:T(1,128)S(1)}, u32[]{:S(2)}, u32[]{:S(2)}) collective-permute-start(f32[1,32]{1,0:T(1,128)S(1)} %bitcast.218), channel_id=1, source_target_pairs={{0,1},{1,0},{2,3},{3,2},{4,5},{5,4},{6,7},{7,6},{8,9},{9,8},{10,11... | collective-permute-start | bytes 392 | tf_op jit(solution)/shard_map/ppermute | solution.py:279
  201.1 3.5 %collective-permute-start.28 = (f32[1,32]{1,0:T(1,128)S(1)}, f32[1,32]{1,0:T(1,128)S(1)}, u32[]{:S(2)}, u32[]{:S(2)}) collective-permute-start(f32[1,32]{1,0:T(1,128)S(1)} %bitcast.219), channel_id=1, source_target_pairs={{0,2},{1,3},{2,0},{3,1},{4,6},{5,7},{6,4},{7,5},{8,10},{9,11},{10,... | collective-permute-start | bytes 392 | tf_op jit(solution)/shard_map/ppermute | solution.py:279
  202.7 4.4 %collective-permute-start.29 = (f32[1,32]{1,0:T(1,128)S(1)}, f32[1,32]{1,0:T(1,128)S(1)}, u32[]{:S(2)}, u32[]{:S(2)}) collective-permute-start(f32[1,32]{1,0:T(1,128)S(1)} %bitcast.220), channel_id=1, source_target_pairs={{0,3},{1,2},{2,1},{3,0},{4,7},{5,6},{6,5},{7,4},{8,11},{9,10},{10,... | collective-permute-start | bytes 392 | tf_op jit(solution)/shard_map/ppermute | solution.py:279
  207.1 4.4 %collective-permute-start.30 = (f32[1,32]{1,0:T(1,128)S(1)}, f32[1,32]{1,0:T(1,128)S(1)}, u32[]{:S(2)}, u32[]{:S(2)}) collective-permute-start(f32[1,32]{1,0:T(1,128)S(1)} %add_add_fusion.1), channel_id=1, source_target_pairs={{0,16},{1,17},{2,18},{3,19},{4,20},{5,21},{6,22},{7,23},{8,24},{9,... | collective-permute-start | bytes 392 | tf_op jit(solution)/shard_map/ppermute | solution.py:279
  207.1 5.4 %collective-permute-start.31 = (f32[1,32]{1,0:T(1,128)S(1)}, f32[1,32]{1,0:T(1,128)S(1)}, u32[]{:S(2)}, u32[]{:S(2)}) collective-permute-start(f32[1,32]{1,0:T(1,128)S(1)} %add_add_fusion.1), channel_id=1, source_target_pairs={{0,8},{1,9},{2,10},{3,11},{4,12},{5,13},{6,14},{7,15},{8,16},{9,17... | collective-permute-start | bytes 392 | tf_op jit(solution)/shard_map/ppermute | solution.py:279
  208.4 4.1 %collective-permute-start.32 = (f32[1,32]{1,0:T(1,128)S(1)}, f32[1,32]{1,0:T(1,128)S(1)}, u32[]{:S(2)}, u32[]{:S(2)}) collective-permute-start(f32[1,32]{1,0:T(1,128)S(1)} %add_add_fusion.1), channel_id=1, source_target_pairs={{0,24},{1,25},{2,26},{3,27},{4,28},{5,29},{6,30},{7,31},{8,0},{9,1... | collective-permute-start | bytes 392 | tf_op jit(solution)/shard_map/ppermute | solution.py:279
  212.5 1.2 collective-permute-start.33
  (6 other events, 8.6 us)

commit v4 on v3

--- a/solution.py
+++ b/solution.py
@@ -11,6 +11,7 @@
 learn_rate = 0.0016
 AXES = ("pop", "mp")
 CORES = 2
+FIRST_STAGES, NEXT_STAGES = 2, 1
 SPARE_BYTES = 4 * 1024 * 1024
 
 
@@ -134,22 +135,24 @@
             source = base_refs[base[0]].at[pl.ds(base[1], row)]
             copies.append(pltpu.make_async_copy(source, totals[g], total_sems.at[g]))
         group_copies.append(copies)
-    started = set()
+    taken, stages = set(), []
     for g, (_, first, _, _) in enumerate(plan):
-        for k, copy in enumerate(weight_copies):
-            if plane_of[k] >= first and k not in started:
-                started.add(k)
-                copy.start()
-        for copy in group_copies[g]:
+        fresh = [k for k in range(len(w_refs)) if plane_of[k] >= first and k not in taken]
+        taken.update(fresh)
+        stages.append([weight_copies[k] for k in fresh] + group_copies[g])
+    queue = list(stages)
+
+    def start_stages(count):
+        for copy in [c for stage in queue[:count] for c in stage]:
             copy.start()
+        del queue[:count]
+
+    start_stages(FIRST_STAGES)
     done_rows, out_copies = 0, []
     for g, (_, first, base, own_vectors) in enumerate(plan):
-        for k in sorted(started):
-            if plane_of[k] >= first:
-                started.remove(k)
-                weight_copies[k].wait()
-        for copy in group_copies[g]:
+        for copy in stages[g]:
             copy.wait()
+        start_stages(NEXT_STAGES)
         count = rows[g].shape[0]
         values = [
             jnp.dot(rows[g][...], weights[part, first * plane_rows :], preferred_element_type=jnp.float32)
@@ -184,9 +187,9 @@
                 found.append(value)
             if read_out:
                 gate, up = found
-                hidden = (0.5 * gate * (1.0 + jnp.tanh(0.5 * gate)) * up).astype(jnp.bfloat16)
-                terms = hidden.astype(jnp.float32) * head
-                out_ref[member] = jnp.sum(terms.reshape(seq // 8, 8, columns), axis=0)
+                half = 0.5 * gate
+                hidden = (half + half * jnp.tanh(half)) * up
+                out_ref[member] = jnp.sum(hidden.reshape(seq // 8, 8, columns), axis=0) * head
         if not read_out:
             target = out_ref.at[pl.ds(done_rows, count)]
             out_copies.append(pltpu.make_async_copy(totals[g], target, total_sems.at[g]))
@@ -221,8 +224,10 @@
         buffers.append(pltpu.VMEM((size, (len(keys) - first) * plane_rows), jnp.bfloat16))
         if base is not None or not read_out:
             buffers.append(pltpu.VMEM((size, 2 * columns), jnp.bfloat16))
-    given = [*arrays, *[chunk for _, _, _, chunk in chunks], *base_arrays]
-    given = [pltpu.with_memory_space_constraint(a, pltpu.HBM) for a in given]
+    far = [pltpu.with_memory_space_constraint(a, pltpu.HBM) for a in [*arrays, *base_arrays]]
+    near = [chunk for _, _, _, chunk in chunks]
+    near[::2] = [pltpu.with_memory_space_constraint(a, pltpu.HBM) for a in near[::2]]
+    given = [*far[: len(arrays)], *near, *far[len(arrays) :]]
     extra = [*ranks, *vectors, *read_out]
     held = sum(2 * math.prod(b.shape) for b in buffers) + 4 * total * columns
     held += sum(4 * 128 * a.size // min(128, a.shape[-1]) for a in extra)
@@ -255,6 +260,28 @@
     return terms[0]
 
 
+def own_scores(first, second, start, count, seq):
+    def kernel(start_ref, first_ref, second_ref, out_ref):
+        rewards = (first_ref[...] + second_ref[...]) / seq
+        total = rewards.shape[1]
+        mean = jnp.sum(rewards, axis=1, keepdims=True) / total
+        spread = jnp.sum((rewards - mean) ** 2, axis=1, keepdims=True) / total
+        scores = (rewards - mean) / jnp.sqrt(spread + 1e-05)
+        places = lax.broadcasted_iota(jnp.int32, (count, total), 1)
+        wanted = start_ref[0] + lax.broadcasted_iota(jnp.int32, (count, total), 0)
+        column = jnp.sum(jnp.where(places == wanted, scores, 0.0), axis=1, keepdims=True)
+        row, lane = [lax.broadcasted_iota(jnp.int32, (count, count), axis) for axis in range(2)]
+        out_ref[...] = jnp.sum(jnp.where(row == lane, column, 0.0), axis=0, keepdims=True)
+
+    vmem = pl.BlockSpec(memory_space=pltpu.VMEM)
+    return pl.pallas_call(
+        kernel,
+        out_shape=jax.ShapeDtypeStruct((1, count), jnp.float32),
+        in_specs=[pl.BlockSpec(memory_space=pltpu.SMEM), vmem, vmem],
+        out_specs=vmem,
+    )(start.reshape(1), *[pltpu.with_memory_space_constraint(a, pltpu.VMEM) for a in (first, second)]).reshape(count)
+
+
 def spread_plan(planes, prompts, gate_weight, up_weight, reward_head, member_seeds, counters, member_ranks):
     members_here, seq, width = prompts.shape
     own_rows, own_cols = gate_weight.shape
@@ -331,6 +358,7 @@
 
     small = jnp.stack([member_seeds, counters, member_ranks])
     own_member = lax.dynamic_index_in_dim(prompts, mp_index, 0, keepdims=False)
+    own_member, small = tie(own_member, small)
     hops = [[own_member, up(own_member, 1)], [own_member, down(own_member, 1)]]
     small_here = jnp.stack([small] + [turn(small, s) for s in range(1, planes)])
     small_other = swap_core(small_here)
@@ -363,16 +391,16 @@
             axis=1,
         )
 
+    def on_vector(rows, vector):
+        return lax.dot_general(
+            rows, vector, (((1,), (1,)), ((), ())), preferred_element_type=jnp.float32
+        )
+
     def projected(r, vectors, some):
         found = []
         for i in some:
             parts = [
-                lax.dot_general(
-                    array[first : first + rows],
-                    vectors[i],
-                    (((1,), (1,)), ((), ())),
-                    preferred_element_type=jnp.float32,
-                )
+                on_vector(array[first : first + rows], vectors[i])
                 for array, first, rows in members[r * members_here + i]
             ]
             found.append(parts[0] if len(parts) == 1 else jnp.concatenate(parts))
@@ -413,7 +441,7 @@
 
     half = seq // 2
     fresh = [(0, 0, own_rows)]
-    base, early, early_planes = None, 0, 0
+    base, early, early_planes, waiting = None, 0, 0, 0
 
     def on(some, first, base=None, vectors=None):
         groups = []
@@ -428,9 +456,8 @@
             groups.append((segments, first, None if base is None else (base, i * seq), vectors if vectors is None else vectors + i))
         return groups
 
-    next_here = round_block(1)
-    to_x, to_y, hops[0][1], hops[1][1] = tie(next_here, next_here, hops[0][1], hops[1][1])
-    next_here = to_x
+    hops[0][1], hops[1][1] = tie(hops[0][1], hops[1][1])
+    to_x = to_y = next_here = round_block(1)
     for phase in range(1, planes + 1):
         if phase < planes - 1:
             hops[0].append(up(hops[0][phase], phase + 1))
@@ -461,8 +488,11 @@
 
         ahead = ()
         if phase in leave and phase < planes:
-            hops, new_x, new_y = tie(hops, new_x, new_y)
+            held = [members[waiting * members_here + i][0][0] for i in range(members_here - 1) if waiting]
+            hops, new_x, new_y, held = tie(hops, new_x, new_y, held)
             ahead = next_sends()
+            projs += [on_vector(array, vectors[waiting][i]) for i, array in enumerate(held)]
+            waiting = 0
         held = [chunk for _, _, _, chunk in new_chunks]
         parts = (hops, new_x, new_y, ahead, landed, held, outgoing, base, cols, late, projs, head)
         hops, new_x, new_y, ahead, landed, held, outgoing, base, cols, late, projs, head = tie(*parts)
@@ -476,7 +506,9 @@
             projs += projected(phase - 1, vectors[phase - 1], [members_here - 1])
         if phase < planes:
             members += [[(here, 0, seq)], [(new_x, 0, seq)], [(new_y, 0, seq)]]
-        if phase < planes - 1:
+        if phase < planes - 1 and phase not in leave:
+            waiting = phase
+        elif phase < planes - 1:
             projs += projected(phase, vectors[phase], range(members_here - 1))
 
     last = [c for key in fresh for c in add_chunks(key)]
@@ -499,8 +531,7 @@
         swap_in_plane(rewards, 2) + swap_in_plane(rewards, 3)
     )
     rewards = tree_sum([rewards] + [turn(rewards, s) for s in range(1, planes)])
-    rewards = (rewards + swap_core(rewards)).reshape(total) / seq
-    own = lax.dynamic_slice_in_dim(normalized(rewards), pop_index * members_here, members_here)
+    own = own_scores(rewards, swap_core(rewards), pop_index * members_here, members_here, seq)
     return new_gate, new_up, own
 
 

time: 218 us -> 210 us (0.963)
  starting transfers between devices: 46.5 us -> 42.2 us
  local copies, waits for them, and re-layouts: 15.2 us -> 12.4 us
    ppermute x34, starting transfers between devices: 46.5 us -> 42.2 us  [send(): return lax.ppermute(value, AXES, pairs(move, keep))]
    unnamed x40 -> x58, local copies, waits for them, and re-layouts: 3.22 us -> 0.15 us
    pallas_call x3, Pallas kernels: 39 us -> 36.1 us  [product(): pl.pallas_call(lambda *refs: product_kernel(plan, counts, plane_of, seq,...]
  transfers between devices with their start and end apart: 34 -> 34, of which waited for: 17 -> 20; matrix products, arithmetic and copies ran while one was open for 19% -> 21% of each run, Pallas kernels for 12% -> 11%
where the time goes in v4:
time: 210 us; the launch traced here: 209 us
  waiting for transfers between devices  78.9 us (38%)
  starting transfers between devices  42.2 us (20%)
  Pallas kernels  36.9 us (18%)
  matrix products  20.1 us (10%)
  other arithmetic  16.8 us (8%)
  local copies, waits for them, and re-layouts  12.4 us (6%)
    ppermute x34, waiting for transfers between devices, send(): return lax.ppermute(value, AXES, pairs(move, keep))  78.9 us
    ppermute x34, starting transfers between devices, send(): return lax.ppermute(value, AXES, pairs(move, keep))  42.2 us
    pallas_call x3, Pallas kernels, product(): pl.pallas_call(lambda *refs: product_kernel(plan, counts, plane_of, seq,...  36.1 us
    dot_general x12, matrix products, on_vector(): lax.dot_general(rows, vector, (((1,), (1,)), ((), ())), preferred_element...  16.7 us
    slice x6, local copies, waits for them, and re-layouts, next_sends(): to_x, to_y, here = ([new_y[:half]], [new_x[half:seq]], None)  5.97 us
  transfers between devices with their start and end apart: 34, of which 20 were waited for; matrix products, arithmetic and copies ran while one was open for 21% of the time, Pallas kernels for 11%

profile of v4, /device:TPU:0, one launch (start us, length us, event | category | flops | bytes accessed | tf_op | source)
XLA Modules:
  0.0 208.9 jit_solution(2072111027085793160)
XLA Ops:
  0.7 1.3 dynamic-slice_bitcast_fusion
  2.0 3.1 %collective-permute-start = (s32[3,4]{1,0:T(4,128)S(1)}, s32[3,4]{1,0:T(4,128)S(1)}, u32[]{:S(2)}, u32[]{:S(2)}) collective-permute-start(s32[3,4]{1,0:T(4,128)S(1)} %pad_add_fusion.1), channel_id=1, source_target_pairs={{0,8},{1,9},{2,10},{3,11},{4,12},{5,13},{6,14},{7,15},{8,16},{9,17... | collective-permute-start | bytes 152 | tf_op jit(solution)/shard_map/ppermute | solution.py:306
  5.1 2.6 %collective-permute-start.1 = (s32[3,4]{1,0:T(4,128)S(1)}, s32[3,4]{1,0:T(4,128)S(1)}, u32[]{:S(2)}, u32[]{:S(2)}) collective-permute-start(s32[3,4]{1,0:T(4,128)S(1)} %pad_add_fusion.1), channel_id=1, source_target_pairs={{0,16},{1,17},{2,18},{3,19},{4,20},{5,21},{6,22},{7,23},{8,24},{9,... | collective-permute-start | bytes 152 | tf_op jit(solution)/shard_map/ppermute | solution.py:306
  7.7 1.3 collective-permute-start.2
  9.0 3.6 %collective-permute-start.4 = (bf16[128,4096]{1,0:T(8,128)(2,1)S(1)}, bf16[128,4096]{1,0:T(8,128)(2,1)}, u32[]{:S(2)}, u32[]{:S(2)}) collective-permute-start(bf16[128,4096]{1,0:T(8,128)(2,1)S(1)} %dynamic-slice_bitcast_fusion), channel_id=1, source_target_pairs={{0,8},{1,9},{2,10},{3,11},{4,12},{5,13},{6,14},{7,15},{8,16},{9,17... | collective-permute-start | bytes 3145736 | tf_op jit(solution)/shard_map/ppermute | solution.py:306
  12.6 1.3 collective-permute-start.5
  15.5 2.7 %fusion.130 = (bf16[4,1,4096]{2,1,0:T(2,128)(2,1)S(1)}, bf16[4,1,4096]{2,1,0:T(2,128)(2,1)S(1)}, bf16[4,1,4096]{2,1,0:T(2,128)(2,1)}, bf16[4,1,4096]{2,1,0:T(2,1...) fusion(s32[4096]{0:T(1024)S(1)} %iota_multiply_fusion, ...), kind=kLoop, calls=%fused_computation.194 | loop fusion | flops 1966080 | bytes 278656 | tf_op jit(solution)/shard_map/convert_element_type | solution.py:390
  18.2 1.6 convolution_bitcast_fusion
  19.9 1.6 convolution_bitcast_fusion.1
  21.5 2.2 %convolution_bitcast_fusion.2 = f32[128,2]{0,1:T(2,128)} fusion(bf16[4,128,4096]{2,1,0:T(8,128)(2,1)} %param.7, bf16[4,1,4096]{2,1,0:T(2,128)(2,1)S(1)} %get-tuple-element.181, bf16[4,1,4096]{2,1,0:T(2,128)(2,1)S(1)} %get-tuple-element.180), kind=kOutput, calls=%fused_computation.12 | convolution fusion | flops 2129920 | bytes 1115136 | tf_op jit(solution)/shard_map/dot_general | solution.py:395
  23.7 2.2 %convolution_bitcast_fusion.3 = f32[128,2]{0,1:T(2,128)} fusion(bf16[4,128,4096]{2,1,0:T(8,128)(2,1)} %param.7, bf16[4,1,4096]{2,1,0:T(2,128)(2,1)S(1)} %get-tuple-element.181, bf16[4,1,4096]{2,1,0:T(2,128)(2,1)S(1)} %get-tuple-element.180), kind=kOutput, calls=%fused_computation.13 | convolution fusion | flops 2129920 | bytes 1115136 | tf_op jit(solution)/shard_map/dot_general | solution.py:395
  28.5 2.6 %add_convert_fusion = bf16[512,2048]{1,0:T(8,128)(2,1)S(1)} fusion(bf16[512,2048]{1,0:T(8,128)(2,1)} %param.9, s32[32]{0:T(128)S(1)} %get-tuple-element.214, s32[2048]{0:T(1024)S(1)} %add_multiply_fusion, s32[32]{0:T(128)S(1)} %get-tuple-element.213, f32[32]{0:T(128)S(1)} %reshape.1829, s32[512]{0:T(512)S(1)} %add_multiply_fusion.2), kind=kOutput, calls=%fused_computation | convolution fusion | flops 72531968 | bytes 4204928 | tf_op jit(solution)/shard_map/dot_general | solution.py:48
  33.2 5.2 %collective-permute-done.5 = bf16[128,4096]{1,0:T(8,128)(2,1)} collective-permute-done((bf16[128,4096]{1,0:T(8,128)(2,1)S(1)}, bf16[128,4096]{1,0:T(8,128)(2,1)}, u32[]{:S(2)}, u32[]{:S(2)}) %collective-permute-start.5) | collective-permute-done | bytes 1048608 | tf_op jit(solution)/shard_map/ppermute | solution.py:306
  38.4 1.3 broadcast_select_fusion.refs_2_
  39.7 1.6 collective-permute-start.8
  41.3 1.5 collective-permute-start.9
  42.8 1.6 collective-permute-start.6
  50.0 12.6 %collective-permute-done.8.refs_3_ = bf16[128,4096]{1,0:T(8,128)(2,1)S(1)} collective-permute-done((bf16[128,4096]{1,0:T(8,128)(2,1)S(1)}, bf16[128,4096]{1,0:T(8,128)(2,1)S(1)}, u32[]{:S(2)}, u32[]{:S(2)}) %collective-permute-start.8) | collective-permute-done | bytes 1048608 | tf_op jit(solution)/shard_map/ppermute | solution.py:306
  63.9 5.1 %collective-permute-done.7 = bf16[128,4096]{1,0:T(8,128)(2,1)} collective-permute-done((bf16[128,4096]{1,0:T(8,128)(2,1)}, bf16[128,4096]{1,0:T(8,128)(2,1)}, u32[]{:S(2)}, u32[]{:S(2)}) %collective-permute-start.7) | collective-permute-done | bytes 1048608 | tf_op jit(solution)/shard_map/ppermute | solution.py:306
  69.0 1.4 select_select_fusion.1.refs_7_
  70.4 2.0 pad_maximum_fusion
  74.2 1.3 collective-permute-start.12
  76.5 23.6 %collective-permute-done.12 = bf16[128,4096]{1,0:T(8,128)(2,1)} collective-permute-done((bf16[128,4096]{1,0:T(8,128)(2,1)}, bf16[128,4096]{1,0:T(8,128)(2,1)}, u32[]{:S(2)}, u32[]{:S(2)}) %collective-permute-start.12) | collective-permute-done | bytes 1048608 | tf_op jit(solution)/shard_map/ppermute | solution.py:306
  100.0 5.3 %collective-permute-done.13.refs_5_ = bf16[192,4096]{1,0:T(8,128)(2,1)} collective-permute-done((bf16[192,4096]{1,0:T(8,128)(2,1)}, bf16[192,4096]{1,0:T(8,128)(2,1)}, u32[]{:S(2)}, u32[]{:S(2)}) %collective-permute-start.13) | collective-permute-done | bytes 1572896 | tf_op jit(solution)/shard_map/ppermute | solution.py:306
  105.6 1.4 select_select_fusion.refs_10_
  112.2 2.0 pad_maximum_fusion.2
  114.1 6.1 %collective-permute-done.15.refs_10_.refs_13_.refs_15_ = bf16[2,512,512]{2,1,0:T(8,128)(2,1)} collective-permute-done((bf16[2,512,512]{2,1,0:T(8,128)(2,1)}, bf16[2,512,512]{2,1,0:T(8,128)(2,1)}, u32[]{:S(2)}, u32[]{:S(2)}) %collective-permute-start.15) | collective-permute-done | bytes 1048608 | tf_op jit(solution)/shard_map/ppermute | solution.py:306
  120.2 1.5 collective-permute-start.16
  121.7 1.5 collective-permute-start.17
  123.9 4.0 %collective-permute-start.19 = (bf16[2,256,512]{2,1,0:T(8,128)(2,1)}, bf16[2,256,512]{2,1,0:T(8,128)(2,1)}, u32[]{:S(2)}, u32[]{:S(2)}) collective-permute-start(bf16[2,256,512]{2,1,0:T(8,128)(2,1)} %pad_maximum_fusion.7), channel_id=1, source_target_pairs={{0,24},{1,25},{2,26},{3,27},{4,28},{5,29},{6,30},{7,31},{8,0},{9,1... | collective-permute-start | bytes 1572872 | tf_op jit(solution)/shard_map/ppermute | solution.py:306
  129.1 1.3 fusion.19
  130.4 1.6 fusion.7
  132.1 1.6 fusion.9
  135.4 10.4 %shard_map.94.refs_17_ = bf16[1408,1024]{1,0:T(8,128)(2,1)} custom-call(s32[8]{0:T(128)S(1)} %stack.218.refs_0_, bf16[512,4096]{1,0:T(8,128)(2,1)} %bitcast.202, bf16[128,4096]{1,0:T(8,128)(2,1)} %copy-done.2, bf16[128,4096]{1,0:T(8,128)(2,1)} %copy-done.4, bf16[128,4096]{1,0:T(8,128)(2,1)} %copy-done.6, bf16[192,4096]{1,0:T(8,128)(2,1)} %collective-permute-done.13.refs_5_, ...), custom_call_target="tpu_custom_call" | custom-call | flops 1 | bytes 1 | tf_op jit(solution)/shard_map/pallas_call | solution.py:240
  145.8 8.2 %collective-permute-done.16.refs_8_ = bf16[192,4096]{1,0:T(8,128)(2,1)} collective-permute-done((bf16[192,4096]{1,0:T(8,128)(2,1)}, bf16[192,4096]{1,0:T(8,128)(2,1)}, u32[]{:S(2)}, u32[]{:S(2)}) %collective-permute-start.16) | collective-permute-done | bytes 1572896 | tf_op jit(solution)/shard_map/ppermute | solution.py:306
  155.3 1.9 slice.158
  157.1 1.9 slice.159
  159.0 2.1 %collective-permute-done.19.refs_19_ = bf16[2,256,512]{2,1,0:T(8,128)(2,1)} collective-permute-done((bf16[2,256,512]{2,1,0:T(8,128)(2,1)}, bf16[2,256,512]{2,1,0:T(8,128)(2,1)}, u32[]{:S(2)}, u32[]{:S(2)}) %collective-permute-start.19) | collective-permute-done | bytes 524320 | tf_op jit(solution)/shard_map/ppermute | solution.py:306
  162.2 3.6 %collective-permute-start.23 = (bf16[2,256,512]{2,1,0:T(8,128)(2,1)}, bf16[2,256,512]{2,1,0:T(8,128)(2,1)}, u32[]{:S(2)}, u32[]{:S(2)}) collective-permute-start(bf16[2,256,512]{2,1,0:T(8,128)(2,1)} %pad_maximum_fusion.8), channel_id=1, source_target_pairs={{0,24},{1,25},{2,26},{3,27},{4,28},{5,29},{6,30},{7,31},{8,0},{9,1... | collective-permute-start | bytes 1572872 | tf_op jit(solution)/shard_map/ppermute | solution.py:306
  165.9 13.5 %shard_map.95.refs_23_ = bf16[1920,1024]{1,0:T(8,128)(2,1)} custom-call(s32[12]{0:T(128)S(1)} %stack.219.refs_0_, bf16[512,4096]{1,0:T(8,128)(2,1)} %bitcast.203, bf16[128,4096]{1,0:T(8,128)(2,1)} %copy-done.2, bf16[128,4096]{1,0:T(8,128)(2,1)} %copy-done.4, bf16[128,4096]{1,0:T(8,128)(2,1)} %copy-done.6, bf16[192,4096]{1,0:T(8,128)(2,1)} %collective-permute-done.13.refs_5_, ...), custom_call_target="tpu_custom_call" | custom-call | flops 1 | bytes 1 | tf_op jit(solution)/shard_map/pallas_call | solution.py:240
  180.2 1.6 collective-permute-done.26.refs_22_
  181.9 12.2 %shard_map.96 = f32[16,8,512]{2,1,0:T(8,128)S(1)} custom-call(s32[20]{0:T(128)S(1)} %stack.194.refs_0_, bf16[512,4096]{1,0:T(8,128)(2,1)} %bitcast.204, bf16[128,4096]{1,0:T(8,128)(2,1)} %copy-done.2, bf16[128,4096]{1,0:T(8,128)(2,1)} %copy-done.4, bf16[128,4096]{1,0:T(8,128)(2,1)} %copy-done.6, bf16[192,4096]{1,0:T(8,128)(2,1)} %collective-permute-done.13.refs_5_, ...), custom_call_target="tpu_custom_call" | custom-call | flops 1 | bytes 1 | tf_op jit(solution)/shard_map/pallas_call | solution.py:240
  194.4 1.6 collective-permute-start.27
  196.5 1.5 collective-permute-start.29
  198.0 1.5 collective-permute-done.28
  199.5 1.4 collective-permute-done.29
  200.9 2.5 %collective-permute-start.31 = (f32[1,32]{1,0:T(1,128)S(1)}, f32[1,32]{1,0:T(1,128)S(1)}, u32[]{:S(2)}, u32[]{:S(2)}) collective-permute-start(f32[1,32]{1,0:T(1,128)S(1)} %add_add_fusion.1), channel_id=1, source_target_pairs={{0,8},{1,9},{2,10},{3,11},{4,12},{5,13},{6,14},{7,15},{8,16},{9,17... | collective-permute-start | bytes 392 | tf_op jit(solution)/shard_map/ppermute | solution.py:306
  203.4 1.4 collective-permute-start.32
  (166 shorter events, 32.4 us)
Async XLA Ops:
  2.0 13.1 %collective-permute-start = (s32[3,4]{1,0:T(4,128)S(1)}, s32[3,4]{1,0:T(4,128)S(1)}, u32[]{:S(2)}, u32[]{:S(2)}) collective-permute-start(s32[3,4]{1,0:T(4,128)S(1)} %pad_add_fusion.1), channel_id=1, source_target_pairs={{0,8},{1,9},{2,10},{3,11},{4,12},{5,13},{6,14},{7,15},{8,16},{9,17... | collective-permute-start | bytes 152 | tf_op jit(solution)/shard_map/ppermute | solution.py:306
  5.1 10.0 %collective-permute-start.1 = (s32[3,4]{1,0:T(4,128)S(1)}, s32[3,4]{1,0:T(4,128)S(1)}, u32[]{:S(2)}, u32[]{:S(2)}) collective-permute-start(s32[3,4]{1,0:T(4,128)S(1)} %pad_add_fusion.1), channel_id=1, source_target_pairs={{0,16},{1,17},{2,18},{3,19},{4,20},{5,21},{6,22},{7,23},{8,24},{9,... | collective-permute-start | bytes 152 | tf_op jit(solution)/shard_map/ppermute | solution.py:306
  7.7 7.4 %collective-permute-start.2 = (s32[3,4]{1,0:T(4,128)S(1)}, s32[3,4]{1,0:T(4,128)S(1)}, u32[]{:S(2)}, u32[]{:S(2)}) collective-permute-start(s32[3,4]{1,0:T(4,128)S(1)} %pad_add_fusion.1), channel_id=1, source_target_pairs={{0,24},{1,25},{2,26},{3,27},{4,28},{5,29},{6,30},{7,31},{8,0},{9,1... | collective-permute-start | bytes 152 | tf_op jit(solution)/shard_map/ppermute | solution.py:306
  9.0 24.1 %collective-permute-start.4 = (bf16[128,4096]{1,0:T(8,128)(2,1)S(1)}, bf16[128,4096]{1,0:T(8,128)(2,1)}, u32[]{:S(2)}, u32[]{:S(2)}) collective-permute-start(bf16[128,4096]{1,0:T(8,128)(2,1)S(1)} %dynamic-slice_bitcast_fusion), channel_id=1, source_target_pairs={{0,8},{1,9},{2,10},{3,11},{4,12},{5,13},{6,14},{7,15},{8,16},{9,17... | collective-permute-start | bytes 3145736 | tf_op jit(solution)/shard_map/ppermute | solution.py:306
  12.6 25.8 %collective-permute-start.5 = (bf16[128,4096]{1,0:T(8,128)(2,1)S(1)}, bf16[128,4096]{1,0:T(8,128)(2,1)}, u32[]{:S(2)}, u32[]{:S(2)}) collective-permute-start(bf16[128,4096]{1,0:T(8,128)(2,1)S(1)} %dynamic-slice_bitcast_fusion), channel_id=1, source_target_pairs={{8,0},{9,1},{10,2},{11,3},{12,4},{13,5},{14,6},{15,7},{16,8},{17,9... | collective-permute-start | bytes 3145736 | tf_op jit(solution)/shard_map/ppermute | solution.py:306
  26.0 1.8 collective-permute-start.3
  31.1 14.9 %copy-start.10 = (bf16[512,2048]{1,0:T(8,128)(2,1)}, bf16[512,2048]{1,0:T(8,128)(2,1)S(1)}, u32[]{:S(2)}) copy-start(bf16[512,2048]{1,0:T(8,128)(2,1)S(1)} %add_convert_fusion) | copy-start | bytes 6291460
  32.0 14.0 %copy-start.11 = (bf16[512,2048]{1,0:T(8,128)(2,1)}, bf16[512,2048]{1,0:T(8,128)(2,1)S(1)}, u32[]{:S(2)}) copy-start(bf16[512,2048]{1,0:T(8,128)(2,1)S(1)} %add_convert_fusion.1) | copy-start | bytes 6291460
  32.5 13.7 %copy-start.8 = (bf16[2,512,512]{2,1,0:T(8,128)(2,1)}, bf16[2,512,512]{2,1,0:T(8,128)(2,1)S(1)}, u32[]{:S(2)}) copy-start(bf16[2,512,512]{2,1,0:T(8,128)(2,1)S(1)} %pad_maximum_fusion.4.refs_8_.refs_11_.refs_13_) | copy-start | bytes 3145732
  32.5 13.3 %copy-start.16 = (bf16[4,1,4096]{2,1,0:T(2,128)(2,1)S(1)}, bf16[4,1,4096]{2,1,0:T(2,128)(2,1)}, u32[]{:S(2)}) copy-start(bf16[4,1,4096]{2,1,0:T(2,128)(2,1)} %get-tuple-element.178) | copy-start | bytes 98308
  32.5 13.3 %copy-start.17 = (bf16[4,1,4096]{2,1,0:T(2,128)(2,1)S(1)}, bf16[4,1,4096]{2,1,0:T(2,128)(2,1)}, u32[]{:S(2)}) copy-start(bf16[4,1,4096]{2,1,0:T(2,128)(2,1)} %get-tuple-element.179) | copy-start | bytes 98308
  32.5 13.3 %copy-start.19 = (bf16[1,2,4096]{2,1,0:T(2,128)(2,1)S(1)}, bf16[1,2,4096]{2,1,0:T(2,128)(2,1)}, u32[]{:S(2)}) copy-start(bf16[1,2,4096]{2,1,0:T(2,128)(2,1)} %slice_maximum_fusion) | copy-start | bytes 49156
  32.5 17.5 %collective-permute-start.10 = (bf16[2,512,512]{2,1,0:T(8,128)(2,1)S(1)}, bf16[2,512,512]{2,1,0:T(8,128)(2,1)S(1)}, u32[]{:S(2)}, u32[]{:S(2)}) collective-permute-start(bf16[2,512,512]{2,1,0:T(8,128)(2,1)S(1)} %pad_maximum_fusion.4.refs_8_.refs_11_.refs_13_), channel_id=1, source_target_pairs={{0,4},{1,5},{2,6},{3,7},{4,0},{5,1},{6,2},{7,3},{8,12},{9,13},{10,... | collective-permute-start | bytes 3145736 | tf_op jit(solution)/shard_map/ppermute | solution.py:306
  39.7 22.9 %collective-permute-start.8 = (bf16[128,4096]{1,0:T(8,128)(2,1)S(1)}, bf16[128,4096]{1,0:T(8,128)(2,1)S(1)}, u32[]{:S(2)}, u32[]{:S(2)}) collective-permute-start(bf16[128,4096]{1,0:T(8,128)(2,1)S(1)} %broadcast_select_fusion.refs_2_), channel_id=1, source_target_pairs={{0,1},{1,0},{2,3},{3,2},{4,5},{5,4},{6,7},{7,6},{8,9},{9,8},{10,11... | collective-permute-start | bytes 3145736 | tf_op jit(solution)/shard_map/ppermute | solution.py:306
  41.3 22.6 %collective-permute-start.9 = (bf16[128,4096]{1,0:T(8,128)(2,1)S(1)}, bf16[128,4096]{1,0:T(8,128)(2,1)S(1)}, u32[]{:S(2)}, u32[]{:S(2)}) collective-permute-start(bf16[128,4096]{1,0:T(8,128)(2,1)S(1)} %broadcast_select_fusion.refs_2_), channel_id=1, source_target_pairs={{0,2},{1,3},{2,0},{3,1},{4,6},{5,7},{6,4},{7,5},{8,10},{9,11},{10,... | collective-permute-start | bytes 3145736 | tf_op jit(solution)/shard_map/ppermute | solution.py:306
  42.8 21.1 %collective-permute-start.6 = (bf16[128,4096]{1,0:T(8,128)(2,1)}, bf16[128,4096]{1,0:T(8,128)(2,1)}, u32[]{:S(2)}, u32[]{:S(2)}) collective-permute-start(bf16[128,4096]{1,0:T(8,128)(2,1)} %collective-permute-done.4), channel_id=1, source_target_pairs={{8,16},{9,17},{10,18},{11,19},{12,20},{13,21},{14,22},{15,23},{16,... | collective-permute-start | bytes 3145736 | tf_op jit(solution)/shard_map/ppermute | solution.py:306
  44.4 24.5 %collective-permute-start.7 = (bf16[128,4096]{1,0:T(8,128)(2,1)}, bf16[128,4096]{1,0:T(8,128)(2,1)}, u32[]{:S(2)}, u32[]{:S(2)}) collective-permute-start(bf16[128,4096]{1,0:T(8,128)(2,1)} %collective-permute-done.5), channel_id=1, source_target_pairs={{8,0},{9,1},{10,2},{11,3},{12,4},{13,5},{14,6},{15,7},{16,8},{17,9... | collective-permute-start | bytes 3145736 | tf_op jit(solution)/shard_map/ppermute | solution.py:306
  72.4 32.9 %collective-permute-start.13 = (bf16[192,4096]{1,0:T(8,128)(2,1)}, bf16[192,4096]{1,0:T(8,128)(2,1)}, u32[]{:S(2)}, u32[]{:S(2)}) collective-permute-start(bf16[192,4096]{1,0:T(8,128)(2,1)} %get-tuple-element.175), channel_id=1, source_target_pairs={{0,1},{1,0},{2,3},{3,2},{4,5},{5,4},{6,7},{7,6},{8,9},{9,8},{10,11... | collective-permute-start | bytes 4718600 | tf_op jit(solution)/shard_map/ppermute | solution.py:306
  73.0 32.6 %collective-permute-start.14 = (bf16[192,4096]{1,0:T(8,128)(2,1)}, bf16[192,4096]{1,0:T(8,128)(2,1)}, u32[]{:S(2)}, u32[]{:S(2)}) collective-permute-start(bf16[192,4096]{1,0:T(8,128)(2,1)} %get-tuple-element.174), channel_id=1, source_target_pairs={{0,2},{1,3},{2,0},{3,1},{4,6},{5,7},{6,4},{7,5},{8,10},{9,11},{10,... | collective-permute-start | bytes 4718600 | tf_op jit(solution)/shard_map/ppermute | solution.py:306
  73.5 3.0 %collective-permute-start.11 = (bf16[128,4096]{1,0:T(8,128)(2,1)}, bf16[128,4096]{1,0:T(8,128)(2,1)S(1)}, u32[]{:S(2)}, u32[]{:S(2)}) collective-permute-start(bf16[128,4096]{1,0:T(8,128)(2,1)} %collective-permute-done.6), channel_id=1, source_target_pairs={{16,24},{17,25},{18,26},{19,27},{20,28},{21,29},{22,30},{23,31}} | collective-permute-start | bytes 3145736 | tf_op jit(solution)/shard_map/ppermute | solution.py:306
  74.2 25.8 %collective-permute-start.12 = (bf16[128,4096]{1,0:T(8,128)(2,1)}, bf16[128,4096]{1,0:T(8,128)(2,1)}, u32[]{:S(2)}, u32[]{:S(2)}) collective-permute-start(bf16[128,4096]{1,0:T(8,128)(2,1)} %collective-permute-done.7), channel_id=1, source_target_pairs={{8,0},{9,1},{10,2},{11,3},{12,4},{13,5},{14,6},{15,7}} | collective-permute-start | bytes 3145736 | tf_op jit(solution)/shard_map/ppermute | solution.py:306
  75.6 31.4 %copy-start.7 = (bf16[128,4096]{1,0:T(8,128)(2,1)S(1)}, bf16[128,4096]{1,0:T(8,128)(2,1)}, u32[]{:S(2)}) copy-start(bf16[128,4096]{1,0:T(8,128)(2,1)} %copy-done.6) | copy-start | bytes 3145732
  75.6 44.6 %collective-permute-start.15 = (bf16[2,512,512]{2,1,0:T(8,128)(2,1)}, bf16[2,512,512]{2,1,0:T(8,128)(2,1)}, u32[]{:S(2)}, u32[]{:S(2)}) collective-permute-start(bf16[2,512,512]{2,1,0:T(8,128)(2,1)} %pad_maximum_fusion.6), channel_id=1, source_target_pairs={{0,16},{1,17},{2,18},{3,19},{4,20},{5,21},{6,22},{7,23},{8,24},{9,... | collective-permute-start | bytes 3145736 | tf_op jit(solution)/shard_map/ppermute | solution.py:306
  112.1 11.3 %copy-start.1 = (bf16[128,4096]{1,0:T(8,128)(2,1)S(1)}, bf16[128,4096]{1,0:T(8,128)(2,1)}, u32[]{:S(2)}) copy-start(bf16[128,4096]{1,0:T(8,128)(2,1)} %copy-done) | copy-start | bytes 3145732
  112.1 11.3 %copy-start.13 = (bf16[4,1,4096]{2,1,0:T(2,128)(2,1)S(1)}, bf16[4,1,4096]{2,1,0:T(2,128)(2,1)}, u32[]{:S(2)}) copy-start(bf16[4,1,4096]{2,1,0:T(2,128)(2,1)} %copy-done.12) | copy-start | bytes 98308
  112.1 11.3 %copy-start.15 = (bf16[4,1,4096]{2,1,0:T(2,128)(2,1)S(1)}, bf16[4,1,4096]{2,1,0:T(2,128)(2,1)}, u32[]{:S(2)}) copy-start(bf16[4,1,4096]{2,1,0:T(2,128)(2,1)} %copy-done.14) | copy-start | bytes 98308
  120.2 33.8 %collective-permute-start.16 = (bf16[192,4096]{1,0:T(8,128)(2,1)}, bf16[192,4096]{1,0:T(8,128)(2,1)}, u32[]{:S(2)}, u32[]{:S(2)}) collective-permute-start(bf16[192,4096]{1,0:T(8,128)(2,1)} %get-tuple-element.113), channel_id=1, source_target_pairs={{0,1},{1,0},{2,3},{3,2},{4,5},{5,4},{6,7},{7,6},{8,9},{9,8},{10,11... | collective-permute-start | bytes 4718600 | tf_op jit(solution)/shard_map/ppermute | solution.py:306
  121.7 33.6 %collective-permute-start.17 = (bf16[192,4096]{1,0:T(8,128)(2,1)}, bf16[192,4096]{1,0:T(8,128)(2,1)}, u32[]{:S(2)}, u32[]{:S(2)}) collective-permute-start(bf16[192,4096]{1,0:T(8,128)(2,1)} %get-tuple-element.114), channel_id=1, source_target_pairs={{0,2},{1,3},{2,0},{3,1},{4,6},{5,7},{6,4},{7,5},{8,10},{9,11},{10,... | collective-permute-start | bytes 4718600 | tf_op jit(solution)/shard_map/ppermute | solution.py:306
  123.3 12.1 %collective-permute-start.20 = (bf16[2,512,512]{2,1,0:T(8,128)(2,1)}, bf16[2,512,512]{2,1,0:T(8,128)(2,1)S(1)}, u32[]{:S(2)}, u32[]{:S(2)}) collective-permute-start(bf16[2,512,512]{2,1,0:T(8,128)(2,1)} %collective-permute-done.15.refs_10_.refs_13_.refs_15_), channel_id=1, source_target_pairs={{0,4},{1,5},{2,6},{3,7},{4,0},{5,1},{6,2},{7,3},{8,12},{9,13},{10,... | collective-permute-start | bytes 3145736 | tf_op jit(solution)/shard_map/ppermute | solution.py:306
  123.3 37.8 %collective-permute-start.18 = (bf16[2,512,512]{2,1,0:T(8,128)(2,1)}, bf16[2,512,512]{2,1,0:T(8,128)(2,1)}, u32[]{:S(2)}, u32[]{:S(2)}) collective-permute-start(bf16[2,512,512]{2,1,0:T(8,128)(2,1)} %pad_maximum_fusion.5), channel_id=1, source_target_pairs={{0,8},{1,9},{2,10},{3,11},{4,12},{5,13},{6,14},{7,15},{8,16},{9,17... | collective-permute-start | bytes 3145736 | tf_op jit(solution)/shard_map/ppermute | solution.py:306
  123.8 9.9 %copy-start.22 = (f32[128,2]{0,1:T(2,128)S(1)}, f32[128,2]{0,1:T(2,128)}, u32[]{:S(2)}) copy-start(f32[128,2]{0,1:T(2,128)} %fusion.171) | copy-start | bytes 3076
  123.8 9.9 %copy-start.23 = (f32[128,2]{0,1:T(2,128)S(1)}, f32[128,2]{0,1:T(2,128)}, u32[]{:S(2)}) copy-start(f32[128,2]{0,1:T(2,128)} %fusion.174) | copy-start | bytes 3076
  123.8 9.9 %copy-start.24 = (f32[128,2]{0,1:T(2,128)S(1)}, f32[128,2]{0,1:T(2,128)}, u32[]{:S(2)}) copy-start(f32[128,2]{0,1:T(2,128)} %fusion.177) | copy-start | bytes 3076
  123.9 37.3 %collective-permute-start.19 = (bf16[2,256,512]{2,1,0:T(8,128)(2,1)}, bf16[2,256,512]{2,1,0:T(8,128)(2,1)}, u32[]{:S(2)}, u32[]{:S(2)}) collective-permute-start(bf16[2,256,512]{2,1,0:T(8,128)(2,1)} %pad_maximum_fusion.7), channel_id=1, source_target_pairs={{0,24},{1,25},{2,26},{3,27},{4,28},{5,29},{6,30},{7,31},{8,0},{9,1... | collective-permute-start | bytes 1572872 | tf_op jit(solution)/shard_map/ppermute | solution.py:306
  145.8 20.0 %copy-start.18 = (f32[2,5,512]{2,0,1:T(2,128)S(1)}, f32[2,5,512]{2,0,1:T(2,128)}, u32[]{:S(2)}) copy-start(f32[2,5,512]{2,0,1:T(2,128)} %copy.82) | copy-start | bytes 61444
  161.1 4.8 %collective-permute-start.24 = (bf16[2,512,512]{2,1,0:T(8,128)(2,1)}, bf16[2,512,512]{2,1,0:T(8,128)(2,1)}, u32[]{:S(2)}, u32[]{:S(2)}) collective-permute-start(bf16[2,512,512]{2,1,0:T(8,128)(2,1)} %collective-permute-done.18.refs_15_.refs_17_), channel_id=1, source_target_pairs={{0,4},{1,5},{2,6},{3,7},{4,0},{5,1},{6,2},{7,3},{8,12},{9,13},{10,... | collective-permute-start | bytes 3145736 | tf_op jit(solution)/shard_map/ppermute | solution.py:306
  161.1 18.3 %collective-permute-start.21 = (bf16[64,4096]{1,0:T(8,128)(2,1)}, bf16[64,4096]{1,0:T(8,128)(2,1)}, u32[]{:S(2)}, u32[]{:S(2)}) collective-permute-start(bf16[64,4096]{1,0:T(8,128)(2,1)} %slice.158), channel_id=1, source_target_pairs={{0,1},{1,0},{2,3},{3,2},{4,5},{5,4},{6,7},{7,6},{8,9},{9,8},{10,11... | collective-permute-start | bytes 1572872 | tf_op jit(solution)/shard_map/ppermute | solution.py:306
  161.7 17.7 %collective-permute-start.22 = (bf16[64,4096]{1,0:T(8,128)(2,1)}, bf16[64,4096]{1,0:T(8,128)(2,1)}, u32[]{:S(2)}, u32[]{:S(2)}) collective-permute-start(bf16[64,4096]{1,0:T(8,128)(2,1)} %slice.159), channel_id=1, source_target_pairs={{0,2},{1,3},{2,0},{3,1},{4,6},{5,7},{6,4},{7,5},{8,10},{9,11},{10,... | collective-permute-start | bytes 1572872 | tf_op jit(solution)/shard_map/ppermute | solution.py:306
  162.2 17.2 %collective-permute-start.23 = (bf16[2,256,512]{2,1,0:T(8,128)(2,1)}, bf16[2,256,512]{2,1,0:T(8,128)(2,1)}, u32[]{:S(2)}, u32[]{:S(2)}) collective-permute-start(bf16[2,256,512]{2,1,0:T(8,128)(2,1)} %pad_maximum_fusion.8), channel_id=1, source_target_pairs={{0,24},{1,25},{2,26},{3,27},{4,28},{5,29},{6,30},{7,31},{8,0},{9,1... | collective-permute-start | bytes 1572872 | tf_op jit(solution)/shard_map/ppermute | solution.py:306
  165.8 13.7 %collective-permute-start.25 = (bf16[2,256,512]{2,1,0:T(8,128)(2,1)}, bf16[2,256,512]{2,1,0:T(8,128)(2,1)S(1)}, u32[]{:S(2)}, u32[]{:S(2)}) collective-permute-start(bf16[2,256,512]{2,1,0:T(8,128)(2,1)} %collective-permute-done.19.refs_19_), channel_id=1, source_target_pairs={{0,4},{1,5},{2,6},{3,7},{4,0},{5,1},{6,2},{7,3},{8,12},{9,13},{10,... | collective-permute-start | bytes 1572872 | tf_op jit(solution)/shard_map/ppermute | solution.py:306
  179.4 2.5 %collective-permute-start.26 = (bf16[2,256,512]{2,1,0:T(8,128)(2,1)}, bf16[2,256,512]{2,1,0:T(8,128)(2,1)}, u32[]{:S(2)}, u32[]{:S(2)}) collective-permute-start(bf16[2,256,512]{2,1,0:T(8,128)(2,1)} %collective-permute-done.23.refs_21_), channel_id=1, source_target_pairs={{0,4},{1,5},{2,6},{3,7},{4,0},{5,1},{6,2},{7,3},{8,12},{9,13},{10,... | collective-permute-start | bytes 1572872 | tf_op jit(solution)/shard_map/ppermute | solution.py:306
  194.4 3.6 %collective-permute-start.27 = (f32[1,32]{1,0:T(1,128)S(1)}, f32[1,32]{1,0:T(1,128)S(1)}, u32[]{:S(2)}, u32[]{:S(2)}) collective-permute-start(f32[1,32]{1,0:T(1,128)S(1)} %bitcast.220), channel_id=1, source_target_pairs={{0,1},{1,0},{2,3},{3,2},{4,5},{5,4},{6,7},{7,6},{8,9},{9,8},{10,11... | collective-permute-start | bytes 392 | tf_op jit(solution)/shard_map/ppermute | solution.py:306
  196.0 3.5 %collective-permute-start.28 = (f32[1,32]{1,0:T(1,128)S(1)}, f32[1,32]{1,0:T(1,128)S(1)}, u32[]{:S(2)}, u32[]{:S(2)}) collective-permute-start(f32[1,32]{1,0:T(1,128)S(1)} %bitcast.221), channel_id=1, source_target_pairs={{0,2},{1,3},{2,0},{3,1},{4,6},{5,7},{6,4},{7,5},{8,10},{9,11},{10,... | collective-permute-start | bytes 392 | tf_op jit(solution)/shard_map/ppermute | solution.py:306
  196.5 4.4 %collective-permute-start.29 = (f32[1,32]{1,0:T(1,128)S(1)}, f32[1,32]{1,0:T(1,128)S(1)}, u32[]{:S(2)}, u32[]{:S(2)}) collective-permute-start(f32[1,32]{1,0:T(1,128)S(1)} %bitcast.222), channel_id=1, source_target_pairs={{0,3},{1,2},{2,1},{3,0},{4,7},{5,6},{6,5},{7,4},{8,11},{9,10},{10,... | collective-permute-start | bytes 392 | tf_op jit(solution)/shard_map/ppermute | solution.py:306
  200.9 4.4 %collective-permute-start.30 = (f32[1,32]{1,0:T(1,128)S(1)}, f32[1,32]{1,0:T(1,128)S(1)}, u32[]{:S(2)}, u32[]{:S(2)}) collective-permute-start(f32[1,32]{1,0:T(1,128)S(1)} %add_add_fusion.1), channel_id=1, source_target_pairs={{0,16},{1,17},{2,18},{3,19},{4,20},{5,21},{6,22},{7,23},{8,24},{9,... | collective-permute-start | bytes 392 | tf_op jit(solution)/shard_map/ppermute | solution.py:306
  200.9 5.4 %collective-permute-start.31 = (f32[1,32]{1,0:T(1,128)S(1)}, f32[1,32]{1,0:T(1,128)S(1)}, u32[]{:S(2)}, u32[]{:S(2)}) collective-permute-start(f32[1,32]{1,0:T(1,128)S(1)} %add_add_fusion.1), channel_id=1, source_target_pairs={{0,8},{1,9},{2,10},{3,11},{4,12},{5,13},{6,14},{7,15},{8,16},{9,17... | collective-permute-start | bytes 392 | tf_op jit(solution)/shard_map/ppermute | solution.py:306
  203.4 3.5 %collective-permute-start.32 = (f32[1,32]{1,0:T(1,128)S(1)}, f32[1,32]{1,0:T(1,128)S(1)}, u32[]{:S(2)}, u32[]{:S(2)}) collective-permute-start(f32[1,32]{1,0:T(1,128)S(1)} %add_add_fusion.1), channel_id=1, source_target_pairs={{0,24},{1,25},{2,26},{3,27},{4,28},{5,29},{6,30},{7,31},{8,0},{9,1... | collective-permute-start | bytes 392 | tf_op jit(solution)/shard_map/ppermute | solution.py:306
  207.0 1.1 collective-permute-start.33
  (15 other events, 76.0 us)

commit v5 on v4

--- a/solution.py
+++ b/solution.py
@@ -11,7 +11,6 @@
 learn_rate = 0.0016
 AXES = ("pop", "mp")
 CORES = 2
-FIRST_STAGES, NEXT_STAGES = 2, 1
 SPARE_BYTES = 4 * 1024 * 1024
 
 
@@ -147,12 +146,12 @@
             copy.start()
         del queue[:count]
 
-    start_stages(FIRST_STAGES)
+    start_stages(2 if read_out else 1)
     done_rows, out_copies = 0, []
     for g, (_, first, base, own_vectors) in enumerate(plan):
         for copy in stages[g]:
             copy.wait()
-        start_stages(NEXT_STAGES)
+        start_stages(1 if read_out else 2)
         count = rows[g].shape[0]
         values = [
             jnp.dot(rows[g][...], weights[part, first * plane_rows :], preferred_element_type=jnp.float32)
@@ -227,6 +226,7 @@
     far = [pltpu.with_memory_space_constraint(a, pltpu.HBM) for a in [*arrays, *base_arrays]]
     near = [chunk for _, _, _, chunk in chunks]
     near[::2] = [pltpu.with_memory_space_constraint(a, pltpu.HBM) for a in near[::2]]
+    near[-1] = pltpu.with_memory_space_constraint(near[-1], pltpu.VMEM)
     given = [*far[: len(arrays)], *near, *far[len(arrays) :]]
     extra = [*ranks, *vectors, *read_out]
     held = sum(2 * math.prod(b.shape) for b in buffers) + 4 * total * columns

time: 210 us -> 210 us (level)
  no operation moved by 1% of the time
where the time goes in v5:
time: 210 us; the launch traced here: 209 us
  waiting for transfers between devices  79.1 us (38%)
  starting transfers between devices  42.2 us (20%)
  Pallas kernels  36.6 us (17%)
  matrix products  20.1 us (10%)
  other arithmetic  16.8 us (8%)
  local copies, waits for them, and re-layouts  12.4 us (6%)
    ppermute x34, waiting for transfers between devices, send(): return lax.ppermute(value, AXES, pairs(move, keep))  79.1 us
    ppermute x34, starting transfers between devices, send(): return lax.ppermute(value, AXES, pairs(move, keep))  42.2 us
    pallas_call x3, Pallas kernels, product(): pl.pallas_call(lambda *refs: product_kernel(plan, counts, plane_of, seq,...  35.9 us
    dot_general x12, matrix products, on_vector(): lax.dot_general(rows, vector, (((1,), (1,)), ((), ())), preferred_element...  16.7 us
    slice x6, local copies, waits for them, and re-layouts, next_sends(): to_x, to_y, here = ([new_y[:half]], [new_x[half:seq]], None)  5.97 us
  transfers between devices with their start and end apart: 34, of which 20 were waited for; matrix products, arithmetic and copies ran while one was open for 21% of the time, Pallas kernels for 11%

profile of v5, /device:TPU:0, one launch (start us, length us, event | category | flops | bytes accessed | tf_op | source)
XLA Modules:
  0.0 208.9 jit_solution(6310419316683357863)
XLA Ops:
  0.7 1.3 dynamic-slice_bitcast_fusion
  2.0 3.1 %collective-permute-start = (s32[3,4]{1,0:T(4,128)S(1)}, s32[3,4]{1,0:T(4,128)S(1)}, u32[]{:S(2)}, u32[]{:S(2)}) collective-permute-start(s32[3,4]{1,0:T(4,128)S(1)} %pad_add_fusion.1), channel_id=1, source_target_pairs={{0,8},{1,9},{2,10},{3,11},{4,12},{5,13},{6,14},{7,15},{8,16},{9,17... | collective-permute-start | bytes 152 | tf_op jit(solution)/shard_map/ppermute | solution.py:306
  5.1 2.6 %collective-permute-start.1 = (s32[3,4]{1,0:T(4,128)S(1)}, s32[3,4]{1,0:T(4,128)S(1)}, u32[]{:S(2)}, u32[]{:S(2)}) collective-permute-start(s32[3,4]{1,0:T(4,128)S(1)} %pad_add_fusion.1), channel_id=1, source_target_pairs={{0,16},{1,17},{2,18},{3,19},{4,20},{5,21},{6,22},{7,23},{8,24},{9,... | collective-permute-start | bytes 152 | tf_op jit(solution)/shard_map/ppermute | solution.py:306
  7.7 1.3 collective-permute-start.2
  9.0 3.6 %collective-permute-start.4 = (bf16[128,4096]{1,0:T(8,128)(2,1)S(1)}, bf16[128,4096]{1,0:T(8,128)(2,1)}, u32[]{:S(2)}, u32[]{:S(2)}) collective-permute-start(bf16[128,4096]{1,0:T(8,128)(2,1)S(1)} %dynamic-slice_bitcast_fusion), channel_id=1, source_target_pairs={{0,8},{1,9},{2,10},{3,11},{4,12},{5,13},{6,14},{7,15},{8,16},{9,17... | collective-permute-start | bytes 3145736 | tf_op jit(solution)/shard_map/ppermute | solution.py:306
  12.6 1.3 collective-permute-start.5
  15.5 2.7 %fusion.130 = (bf16[4,1,4096]{2,1,0:T(2,128)(2,1)S(1)}, bf16[4,1,4096]{2,1,0:T(2,128)(2,1)S(1)}, bf16[4,1,4096]{2,1,0:T(2,128)(2,1)}, bf16[4,1,4096]{2,1,0:T(2,1...) fusion(s32[4096]{0:T(1024)S(1)} %iota_multiply_fusion, ...), kind=kLoop, calls=%fused_computation.194 | loop fusion | flops 1966080 | bytes 278656 | tf_op jit(solution)/shard_map/convert_element_type | solution.py:390
  18.2 1.6 convolution_bitcast_fusion
  19.9 1.6 convolution_bitcast_fusion.1
  21.5 2.2 %convolution_bitcast_fusion.2 = f32[128,2]{0,1:T(2,128)} fusion(bf16[4,128,4096]{2,1,0:T(8,128)(2,1)} %param.7, bf16[4,1,4096]{2,1,0:T(2,128)(2,1)S(1)} %get-tuple-element.181, bf16[4,1,4096]{2,1,0:T(2,128)(2,1)S(1)} %get-tuple-element.180), kind=kOutput, calls=%fused_computation.12 | convolution fusion | flops 2129920 | bytes 1115136 | tf_op jit(solution)/shard_map/dot_general | solution.py:395
  23.7 2.2 %convolution_bitcast_fusion.3 = f32[128,2]{0,1:T(2,128)} fusion(bf16[4,128,4096]{2,1,0:T(8,128)(2,1)} %param.7, bf16[4,1,4096]{2,1,0:T(2,128)(2,1)S(1)} %get-tuple-element.181, bf16[4,1,4096]{2,1,0:T(2,128)(2,1)S(1)} %get-tuple-element.180), kind=kOutput, calls=%fused_computation.13 | convolution fusion | flops 2129920 | bytes 1115136 | tf_op jit(solution)/shard_map/dot_general | solution.py:395
  28.5 2.6 %add_convert_fusion = bf16[512,2048]{1,0:T(8,128)(2,1)S(1)} fusion(bf16[512,2048]{1,0:T(8,128)(2,1)} %param.9, s32[32]{0:T(128)S(1)} %get-tuple-element.214, s32[2048]{0:T(1024)S(1)} %add_multiply_fusion, s32[32]{0:T(128)S(1)} %get-tuple-element.213, f32[32]{0:T(128)S(1)} %reshape.1829, s32[512]{0:T(512)S(1)} %add_multiply_fusion.2), kind=kOutput, calls=%fused_computation | convolution fusion | flops 72531968 | bytes 4204928 | tf_op jit(solution)/shard_map/dot_general | solution.py:47
  33.2 5.2 %collective-permute-done.5 = bf16[128,4096]{1,0:T(8,128)(2,1)} collective-permute-done((bf16[128,4096]{1,0:T(8,128)(2,1)S(1)}, bf16[128,4096]{1,0:T(8,128)(2,1)}, u32[]{:S(2)}, u32[]{:S(2)}) %collective-permute-start.5) | collective-permute-done | bytes 1048608 | tf_op jit(solution)/shard_map/ppermute | solution.py:306
  38.4 1.3 broadcast_select_fusion.refs_2_
  39.7 1.6 collective-permute-start.8
  41.3 1.5 collective-permute-start.9
  42.8 1.6 collective-permute-start.6
  44.4 1.3 collective-permute-start.7
  50.0 12.6 %collective-permute-done.8.refs_3_ = bf16[128,4096]{1,0:T(8,128)(2,1)S(1)} collective-permute-done((bf16[128,4096]{1,0:T(8,128)(2,1)S(1)}, bf16[128,4096]{1,0:T(8,128)(2,1)S(1)}, u32[]{:S(2)}, u32[]{:S(2)}) %collective-permute-start.8) | collective-permute-done | bytes 1048608 | tf_op jit(solution)/shard_map/ppermute | solution.py:306
  63.9 5.1 %collective-permute-done.7 = bf16[128,4096]{1,0:T(8,128)(2,1)} collective-permute-done((bf16[128,4096]{1,0:T(8,128)(2,1)}, bf16[128,4096]{1,0:T(8,128)(2,1)}, u32[]{:S(2)}, u32[]{:S(2)}) %collective-permute-start.7) | collective-permute-done | bytes 1048608 | tf_op jit(solution)/shard_map/ppermute | solution.py:306
  69.0 1.4 select_select_fusion.1.refs_7_
  70.4 2.0 pad_maximum_fusion
  74.2 1.3 collective-permute-start.12
  76.5 23.6 %collective-permute-done.12 = bf16[128,4096]{1,0:T(8,128)(2,1)} collective-permute-done((bf16[128,4096]{1,0:T(8,128)(2,1)}, bf16[128,4096]{1,0:T(8,128)(2,1)}, u32[]{:S(2)}, u32[]{:S(2)}) %collective-permute-start.12) | collective-permute-done | bytes 1048608 | tf_op jit(solution)/shard_map/ppermute | solution.py:306
  100.0 5.3 %collective-permute-done.13.refs_5_ = bf16[192,4096]{1,0:T(8,128)(2,1)} collective-permute-done((bf16[192,4096]{1,0:T(8,128)(2,1)}, bf16[192,4096]{1,0:T(8,128)(2,1)}, u32[]{:S(2)}, u32[]{:S(2)}) %collective-permute-start.13) | collective-permute-done | bytes 1572896 | tf_op jit(solution)/shard_map/ppermute | solution.py:306
  105.6 1.4 select_select_fusion.refs_10_
  112.2 2.0 pad_maximum_fusion.2
  114.1 6.1 %collective-permute-done.15.refs_10_.refs_13_.refs_15_ = bf16[2,512,512]{2,1,0:T(8,128)(2,1)} collective-permute-done((bf16[2,512,512]{2,1,0:T(8,128)(2,1)}, bf16[2,512,512]{2,1,0:T(8,128)(2,1)}, u32[]{:S(2)}, u32[]{:S(2)}) %collective-permute-start.15) | collective-permute-done | bytes 1048608 | tf_op jit(solution)/shard_map/ppermute | solution.py:306
  120.2 1.5 collective-permute-start.16
  121.7 1.5 collective-permute-start.17
  123.9 4.0 %collective-permute-start.19 = (bf16[2,256,512]{2,1,0:T(8,128)(2,1)}, bf16[2,256,512]{2,1,0:T(8,128)(2,1)}, u32[]{:S(2)}, u32[]{:S(2)}) collective-permute-start(bf16[2,256,512]{2,1,0:T(8,128)(2,1)} %pad_maximum_fusion.7), channel_id=1, source_target_pairs={{0,24},{1,25},{2,26},{3,27},{4,28},{5,29},{6,30},{7,31},{8,0},{9,1... | collective-permute-start | bytes 1572872 | tf_op jit(solution)/shard_map/ppermute | solution.py:306
  129.1 1.3 fusion.19
  130.4 1.6 fusion.7
  132.1 1.6 fusion.9
  135.4 10.4 %shard_map.94.refs_17_ = bf16[1408,1024]{1,0:T(8,128)(2,1)} custom-call(s32[8]{0:T(128)S(1)} %stack.218.refs_0_, bf16[512,4096]{1,0:T(8,128)(2,1)} %bitcast.202, bf16[128,4096]{1,0:T(8,128)(2,1)} %copy-done.2, bf16[128,4096]{1,0:T(8,128)(2,1)} %copy-done.4, bf16[128,4096]{1,0:T(8,128)(2,1)} %copy-done.6, bf16[192,4096]{1,0:T(8,128)(2,1)} %collective-permute-done.13.refs_5_, ...), custom_call_target="tpu_custom_call" | custom-call | flops 1 | bytes 1 | tf_op jit(solution)/shard_map/pallas_call | solution.py:240
  145.8 8.2 %collective-permute-done.16.refs_8_ = bf16[192,4096]{1,0:T(8,128)(2,1)} collective-permute-done((bf16[192,4096]{1,0:T(8,128)(2,1)}, bf16[192,4096]{1,0:T(8,128)(2,1)}, u32[]{:S(2)}, u32[]{:S(2)}) %collective-permute-start.16) | collective-permute-done | bytes 1572896 | tf_op jit(solution)/shard_map/ppermute | solution.py:306
  155.3 1.9 slice.158
  157.1 1.9 slice.159
  159.0 2.1 %collective-permute-done.19.refs_19_ = bf16[2,256,512]{2,1,0:T(8,128)(2,1)} collective-permute-done((bf16[2,256,512]{2,1,0:T(8,128)(2,1)}, bf16[2,256,512]{2,1,0:T(8,128)(2,1)}, u32[]{:S(2)}, u32[]{:S(2)}) %collective-permute-start.19) | collective-permute-done | bytes 524320 | tf_op jit(solution)/shard_map/ppermute | solution.py:306
  162.2 3.6 %collective-permute-start.23 = (bf16[2,256,512]{2,1,0:T(8,128)(2,1)}, bf16[2,256,512]{2,1,0:T(8,128)(2,1)}, u32[]{:S(2)}, u32[]{:S(2)}) collective-permute-start(bf16[2,256,512]{2,1,0:T(8,128)(2,1)} %pad_maximum_fusion.8), channel_id=1, source_target_pairs={{0,24},{1,25},{2,26},{3,27},{4,28},{5,29},{6,30},{7,31},{8,0},{9,1... | collective-permute-start | bytes 1572872 | tf_op jit(solution)/shard_map/ppermute | solution.py:306
  165.9 13.2 %shard_map.95.refs_23_ = bf16[1920,1024]{1,0:T(8,128)(2,1)} custom-call(s32[12]{0:T(128)S(1)} %stack.219.refs_0_, bf16[512,4096]{1,0:T(8,128)(2,1)} %bitcast.203, bf16[128,4096]{1,0:T(8,128)(2,1)} %copy-done.2, bf16[128,4096]{1,0:T(8,128)(2,1)} %copy-done.4, bf16[128,4096]{1,0:T(8,128)(2,1)} %copy-done.6, bf16[192,4096]{1,0:T(8,128)(2,1)} %collective-permute-done.13.refs_5_, ...), custom_call_target="tpu_custom_call" | custom-call | flops 1 | bytes 1 | tf_op jit(solution)/shard_map/pallas_call | solution.py:240
  180.0 1.6 collective-permute-done.26.refs_22_
  181.6 12.2 %shard_map.96 = f32[16,8,512]{2,1,0:T(8,128)S(1)} custom-call(s32[20]{0:T(128)S(1)} %stack.194.refs_0_, bf16[512,4096]{1,0:T(8,128)(2,1)} %bitcast.204, bf16[128,4096]{1,0:T(8,128)(2,1)} %copy-done.2, bf16[128,4096]{1,0:T(8,128)(2,1)} %copy-done.4, bf16[128,4096]{1,0:T(8,128)(2,1)} %copy-done.6, bf16[192,4096]{1,0:T(8,128)(2,1)} %collective-permute-done.13.refs_5_, ...), custom_call_target="tpu_custom_call" | custom-call | flops 1 | bytes 1 | tf_op jit(solution)/shard_map/pallas_call | solution.py:240
  194.1 1.6 collective-permute-start.27
  196.2 1.5 collective-permute-start.29
  197.8 1.5 collective-permute-done.28
  199.2 1.4 collective-permute-done.29
  200.7 2.7 %collective-permute-start.31 = (f32[1,32]{1,0:T(1,128)S(1)}, f32[1,32]{1,0:T(1,128)S(1)}, u32[]{:S(2)}, u32[]{:S(2)}) collective-permute-start(f32[1,32]{1,0:T(1,128)S(1)} %add_add_fusion.1), channel_id=1, source_target_pairs={{0,8},{1,9},{2,10},{3,11},{4,12},{5,13},{6,14},{7,15},{8,16},{9,17... | collective-permute-start | bytes 392 | tf_op jit(solution)/shard_map/ppermute | solution.py:306
  (166 shorter events, 32.5 us)
Async XLA Ops:
  2.0 13.1 %collective-permute-start = (s32[3,4]{1,0:T(4,128)S(1)}, s32[3,4]{1,0:T(4,128)S(1)}, u32[]{:S(2)}, u32[]{:S(2)}) collective-permute-start(s32[3,4]{1,0:T(4,128)S(1)} %pad_add_fusion.1), channel_id=1, source_target_pairs={{0,8},{1,9},{2,10},{3,11},{4,12},{5,13},{6,14},{7,15},{8,16},{9,17... | collective-permute-start | bytes 152 | tf_op jit(solution)/shard_map/ppermute | solution.py:306
  5.1 10.0 %collective-permute-start.1 = (s32[3,4]{1,0:T(4,128)S(1)}, s32[3,4]{1,0:T(4,128)S(1)}, u32[]{:S(2)}, u32[]{:S(2)}) collective-permute-start(s32[3,4]{1,0:T(4,128)S(1)} %pad_add_fusion.1), channel_id=1, source_target_pairs={{0,16},{1,17},{2,18},{3,19},{4,20},{5,21},{6,22},{7,23},{8,24},{9,... | collective-permute-start | bytes 152 | tf_op jit(solution)/shard_map/ppermute | solution.py:306
  7.7 7.4 %collective-permute-start.2 = (s32[3,4]{1,0:T(4,128)S(1)}, s32[3,4]{1,0:T(4,128)S(1)}, u32[]{:S(2)}, u32[]{:S(2)}) collective-permute-start(s32[3,4]{1,0:T(4,128)S(1)} %pad_add_fusion.1), channel_id=1, source_target_pairs={{0,24},{1,25},{2,26},{3,27},{4,28},{5,29},{6,30},{7,31},{8,0},{9,1... | collective-permute-start | bytes 152 | tf_op jit(solution)/shard_map/ppermute | solution.py:306
  9.0 24.1 %collective-permute-start.4 = (bf16[128,4096]{1,0:T(8,128)(2,1)S(1)}, bf16[128,4096]{1,0:T(8,128)(2,1)}, u32[]{:S(2)}, u32[]{:S(2)}) collective-permute-start(bf16[128,4096]{1,0:T(8,128)(2,1)S(1)} %dynamic-slice_bitcast_fusion), channel_id=1, source_target_pairs={{0,8},{1,9},{2,10},{3,11},{4,12},{5,13},{6,14},{7,15},{8,16},{9,17... | collective-permute-start | bytes 3145736 | tf_op jit(solution)/shard_map/ppermute | solution.py:306
  12.6 25.8 %collective-permute-start.5 = (bf16[128,4096]{1,0:T(8,128)(2,1)S(1)}, bf16[128,4096]{1,0:T(8,128)(2,1)}, u32[]{:S(2)}, u32[]{:S(2)}) collective-permute-start(bf16[128,4096]{1,0:T(8,128)(2,1)S(1)} %dynamic-slice_bitcast_fusion), channel_id=1, source_target_pairs={{8,0},{9,1},{10,2},{11,3},{12,4},{13,5},{14,6},{15,7},{16,8},{17,9... | collective-permute-start | bytes 3145736 | tf_op jit(solution)/shard_map/ppermute | solution.py:306
  26.0 1.8 collective-permute-start.3
  31.1 14.9 %copy-start.10 = (bf16[512,2048]{1,0:T(8,128)(2,1)}, bf16[512,2048]{1,0:T(8,128)(2,1)S(1)}, u32[]{:S(2)}) copy-start(bf16[512,2048]{1,0:T(8,128)(2,1)S(1)} %add_convert_fusion) | copy-start | bytes 6291460
  32.0 14.0 %copy-start.11 = (bf16[512,2048]{1,0:T(8,128)(2,1)}, bf16[512,2048]{1,0:T(8,128)(2,1)S(1)}, u32[]{:S(2)}) copy-start(bf16[512,2048]{1,0:T(8,128)(2,1)S(1)} %add_convert_fusion.1) | copy-start | bytes 6291460
  32.5 13.7 %copy-start.8 = (bf16[2,512,512]{2,1,0:T(8,128)(2,1)}, bf16[2,512,512]{2,1,0:T(8,128)(2,1)S(1)}, u32[]{:S(2)}) copy-start(bf16[2,512,512]{2,1,0:T(8,128)(2,1)S(1)} %pad_maximum_fusion.4.refs_8_.refs_11_.refs_13_) | copy-start | bytes 3145732
  32.5 13.3 %copy-start.16 = (bf16[4,1,4096]{2,1,0:T(2,128)(2,1)S(1)}, bf16[4,1,4096]{2,1,0:T(2,128)(2,1)}, u32[]{:S(2)}) copy-start(bf16[4,1,4096]{2,1,0:T(2,128)(2,1)} %get-tuple-element.178) | copy-start | bytes 98308
  32.5 13.3 %copy-start.17 = (bf16[4,1,4096]{2,1,0:T(2,128)(2,1)S(1)}, bf16[4,1,4096]{2,1,0:T(2,128)(2,1)}, u32[]{:S(2)}) copy-start(bf16[4,1,4096]{2,1,0:T(2,128)(2,1)} %get-tuple-element.179) | copy-start | bytes 98308
  32.5 13.3 %copy-start.19 = (bf16[1,2,4096]{2,1,0:T(2,128)(2,1)S(1)}, bf16[1,2,4096]{2,1,0:T(2,128)(2,1)}, u32[]{:S(2)}) copy-start(bf16[1,2,4096]{2,1,0:T(2,128)(2,1)} %slice_maximum_fusion) | copy-start | bytes 49156
  32.5 17.5 %collective-permute-start.10 = (bf16[2,512,512]{2,1,0:T(8,128)(2,1)S(1)}, bf16[2,512,512]{2,1,0:T(8,128)(2,1)S(1)}, u32[]{:S(2)}, u32[]{:S(2)}) collective-permute-start(bf16[2,512,512]{2,1,0:T(8,128)(2,1)S(1)} %pad_maximum_fusion.4.refs_8_.refs_11_.refs_13_), channel_id=1, source_target_pairs={{0,4},{1,5},{2,6},{3,7},{4,0},{5,1},{6,2},{7,3},{8,12},{9,13},{10,... | collective-permute-start | bytes 3145736 | tf_op jit(solution)/shard_map/ppermute | solution.py:306
  39.7 22.9 %collective-permute-start.8 = (bf16[128,4096]{1,0:T(8,128)(2,1)S(1)}, bf16[128,4096]{1,0:T(8,128)(2,1)S(1)}, u32[]{:S(2)}, u32[]{:S(2)}) collective-permute-start(bf16[128,4096]{1,0:T(8,128)(2,1)S(1)} %broadcast_select_fusion.refs_2_), channel_id=1, source_target_pairs={{0,1},{1,0},{2,3},{3,2},{4,5},{5,4},{6,7},{7,6},{8,9},{9,8},{10,11... | collective-permute-start | bytes 3145736 | tf_op jit(solution)/shard_map/ppermute | solution.py:306
  41.3 22.6 %collective-permute-start.9 = (bf16[128,4096]{1,0:T(8,128)(2,1)S(1)}, bf16[128,4096]{1,0:T(8,128)(2,1)S(1)}, u32[]{:S(2)}, u32[]{:S(2)}) collective-permute-start(bf16[128,4096]{1,0:T(8,128)(2,1)S(1)} %broadcast_select_fusion.refs_2_), channel_id=1, source_target_pairs={{0,2},{1,3},{2,0},{3,1},{4,6},{5,7},{6,4},{7,5},{8,10},{9,11},{10,... | collective-permute-start | bytes 3145736 | tf_op jit(solution)/shard_map/ppermute | solution.py:306
  42.8 21.1 %collective-permute-start.6 = (bf16[128,4096]{1,0:T(8,128)(2,1)}, bf16[128,4096]{1,0:T(8,128)(2,1)}, u32[]{:S(2)}, u32[]{:S(2)}) collective-permute-start(bf16[128,4096]{1,0:T(8,128)(2,1)} %collective-permute-done.4), channel_id=1, source_target_pairs={{8,16},{9,17},{10,18},{11,19},{12,20},{13,21},{14,22},{15,23},{16,... | collective-permute-start | bytes 3145736 | tf_op jit(solution)/shard_map/ppermute | solution.py:306
  44.4 24.5 %collective-permute-start.7 = (bf16[128,4096]{1,0:T(8,128)(2,1)}, bf16[128,4096]{1,0:T(8,128)(2,1)}, u32[]{:S(2)}, u32[]{:S(2)}) collective-permute-start(bf16[128,4096]{1,0:T(8,128)(2,1)} %collective-permute-done.5), channel_id=1, source_target_pairs={{8,0},{9,1},{10,2},{11,3},{12,4},{13,5},{14,6},{15,7},{16,8},{17,9... | collective-permute-start | bytes 3145736 | tf_op jit(solution)/shard_map/ppermute | solution.py:306
  72.4 32.9 %collective-permute-start.13 = (bf16[192,4096]{1,0:T(8,128)(2,1)}, bf16[192,4096]{1,0:T(8,128)(2,1)}, u32[]{:S(2)}, u32[]{:S(2)}) collective-permute-start(bf16[192,4096]{1,0:T(8,128)(2,1)} %get-tuple-element.175), channel_id=1, source_target_pairs={{0,1},{1,0},{2,3},{3,2},{4,5},{5,4},{6,7},{7,6},{8,9},{9,8},{10,11... | collective-permute-start | bytes 4718600 | tf_op jit(solution)/shard_map/ppermute | solution.py:306
  73.0 32.6 %collective-permute-start.14 = (bf16[192,4096]{1,0:T(8,128)(2,1)}, bf16[192,4096]{1,0:T(8,128)(2,1)}, u32[]{:S(2)}, u32[]{:S(2)}) collective-permute-start(bf16[192,4096]{1,0:T(8,128)(2,1)} %get-tuple-element.174), channel_id=1, source_target_pairs={{0,2},{1,3},{2,0},{3,1},{4,6},{5,7},{6,4},{7,5},{8,10},{9,11},{10,... | collective-permute-start | bytes 4718600 | tf_op jit(solution)/shard_map/ppermute | solution.py:306
  73.5 3.0 %collective-permute-start.11 = (bf16[128,4096]{1,0:T(8,128)(2,1)}, bf16[128,4096]{1,0:T(8,128)(2,1)S(1)}, u32[]{:S(2)}, u32[]{:S(2)}) collective-permute-start(bf16[128,4096]{1,0:T(8,128)(2,1)} %collective-permute-done.6), channel_id=1, source_target_pairs={{16,24},{17,25},{18,26},{19,27},{20,28},{21,29},{22,30},{23,31}} | collective-permute-start | bytes 3145736 | tf_op jit(solution)/shard_map/ppermute | solution.py:306
  74.2 25.8 %collective-permute-start.12 = (bf16[128,4096]{1,0:T(8,128)(2,1)}, bf16[128,4096]{1,0:T(8,128)(2,1)}, u32[]{:S(2)}, u32[]{:S(2)}) collective-permute-start(bf16[128,4096]{1,0:T(8,128)(2,1)} %collective-permute-done.7), channel_id=1, source_target_pairs={{8,0},{9,1},{10,2},{11,3},{12,4},{13,5},{14,6},{15,7}} | collective-permute-start | bytes 3145736 | tf_op jit(solution)/shard_map/ppermute | solution.py:306
  75.6 31.4 %copy-start.7 = (bf16[128,4096]{1,0:T(8,128)(2,1)S(1)}, bf16[128,4096]{1,0:T(8,128)(2,1)}, u32[]{:S(2)}) copy-start(bf16[128,4096]{1,0:T(8,128)(2,1)} %copy-done.6) | copy-start | bytes 3145732
  75.6 44.6 %collective-permute-start.15 = (bf16[2,512,512]{2,1,0:T(8,128)(2,1)}, bf16[2,512,512]{2,1,0:T(8,128)(2,1)}, u32[]{:S(2)}, u32[]{:S(2)}) collective-permute-start(bf16[2,512,512]{2,1,0:T(8,128)(2,1)} %pad_maximum_fusion.6), channel_id=1, source_target_pairs={{0,16},{1,17},{2,18},{3,19},{4,20},{5,21},{6,22},{7,23},{8,24},{9,... | collective-permute-start | bytes 3145736 | tf_op jit(solution)/shard_map/ppermute | solution.py:306
  112.1 11.3 %copy-start.1 = (bf16[128,4096]{1,0:T(8,128)(2,1)S(1)}, bf16[128,4096]{1,0:T(8,128)(2,1)}, u32[]{:S(2)}) copy-start(bf16[128,4096]{1,0:T(8,128)(2,1)} %copy-done) | copy-start | bytes 3145732
  112.1 11.3 %copy-start.13 = (bf16[4,1,4096]{2,1,0:T(2,128)(2,1)S(1)}, bf16[4,1,4096]{2,1,0:T(2,128)(2,1)}, u32[]{:S(2)}) copy-start(bf16[4,1,4096]{2,1,0:T(2,128)(2,1)} %copy-done.12) | copy-start | bytes 98308
  112.1 11.3 %copy-start.15 = (bf16[4,1,4096]{2,1,0:T(2,128)(2,1)S(1)}, bf16[4,1,4096]{2,1,0:T(2,128)(2,1)}, u32[]{:S(2)}) copy-start(bf16[4,1,4096]{2,1,0:T(2,128)(2,1)} %copy-done.14) | copy-start | bytes 98308
  120.2 33.8 %collective-permute-start.16 = (bf16[192,4096]{1,0:T(8,128)(2,1)}, bf16[192,4096]{1,0:T(8,128)(2,1)}, u32[]{:S(2)}, u32[]{:S(2)}) collective-permute-start(bf16[192,4096]{1,0:T(8,128)(2,1)} %get-tuple-element.113), channel_id=1, source_target_pairs={{0,1},{1,0},{2,3},{3,2},{4,5},{5,4},{6,7},{7,6},{8,9},{9,8},{10,11... | collective-permute-start | bytes 4718600 | tf_op jit(solution)/shard_map/ppermute | solution.py:306
  121.7 33.6 %collective-permute-start.17 = (bf16[192,4096]{1,0:T(8,128)(2,1)}, bf16[192,4096]{1,0:T(8,128)(2,1)}, u32[]{:S(2)}, u32[]{:S(2)}) collective-permute-start(bf16[192,4096]{1,0:T(8,128)(2,1)} %get-tuple-element.114), channel_id=1, source_target_pairs={{0,2},{1,3},{2,0},{3,1},{4,6},{5,7},{6,4},{7,5},{8,10},{9,11},{10,... | collective-permute-start | bytes 4718600 | tf_op jit(solution)/shard_map/ppermute | solution.py:306
  123.3 12.1 %collective-permute-start.20 = (bf16[2,512,512]{2,1,0:T(8,128)(2,1)}, bf16[2,512,512]{2,1,0:T(8,128)(2,1)S(1)}, u32[]{:S(2)}, u32[]{:S(2)}) collective-permute-start(bf16[2,512,512]{2,1,0:T(8,128)(2,1)} %collective-permute-done.15.refs_10_.refs_13_.refs_15_), channel_id=1, source_target_pairs={{0,4},{1,5},{2,6},{3,7},{4,0},{5,1},{6,2},{7,3},{8,12},{9,13},{10,... | collective-permute-start | bytes 3145736 | tf_op jit(solution)/shard_map/ppermute | solution.py:306
  123.3 37.8 %collective-permute-start.18 = (bf16[2,512,512]{2,1,0:T(8,128)(2,1)}, bf16[2,512,512]{2,1,0:T(8,128)(2,1)}, u32[]{:S(2)}, u32[]{:S(2)}) collective-permute-start(bf16[2,512,512]{2,1,0:T(8,128)(2,1)} %pad_maximum_fusion.5), channel_id=1, source_target_pairs={{0,8},{1,9},{2,10},{3,11},{4,12},{5,13},{6,14},{7,15},{8,16},{9,17... | collective-permute-start | bytes 3145736 | tf_op jit(solution)/shard_map/ppermute | solution.py:306
  123.8 9.9 %copy-start.22 = (f32[128,2]{0,1:T(2,128)S(1)}, f32[128,2]{0,1:T(2,128)}, u32[]{:S(2)}) copy-start(f32[128,2]{0,1:T(2,128)} %fusion.171) | copy-start | bytes 3076
  123.8 9.9 %copy-start.23 = (f32[128,2]{0,1:T(2,128)S(1)}, f32[128,2]{0,1:T(2,128)}, u32[]{:S(2)}) copy-start(f32[128,2]{0,1:T(2,128)} %fusion.174) | copy-start | bytes 3076
  123.8 9.9 %copy-start.24 = (f32[128,2]{0,1:T(2,128)S(1)}, f32[128,2]{0,1:T(2,128)}, u32[]{:S(2)}) copy-start(f32[128,2]{0,1:T(2,128)} %fusion.177) | copy-start | bytes 3076
  123.9 37.3 %collective-permute-start.19 = (bf16[2,256,512]{2,1,0:T(8,128)(2,1)}, bf16[2,256,512]{2,1,0:T(8,128)(2,1)}, u32[]{:S(2)}, u32[]{:S(2)}) collective-permute-start(bf16[2,256,512]{2,1,0:T(8,128)(2,1)} %pad_maximum_fusion.7), channel_id=1, source_target_pairs={{0,24},{1,25},{2,26},{3,27},{4,28},{5,29},{6,30},{7,31},{8,0},{9,1... | collective-permute-start | bytes 1572872 | tf_op jit(solution)/shard_map/ppermute | solution.py:306
  145.8 20.0 %copy-start.18 = (f32[2,5,512]{2,0,1:T(2,128)S(1)}, f32[2,5,512]{2,0,1:T(2,128)}, u32[]{:S(2)}) copy-start(f32[2,5,512]{2,0,1:T(2,128)} %copy.82) | copy-start | bytes 61444
  161.1 4.8 %collective-permute-start.24 = (bf16[2,512,512]{2,1,0:T(8,128)(2,1)}, bf16[2,512,512]{2,1,0:T(8,128)(2,1)}, u32[]{:S(2)}, u32[]{:S(2)}) collective-permute-start(bf16[2,512,512]{2,1,0:T(8,128)(2,1)} %collective-permute-done.18.refs_15_.refs_17_), channel_id=1, source_target_pairs={{0,4},{1,5},{2,6},{3,7},{4,0},{5,1},{6,2},{7,3},{8,12},{9,13},{10,... | collective-permute-start | bytes 3145736 | tf_op jit(solution)/shard_map/ppermute | solution.py:306
  161.1 18.0 %collective-permute-start.21 = (bf16[64,4096]{1,0:T(8,128)(2,1)}, bf16[64,4096]{1,0:T(8,128)(2,1)}, u32[]{:S(2)}, u32[]{:S(2)}) collective-permute-start(bf16[64,4096]{1,0:T(8,128)(2,1)} %slice.158), channel_id=1, source_target_pairs={{0,1},{1,0},{2,3},{3,2},{4,5},{5,4},{6,7},{7,6},{8,9},{9,8},{10,11... | collective-permute-start | bytes 1572872 | tf_op jit(solution)/shard_map/ppermute | solution.py:306
  161.7 17.5 %collective-permute-start.22 = (bf16[64,4096]{1,0:T(8,128)(2,1)}, bf16[64,4096]{1,0:T(8,128)(2,1)}, u32[]{:S(2)}, u32[]{:S(2)}) collective-permute-start(bf16[64,4096]{1,0:T(8,128)(2,1)} %slice.159), channel_id=1, source_target_pairs={{0,2},{1,3},{2,0},{3,1},{4,6},{5,7},{6,4},{7,5},{8,10},{9,11},{10,... | collective-permute-start | bytes 1572872 | tf_op jit(solution)/shard_map/ppermute | solution.py:306
  162.2 17.0 %collective-permute-start.23 = (bf16[2,256,512]{2,1,0:T(8,128)(2,1)}, bf16[2,256,512]{2,1,0:T(8,128)(2,1)}, u32[]{:S(2)}, u32[]{:S(2)}) collective-permute-start(bf16[2,256,512]{2,1,0:T(8,128)(2,1)} %pad_maximum_fusion.8), channel_id=1, source_target_pairs={{0,24},{1,25},{2,26},{3,27},{4,28},{5,29},{6,30},{7,31},{8,0},{9,1... | collective-permute-start | bytes 1572872 | tf_op jit(solution)/shard_map/ppermute | solution.py:306
  165.8 13.4 %collective-permute-start.25 = (bf16[2,256,512]{2,1,0:T(8,128)(2,1)}, bf16[2,256,512]{2,1,0:T(8,128)(2,1)S(1)}, u32[]{:S(2)}, u32[]{:S(2)}) collective-permute-start(bf16[2,256,512]{2,1,0:T(8,128)(2,1)} %collective-permute-done.19.refs_19_), channel_id=1, source_target_pairs={{0,4},{1,5},{2,6},{3,7},{4,0},{5,1},{6,2},{7,3},{8,12},{9,13},{10,... | collective-permute-start | bytes 1572872 | tf_op jit(solution)/shard_map/ppermute | solution.py:306
  179.2 2.5 %collective-permute-start.26 = (bf16[2,256,512]{2,1,0:T(8,128)(2,1)}, bf16[2,256,512]{2,1,0:T(8,128)(2,1)}, u32[]{:S(2)}, u32[]{:S(2)}) collective-permute-start(bf16[2,256,512]{2,1,0:T(8,128)(2,1)} %collective-permute-done.23.refs_21_), channel_id=1, source_target_pairs={{0,4},{1,5},{2,6},{3,7},{4,0},{5,1},{6,2},{7,3},{8,12},{9,13},{10,... | collective-permute-start | bytes 1572872 | tf_op jit(solution)/shard_map/ppermute | solution.py:306
  194.1 3.6 %collective-permute-start.27 = (f32[1,32]{1,0:T(1,128)S(1)}, f32[1,32]{1,0:T(1,128)S(1)}, u32[]{:S(2)}, u32[]{:S(2)}) collective-permute-start(f32[1,32]{1,0:T(1,128)S(1)} %bitcast.220), channel_id=1, source_target_pairs={{0,1},{1,0},{2,3},{3,2},{4,5},{5,4},{6,7},{7,6},{8,9},{9,8},{10,11... | collective-permute-start | bytes 392 | tf_op jit(solution)/shard_map/ppermute | solution.py:306
  195.7 3.5 %collective-permute-start.28 = (f32[1,32]{1,0:T(1,128)S(1)}, f32[1,32]{1,0:T(1,128)S(1)}, u32[]{:S(2)}, u32[]{:S(2)}) collective-permute-start(f32[1,32]{1,0:T(1,128)S(1)} %bitcast.221), channel_id=1, source_target_pairs={{0,2},{1,3},{2,0},{3,1},{4,6},{5,7},{6,4},{7,5},{8,10},{9,11},{10,... | collective-permute-start | bytes 392 | tf_op jit(solution)/shard_map/ppermute | solution.py:306
  196.2 4.4 %collective-permute-start.29 = (f32[1,32]{1,0:T(1,128)S(1)}, f32[1,32]{1,0:T(1,128)S(1)}, u32[]{:S(2)}, u32[]{:S(2)}) collective-permute-start(f32[1,32]{1,0:T(1,128)S(1)} %bitcast.222), channel_id=1, source_target_pairs={{0,3},{1,2},{2,1},{3,0},{4,7},{5,6},{6,5},{7,4},{8,11},{9,10},{10,... | collective-permute-start | bytes 392 | tf_op jit(solution)/shard_map/ppermute | solution.py:306
  200.7 4.4 %collective-permute-start.30 = (f32[1,32]{1,0:T(1,128)S(1)}, f32[1,32]{1,0:T(1,128)S(1)}, u32[]{:S(2)}, u32[]{:S(2)}) collective-permute-start(f32[1,32]{1,0:T(1,128)S(1)} %add_add_fusion.1), channel_id=1, source_target_pairs={{0,16},{1,17},{2,18},{3,19},{4,20},{5,21},{6,22},{7,23},{8,24},{9,... | collective-permute-start | bytes 392 | tf_op jit(solution)/shard_map/ppermute | solution.py:306
  200.7 5.4 %collective-permute-start.31 = (f32[1,32]{1,0:T(1,128)S(1)}, f32[1,32]{1,0:T(1,128)S(1)}, u32[]{:S(2)}, u32[]{:S(2)}) collective-permute-start(f32[1,32]{1,0:T(1,128)S(1)} %add_add_fusion.1), channel_id=1, source_target_pairs={{0,8},{1,9},{2,10},{3,11},{4,12},{5,13},{6,14},{7,15},{8,16},{9,17... | collective-permute-start | bytes 392 | tf_op jit(solution)/shard_map/ppermute | solution.py:306
  203.4 3.5 %collective-permute-start.32 = (f32[1,32]{1,0:T(1,128)S(1)}, f32[1,32]{1,0:T(1,128)S(1)}, u32[]{:S(2)}, u32[]{:S(2)}) collective-permute-start(f32[1,32]{1,0:T(1,128)S(1)} %add_add_fusion.1), channel_id=1, source_target_pairs={{0,24},{1,25},{2,26},{3,27},{4,28},{5,29},{6,30},{7,31},{8,0},{9,1... | collective-permute-start | bytes 392 | tf_op jit(solution)/shard_map/ppermute | solution.py:306
  207.0 1.1 collective-permute-start.33
  (15 other events, 76.0 us)

commit v6 on v5

--- a/solution.py
+++ b/solution.py
@@ -527,10 +527,10 @@
         jnp.where(ids[:, None] == jnp.arange(total, dtype=jnp.int32)[None, :], sums[:, None], 0.0),
         axis=0,
     ).reshape(1, total)
+    rewards = tree_sum([rewards] + [turn(rewards, s) for s in range(1, planes)])
     rewards = (rewards + swap_in_plane(rewards, 1)) + (
         swap_in_plane(rewards, 2) + swap_in_plane(rewards, 3)
     )
-    rewards = tree_sum([rewards] + [turn(rewards, s) for s in range(1, planes)])
     own = own_scores(rewards, swap_core(rewards), pop_index * members_here, members_here, seq)
     return new_gate, new_up, own
 

time: 210 us -> 210 us (level)
  no operation moved by 1% of the time
where the time goes in v6:
time: 210 us; the launch traced here: 209 us
  waiting for transfers between devices  79.1 us (38%)
  starting transfers between devices  42.2 us (20%)
  Pallas kernels  36.6 us (17%)
  matrix products  20.1 us (10%)
  other arithmetic  16.8 us (8%)
  local copies, waits for them, and re-layouts  12.4 us (6%)
    ppermute x34, waiting for transfers between devices, send(): return lax.ppermute(value, AXES, pairs(move, keep))  79.1 us
    ppermute x34, starting transfers between devices, send(): return lax.ppermute(value, AXES, pairs(move, keep))  42.2 us
    pallas_call x3, Pallas kernels, product(): pl.pallas_call(lambda *refs: product_kernel(plan, counts, plane_of, seq,...  35.9 us
    dot_general x12, matrix products, on_vector(): lax.dot_general(rows, vector, (((1,), (1,)), ((), ())), preferred_element...  16.7 us
    slice x6, local copies, waits for them, and re-layouts, next_sends(): to_x, to_y, here = ([new_y[:half]], [new_x[half:seq]], None)  5.97 us
  transfers between devices with their start and end apart: 34, of which 20 were waited for; matrix products, arithmetic and copies ran while one was open for 21% of the time, Pallas kernels for 11%

profile of v6, /device:TPU:0, one launch (start us, length us, event | category | flops | bytes accessed | tf_op | source)
XLA Modules:
  0.0 208.9 jit_solution(10897343590779195562)
XLA Ops:
  0.7 1.3 dynamic-slice_bitcast_fusion
  2.0 3.1 %collective-permute-start = (s32[3,4]{1,0:T(4,128)S(1)}, s32[3,4]{1,0:T(4,128)S(1)}, u32[]{:S(2)}, u32[]{:S(2)}) collective-permute-start(s32[3,4]{1,0:T(4,128)S(1)} %pad_add_fusion.1), channel_id=1, source_target_pairs={{0,8},{1,9},{2,10},{3,11},{4,12},{5,13},{6,14},{7,15},{8,16},{9,17... | collective-permute-start | bytes 152 | tf_op jit(solution)/shard_map/ppermute | solution.py:306
  5.1 2.6 %collective-permute-start.1 = (s32[3,4]{1,0:T(4,128)S(1)}, s32[3,4]{1,0:T(4,128)S(1)}, u32[]{:S(2)}, u32[]{:S(2)}) collective-permute-start(s32[3,4]{1,0:T(4,128)S(1)} %pad_add_fusion.1), channel_id=1, source_target_pairs={{0,16},{1,17},{2,18},{3,19},{4,20},{5,21},{6,22},{7,23},{8,24},{9,... | collective-permute-start | bytes 152 | tf_op jit(solution)/shard_map/ppermute | solution.py:306
  7.7 1.3 collective-permute-start.2
  9.0 3.6 %collective-permute-start.4 = (bf16[128,4096]{1,0:T(8,128)(2,1)S(1)}, bf16[128,4096]{1,0:T(8,128)(2,1)}, u32[]{:S(2)}, u32[]{:S(2)}) collective-permute-start(bf16[128,4096]{1,0:T(8,128)(2,1)S(1)} %dynamic-slice_bitcast_fusion), channel_id=1, source_target_pairs={{0,8},{1,9},{2,10},{3,11},{4,12},{5,13},{6,14},{7,15},{8,16},{9,17... | collective-permute-start | bytes 3145736 | tf_op jit(solution)/shard_map/ppermute | solution.py:306
  12.6 1.3 collective-permute-start.5
  15.5 2.7 %fusion.130 = (bf16[4,1,4096]{2,1,0:T(2,128)(2,1)S(1)}, bf16[4,1,4096]{2,1,0:T(2,128)(2,1)S(1)}, bf16[4,1,4096]{2,1,0:T(2,128)(2,1)}, bf16[4,1,4096]{2,1,0:T(2,1...) fusion(s32[4096]{0:T(1024)S(1)} %iota_multiply_fusion, ...), kind=kLoop, calls=%fused_computation.194 | loop fusion | flops 1966080 | bytes 278656 | tf_op jit(solution)/shard_map/convert_element_type | solution.py:390
  18.2 1.6 convolution_bitcast_fusion
  19.9 1.6 convolution_bitcast_fusion.1
  21.5 2.2 %convolution_bitcast_fusion.2 = f32[128,2]{0,1:T(2,128)} fusion(bf16[4,128,4096]{2,1,0:T(8,128)(2,1)} %param.7, bf16[4,1,4096]{2,1,0:T(2,128)(2,1)S(1)} %get-tuple-element.181, bf16[4,1,4096]{2,1,0:T(2,128)(2,1)S(1)} %get-tuple-element.180), kind=kOutput, calls=%fused_computation.12 | convolution fusion | flops 2129920 | bytes 1115136 | tf_op jit(solution)/shard_map/dot_general | solution.py:395
  23.7 2.2 %convolution_bitcast_fusion.3 = f32[128,2]{0,1:T(2,128)} fusion(bf16[4,128,4096]{2,1,0:T(8,128)(2,1)} %param.7, bf16[4,1,4096]{2,1,0:T(2,128)(2,1)S(1)} %get-tuple-element.181, bf16[4,1,4096]{2,1,0:T(2,128)(2,1)S(1)} %get-tuple-element.180), kind=kOutput, calls=%fused_computation.13 | convolution fusion | flops 2129920 | bytes 1115136 | tf_op jit(solution)/shard_map/dot_general | solution.py:395
  28.5 2.6 %add_convert_fusion = bf16[512,2048]{1,0:T(8,128)(2,1)S(1)} fusion(bf16[512,2048]{1,0:T(8,128)(2,1)} %param.9, s32[32]{0:T(128)S(1)} %get-tuple-element.214, s32[2048]{0:T(1024)S(1)} %add_multiply_fusion, s32[32]{0:T(128)S(1)} %get-tuple-element.213, f32[32]{0:T(128)S(1)} %reshape.1829, s32[512]{0:T(512)S(1)} %add_multiply_fusion.2), kind=kOutput, calls=%fused_computation | convolution fusion | flops 72531968 | bytes 4204928 | tf_op jit(solution)/shard_map/dot_general | solution.py:47
  33.2 5.2 %collective-permute-done.5 = bf16[128,4096]{1,0:T(8,128)(2,1)} collective-permute-done((bf16[128,4096]{1,0:T(8,128)(2,1)S(1)}, bf16[128,4096]{1,0:T(8,128)(2,1)}, u32[]{:S(2)}, u32[]{:S(2)}) %collective-permute-start.5) | collective-permute-done | bytes 1048608 | tf_op jit(solution)/shard_map/ppermute | solution.py:306
  38.4 1.3 broadcast_select_fusion.refs_2_
  39.7 1.6 collective-permute-start.8
  41.3 1.5 collective-permute-start.9
  42.8 1.6 collective-permute-start.6
  44.4 1.3 collective-permute-start.7
  50.0 12.6 %collective-permute-done.8.refs_3_ = bf16[128,4096]{1,0:T(8,128)(2,1)S(1)} collective-permute-done((bf16[128,4096]{1,0:T(8,128)(2,1)S(1)}, bf16[128,4096]{1,0:T(8,128)(2,1)S(1)}, u32[]{:S(2)}, u32[]{:S(2)}) %collective-permute-start.8) | collective-permute-done | bytes 1048608 | tf_op jit(solution)/shard_map/ppermute | solution.py:306
  63.9 5.1 %collective-permute-done.7 = bf16[128,4096]{1,0:T(8,128)(2,1)} collective-permute-done((bf16[128,4096]{1,0:T(8,128)(2,1)}, bf16[128,4096]{1,0:T(8,128)(2,1)}, u32[]{:S(2)}, u32[]{:S(2)}) %collective-permute-start.7) | collective-permute-done | bytes 1048608 | tf_op jit(solution)/shard_map/ppermute | solution.py:306
  69.0 1.4 select_select_fusion.1.refs_7_
  70.4 2.0 pad_maximum_fusion
  74.2 1.3 collective-permute-start.12
  76.5 23.6 %collective-permute-done.12 = bf16[128,4096]{1,0:T(8,128)(2,1)} collective-permute-done((bf16[128,4096]{1,0:T(8,128)(2,1)}, bf16[128,4096]{1,0:T(8,128)(2,1)}, u32[]{:S(2)}, u32[]{:S(2)}) %collective-permute-start.12) | collective-permute-done | bytes 1048608 | tf_op jit(solution)/shard_map/ppermute | solution.py:306
  100.0 5.3 %collective-permute-done.13.refs_5_ = bf16[192,4096]{1,0:T(8,128)(2,1)} collective-permute-done((bf16[192,4096]{1,0:T(8,128)(2,1)}, bf16[192,4096]{1,0:T(8,128)(2,1)}, u32[]{:S(2)}, u32[]{:S(2)}) %collective-permute-start.13) | collective-permute-done | bytes 1572896 | tf_op jit(solution)/shard_map/ppermute | solution.py:306
  105.6 1.4 select_select_fusion.refs_10_
  112.2 2.0 pad_maximum_fusion.2
  114.1 6.1 %collective-permute-done.15.refs_10_.refs_13_.refs_15_ = bf16[2,512,512]{2,1,0:T(8,128)(2,1)} collective-permute-done((bf16[2,512,512]{2,1,0:T(8,128)(2,1)}, bf16[2,512,512]{2,1,0:T(8,128)(2,1)}, u32[]{:S(2)}, u32[]{:S(2)}) %collective-permute-start.15) | collective-permute-done | bytes 1048608 | tf_op jit(solution)/shard_map/ppermute | solution.py:306
  120.2 1.5 collective-permute-start.16
  121.7 1.5 collective-permute-start.17
  123.9 4.0 %collective-permute-start.19 = (bf16[2,256,512]{2,1,0:T(8,128)(2,1)}, bf16[2,256,512]{2,1,0:T(8,128)(2,1)}, u32[]{:S(2)}, u32[]{:S(2)}) collective-permute-start(bf16[2,256,512]{2,1,0:T(8,128)(2,1)} %pad_maximum_fusion.7), channel_id=1, source_target_pairs={{0,24},{1,25},{2,26},{3,27},{4,28},{5,29},{6,30},{7,31},{8,0},{9,1... | collective-permute-start | bytes 1572872 | tf_op jit(solution)/shard_map/ppermute | solution.py:306
  129.1 1.3 fusion.19
  130.4 1.6 fusion.7
  132.1 1.6 fusion.9
  135.4 10.4 %shard_map.94.refs_17_ = bf16[1408,1024]{1,0:T(8,128)(2,1)} custom-call(s32[8]{0:T(128)S(1)} %stack.218.refs_0_, bf16[512,4096]{1,0:T(8,128)(2,1)} %bitcast.202, bf16[128,4096]{1,0:T(8,128)(2,1)} %copy-done.2, bf16[128,4096]{1,0:T(8,128)(2,1)} %copy-done.4, bf16[128,4096]{1,0:T(8,128)(2,1)} %copy-done.6, bf16[192,4096]{1,0:T(8,128)(2,1)} %collective-permute-done.13.refs_5_, ...), custom_call_target="tpu_custom_call" | custom-call | flops 1 | bytes 1 | tf_op jit(solution)/shard_map/pallas_call | solution.py:240
  145.8 8.2 %collective-permute-done.16.refs_8_ = bf16[192,4096]{1,0:T(8,128)(2,1)} collective-permute-done((bf16[192,4096]{1,0:T(8,128)(2,1)}, bf16[192,4096]{1,0:T(8,128)(2,1)}, u32[]{:S(2)}, u32[]{:S(2)}) %collective-permute-start.16) | collective-permute-done | bytes 1572896 | tf_op jit(solution)/shard_map/ppermute | solution.py:306
  155.3 1.9 slice.158
  157.1 1.9 slice.159
  159.0 2.1 %collective-permute-done.19.refs_19_ = bf16[2,256,512]{2,1,0:T(8,128)(2,1)} collective-permute-done((bf16[2,256,512]{2,1,0:T(8,128)(2,1)}, bf16[2,256,512]{2,1,0:T(8,128)(2,1)}, u32[]{:S(2)}, u32[]{:S(2)}) %collective-permute-start.19) | collective-permute-done | bytes 524320 | tf_op jit(solution)/shard_map/ppermute | solution.py:306
  162.2 3.6 %collective-permute-start.23 = (bf16[2,256,512]{2,1,0:T(8,128)(2,1)}, bf16[2,256,512]{2,1,0:T(8,128)(2,1)}, u32[]{:S(2)}, u32[]{:S(2)}) collective-permute-start(bf16[2,256,512]{2,1,0:T(8,128)(2,1)} %pad_maximum_fusion.8), channel_id=1, source_target_pairs={{0,24},{1,25},{2,26},{3,27},{4,28},{5,29},{6,30},{7,31},{8,0},{9,1... | collective-permute-start | bytes 1572872 | tf_op jit(solution)/shard_map/ppermute | solution.py:306
  165.9 13.2 %shard_map.95.refs_23_ = bf16[1920,1024]{1,0:T(8,128)(2,1)} custom-call(s32[12]{0:T(128)S(1)} %stack.219.refs_0_, bf16[512,4096]{1,0:T(8,128)(2,1)} %bitcast.203, bf16[128,4096]{1,0:T(8,128)(2,1)} %copy-done.2, bf16[128,4096]{1,0:T(8,128)(2,1)} %copy-done.4, bf16[128,4096]{1,0:T(8,128)(2,1)} %copy-done.6, bf16[192,4096]{1,0:T(8,128)(2,1)} %collective-permute-done.13.refs_5_, ...), custom_call_target="tpu_custom_call" | custom-call | flops 1 | bytes 1 | tf_op jit(solution)/shard_map/pallas_call | solution.py:240
  180.0 1.6 collective-permute-done.26.refs_22_
  181.6 12.2 %shard_map.96 = f32[16,8,512]{2,1,0:T(8,128)S(1)} custom-call(s32[20]{0:T(128)S(1)} %stack.194.refs_0_, bf16[512,4096]{1,0:T(8,128)(2,1)} %bitcast.204, bf16[128,4096]{1,0:T(8,128)(2,1)} %copy-done.2, bf16[128,4096]{1,0:T(8,128)(2,1)} %copy-done.4, bf16[128,4096]{1,0:T(8,128)(2,1)} %copy-done.6, bf16[192,4096]{1,0:T(8,128)(2,1)} %collective-permute-done.13.refs_5_, ...), custom_call_target="tpu_custom_call" | custom-call | flops 1 | bytes 1 | tf_op jit(solution)/shard_map/pallas_call | solution.py:240
  194.2 2.8 %collective-permute-start.28 = (f32[1,32]{1,0:T(1,128)S(1)}, f32[1,32]{1,0:T(1,128)S(1)}, u32[]{:S(2)}, u32[]{:S(2)}) collective-permute-start(f32[1,32]{1,0:T(1,128)S(1)} %bitcast.221), channel_id=1, source_target_pairs={{0,8},{1,9},{2,10},{3,11},{4,12},{5,13},{6,14},{7,15},{8,16},{9,17... | collective-permute-start | bytes 392 | tf_op jit(solution)/shard_map/ppermute | solution.py:306
  200.5 1.5 collective-permute-start.30
  202.5 1.5 collective-permute-start.32
  204.1 1.5 collective-permute-done.31
  205.6 1.4 collective-permute-done.32
  (166 shorter events, 32.5 us)
Async XLA Ops:
  2.0 13.1 %collective-permute-start = (s32[3,4]{1,0:T(4,128)S(1)}, s32[3,4]{1,0:T(4,128)S(1)}, u32[]{:S(2)}, u32[]{:S(2)}) collective-permute-start(s32[3,4]{1,0:T(4,128)S(1)} %pad_add_fusion.1), channel_id=1, source_target_pairs={{0,8},{1,9},{2,10},{3,11},{4,12},{5,13},{6,14},{7,15},{8,16},{9,17... | collective-permute-start | bytes 152 | tf_op jit(solution)/shard_map/ppermute | solution.py:306
  5.1 10.0 %collective-permute-start.1 = (s32[3,4]{1,0:T(4,128)S(1)}, s32[3,4]{1,0:T(4,128)S(1)}, u32[]{:S(2)}, u32[]{:S(2)}) collective-permute-start(s32[3,4]{1,0:T(4,128)S(1)} %pad_add_fusion.1), channel_id=1, source_target_pairs={{0,16},{1,17},{2,18},{3,19},{4,20},{5,21},{6,22},{7,23},{8,24},{9,... | collective-permute-start | bytes 152 | tf_op jit(solution)/shard_map/ppermute | solution.py:306
  7.7 7.4 %collective-permute-start.2 = (s32[3,4]{1,0:T(4,128)S(1)}, s32[3,4]{1,0:T(4,128)S(1)}, u32[]{:S(2)}, u32[]{:S(2)}) collective-permute-start(s32[3,4]{1,0:T(4,128)S(1)} %pad_add_fusion.1), channel_id=1, source_target_pairs={{0,24},{1,25},{2,26},{3,27},{4,28},{5,29},{6,30},{7,31},{8,0},{9,1... | collective-permute-start | bytes 152 | tf_op jit(solution)/shard_map/ppermute | solution.py:306
  9.0 24.1 %collective-permute-start.4 = (bf16[128,4096]{1,0:T(8,128)(2,1)S(1)}, bf16[128,4096]{1,0:T(8,128)(2,1)}, u32[]{:S(2)}, u32[]{:S(2)}) collective-permute-start(bf16[128,4096]{1,0:T(8,128)(2,1)S(1)} %dynamic-slice_bitcast_fusion), channel_id=1, source_target_pairs={{0,8},{1,9},{2,10},{3,11},{4,12},{5,13},{6,14},{7,15},{8,16},{9,17... | collective-permute-start | bytes 3145736 | tf_op jit(solution)/shard_map/ppermute | solution.py:306
  12.6 25.8 %collective-permute-start.5 = (bf16[128,4096]{1,0:T(8,128)(2,1)S(1)}, bf16[128,4096]{1,0:T(8,128)(2,1)}, u32[]{:S(2)}, u32[]{:S(2)}) collective-permute-start(bf16[128,4096]{1,0:T(8,128)(2,1)S(1)} %dynamic-slice_bitcast_fusion), channel_id=1, source_target_pairs={{8,0},{9,1},{10,2},{11,3},{12,4},{13,5},{14,6},{15,7},{16,8},{17,9... | collective-permute-start | bytes 3145736 | tf_op jit(solution)/shard_map/ppermute | solution.py:306
  26.0 1.8 collective-permute-start.3
  31.1 14.9 %copy-start.10 = (bf16[512,2048]{1,0:T(8,128)(2,1)}, bf16[512,2048]{1,0:T(8,128)(2,1)S(1)}, u32[]{:S(2)}) copy-start(bf16[512,2048]{1,0:T(8,128)(2,1)S(1)} %add_convert_fusion) | copy-start | bytes 6291460
  32.0 14.0 %copy-start.11 = (bf16[512,2048]{1,0:T(8,128)(2,1)}, bf16[512,2048]{1,0:T(8,128)(2,1)S(1)}, u32[]{:S(2)}) copy-start(bf16[512,2048]{1,0:T(8,128)(2,1)S(1)} %add_convert_fusion.1) | copy-start | bytes 6291460
  32.5 13.7 %copy-start.8 = (bf16[2,512,512]{2,1,0:T(8,128)(2,1)}, bf16[2,512,512]{2,1,0:T(8,128)(2,1)S(1)}, u32[]{:S(2)}) copy-start(bf16[2,512,512]{2,1,0:T(8,128)(2,1)S(1)} %pad_maximum_fusion.4.refs_8_.refs_11_.refs_13_) | copy-start | bytes 3145732
  32.5 13.3 %copy-start.16 = (bf16[4,1,4096]{2,1,0:T(2,128)(2,1)S(1)}, bf16[4,1,4096]{2,1,0:T(2,128)(2,1)}, u32[]{:S(2)}) copy-start(bf16[4,1,4096]{2,1,0:T(2,128)(2,1)} %get-tuple-element.178) | copy-start | bytes 98308
  32.5 13.3 %copy-start.17 = (bf16[4,1,4096]{2,1,0:T(2,128)(2,1)S(1)}, bf16[4,1,4096]{2,1,0:T(2,128)(2,1)}, u32[]{:S(2)}) copy-start(bf16[4,1,4096]{2,1,0:T(2,128)(2,1)} %get-tuple-element.179) | copy-start | bytes 98308
  32.5 13.3 %copy-start.19 = (bf16[1,2,4096]{2,1,0:T(2,128)(2,1)S(1)}, bf16[1,2,4096]{2,1,0:T(2,128)(2,1)}, u32[]{:S(2)}) copy-start(bf16[1,2,4096]{2,1,0:T(2,128)(2,1)} %slice_maximum_fusion) | copy-start | bytes 49156
  32.5 17.5 %collective-permute-start.10 = (bf16[2,512,512]{2,1,0:T(8,128)(2,1)S(1)}, bf16[2,512,512]{2,1,0:T(8,128)(2,1)S(1)}, u32[]{:S(2)}, u32[]{:S(2)}) collective-permute-start(bf16[2,512,512]{2,1,0:T(8,128)(2,1)S(1)} %pad_maximum_fusion.4.refs_8_.refs_11_.refs_13_), channel_id=1, source_target_pairs={{0,4},{1,5},{2,6},{3,7},{4,0},{5,1},{6,2},{7,3},{8,12},{9,13},{10,... | collective-permute-start | bytes 3145736 | tf_op jit(solution)/shard_map/ppermute | solution.py:306
  39.7 22.9 %collective-permute-start.8 = (bf16[128,4096]{1,0:T(8,128)(2,1)S(1)}, bf16[128,4096]{1,0:T(8,128)(2,1)S(1)}, u32[]{:S(2)}, u32[]{:S(2)}) collective-permute-start(bf16[128,4096]{1,0:T(8,128)(2,1)S(1)} %broadcast_select_fusion.refs_2_), channel_id=1, source_target_pairs={{0,1},{1,0},{2,3},{3,2},{4,5},{5,4},{6,7},{7,6},{8,9},{9,8},{10,11... | collective-permute-start | bytes 3145736 | tf_op jit(solution)/shard_map/ppermute | solution.py:306
  41.3 22.6 %collective-permute-start.9 = (bf16[128,4096]{1,0:T(8,128)(2,1)S(1)}, bf16[128,4096]{1,0:T(8,128)(2,1)S(1)}, u32[]{:S(2)}, u32[]{:S(2)}) collective-permute-start(bf16[128,4096]{1,0:T(8,128)(2,1)S(1)} %broadcast_select_fusion.refs_2_), channel_id=1, source_target_pairs={{0,2},{1,3},{2,0},{3,1},{4,6},{5,7},{6,4},{7,5},{8,10},{9,11},{10,... | collective-permute-start | bytes 3145736 | tf_op jit(solution)/shard_map/ppermute | solution.py:306
  42.8 21.1 %collective-permute-start.6 = (bf16[128,4096]{1,0:T(8,128)(2,1)}, bf16[128,4096]{1,0:T(8,128)(2,1)}, u32[]{:S(2)}, u32[]{:S(2)}) collective-permute-start(bf16[128,4096]{1,0:T(8,128)(2,1)} %collective-permute-done.4), channel_id=1, source_target_pairs={{8,16},{9,17},{10,18},{11,19},{12,20},{13,21},{14,22},{15,23},{16,... | collective-permute-start | bytes 3145736 | tf_op jit(solution)/shard_map/ppermute | solution.py:306
  44.4 24.5 %collective-permute-start.7 = (bf16[128,4096]{1,0:T(8,128)(2,1)}, bf16[128,4096]{1,0:T(8,128)(2,1)}, u32[]{:S(2)}, u32[]{:S(2)}) collective-permute-start(bf16[128,4096]{1,0:T(8,128)(2,1)} %collective-permute-done.5), channel_id=1, source_target_pairs={{8,0},{9,1},{10,2},{11,3},{12,4},{13,5},{14,6},{15,7},{16,8},{17,9... | collective-permute-start | bytes 3145736 | tf_op jit(solution)/shard_map/ppermute | solution.py:306
  72.4 32.9 %collective-permute-start.13 = (bf16[192,4096]{1,0:T(8,128)(2,1)}, bf16[192,4096]{1,0:T(8,128)(2,1)}, u32[]{:S(2)}, u32[]{:S(2)}) collective-permute-start(bf16[192,4096]{1,0:T(8,128)(2,1)} %get-tuple-element.175), channel_id=1, source_target_pairs={{0,1},{1,0},{2,3},{3,2},{4,5},{5,4},{6,7},{7,6},{8,9},{9,8},{10,11... | collective-permute-start | bytes 4718600 | tf_op jit(solution)/shard_map/ppermute | solution.py:306
  73.0 32.6 %collective-permute-start.14 = (bf16[192,4096]{1,0:T(8,128)(2,1)}, bf16[192,4096]{1,0:T(8,128)(2,1)}, u32[]{:S(2)}, u32[]{:S(2)}) collective-permute-start(bf16[192,4096]{1,0:T(8,128)(2,1)} %get-tuple-element.174), channel_id=1, source_target_pairs={{0,2},{1,3},{2,0},{3,1},{4,6},{5,7},{6,4},{7,5},{8,10},{9,11},{10,... | collective-permute-start | bytes 4718600 | tf_op jit(solution)/shard_map/ppermute | solution.py:306
  73.5 3.0 %collective-permute-start.11 = (bf16[128,4096]{1,0:T(8,128)(2,1)}, bf16[128,4096]{1,0:T(8,128)(2,1)S(1)}, u32[]{:S(2)}, u32[]{:S(2)}) collective-permute-start(bf16[128,4096]{1,0:T(8,128)(2,1)} %collective-permute-done.6), channel_id=1, source_target_pairs={{16,24},{17,25},{18,26},{19,27},{20,28},{21,29},{22,30},{23,31}} | collective-permute-start | bytes 3145736 | tf_op jit(solution)/shard_map/ppermute | solution.py:306
  74.2 25.8 %collective-permute-start.12 = (bf16[128,4096]{1,0:T(8,128)(2,1)}, bf16[128,4096]{1,0:T(8,128)(2,1)}, u32[]{:S(2)}, u32[]{:S(2)}) collective-permute-start(bf16[128,4096]{1,0:T(8,128)(2,1)} %collective-permute-done.7), channel_id=1, source_target_pairs={{8,0},{9,1},{10,2},{11,3},{12,4},{13,5},{14,6},{15,7}} | collective-permute-start | bytes 3145736 | tf_op jit(solution)/shard_map/ppermute | solution.py:306
  75.6 31.4 %copy-start.7 = (bf16[128,4096]{1,0:T(8,128)(2,1)S(1)}, bf16[128,4096]{1,0:T(8,128)(2,1)}, u32[]{:S(2)}) copy-start(bf16[128,4096]{1,0:T(8,128)(2,1)} %copy-done.6) | copy-start | bytes 3145732
  75.6 44.6 %collective-permute-start.15 = (bf16[2,512,512]{2,1,0:T(8,128)(2,1)}, bf16[2,512,512]{2,1,0:T(8,128)(2,1)}, u32[]{:S(2)}, u32[]{:S(2)}) collective-permute-start(bf16[2,512,512]{2,1,0:T(8,128)(2,1)} %pad_maximum_fusion.6), channel_id=1, source_target_pairs={{0,16},{1,17},{2,18},{3,19},{4,20},{5,21},{6,22},{7,23},{8,24},{9,... | collective-permute-start | bytes 3145736 | tf_op jit(solution)/shard_map/ppermute | solution.py:306
  112.1 11.3 %copy-start.1 = (bf16[128,4096]{1,0:T(8,128)(2,1)S(1)}, bf16[128,4096]{1,0:T(8,128)(2,1)}, u32[]{:S(2)}) copy-start(bf16[128,4096]{1,0:T(8,128)(2,1)} %copy-done) | copy-start | bytes 3145732
  112.1 11.3 %copy-start.13 = (bf16[4,1,4096]{2,1,0:T(2,128)(2,1)S(1)}, bf16[4,1,4096]{2,1,0:T(2,128)(2,1)}, u32[]{:S(2)}) copy-start(bf16[4,1,4096]{2,1,0:T(2,128)(2,1)} %copy-done.12) | copy-start | bytes 98308
  112.1 11.3 %copy-start.15 = (bf16[4,1,4096]{2,1,0:T(2,128)(2,1)S(1)}, bf16[4,1,4096]{2,1,0:T(2,128)(2,1)}, u32[]{:S(2)}) copy-start(bf16[4,1,4096]{2,1,0:T(2,128)(2,1)} %copy-done.14) | copy-start | bytes 98308
  120.2 33.8 %collective-permute-start.16 = (bf16[192,4096]{1,0:T(8,128)(2,1)}, bf16[192,4096]{1,0:T(8,128)(2,1)}, u32[]{:S(2)}, u32[]{:S(2)}) collective-permute-start(bf16[192,4096]{1,0:T(8,128)(2,1)} %get-tuple-element.113), channel_id=1, source_target_pairs={{0,1},{1,0},{2,3},{3,2},{4,5},{5,4},{6,7},{7,6},{8,9},{9,8},{10,11... | collective-permute-start | bytes 4718600 | tf_op jit(solution)/shard_map/ppermute | solution.py:306
  121.7 33.6 %collective-permute-start.17 = (bf16[192,4096]{1,0:T(8,128)(2,1)}, bf16[192,4096]{1,0:T(8,128)(2,1)}, u32[]{:S(2)}, u32[]{:S(2)}) collective-permute-start(bf16[192,4096]{1,0:T(8,128)(2,1)} %get-tuple-element.114), channel_id=1, source_target_pairs={{0,2},{1,3},{2,0},{3,1},{4,6},{5,7},{6,4},{7,5},{8,10},{9,11},{10,... | collective-permute-start | bytes 4718600 | tf_op jit(solution)/shard_map/ppermute | solution.py:306
  123.3 12.1 %collective-permute-start.20 = (bf16[2,512,512]{2,1,0:T(8,128)(2,1)}, bf16[2,512,512]{2,1,0:T(8,128)(2,1)S(1)}, u32[]{:S(2)}, u32[]{:S(2)}) collective-permute-start(bf16[2,512,512]{2,1,0:T(8,128)(2,1)} %collective-permute-done.15.refs_10_.refs_13_.refs_15_), channel_id=1, source_target_pairs={{0,4},{1,5},{2,6},{3,7},{4,0},{5,1},{6,2},{7,3},{8,12},{9,13},{10,... | collective-permute-start | bytes 3145736 | tf_op jit(solution)/shard_map/ppermute | solution.py:306
  123.3 37.8 %collective-permute-start.18 = (bf16[2,512,512]{2,1,0:T(8,128)(2,1)}, bf16[2,512,512]{2,1,0:T(8,128)(2,1)}, u32[]{:S(2)}, u32[]{:S(2)}) collective-permute-start(bf16[2,512,512]{2,1,0:T(8,128)(2,1)} %pad_maximum_fusion.5), channel_id=1, source_target_pairs={{0,8},{1,9},{2,10},{3,11},{4,12},{5,13},{6,14},{7,15},{8,16},{9,17... | collective-permute-start | bytes 3145736 | tf_op jit(solution)/shard_map/ppermute | solution.py:306
  123.8 9.9 %copy-start.22 = (f32[128,2]{0,1:T(2,128)S(1)}, f32[128,2]{0,1:T(2,128)}, u32[]{:S(2)}) copy-start(f32[128,2]{0,1:T(2,128)} %fusion.171) | copy-start | bytes 3076
  123.8 9.9 %copy-start.23 = (f32[128,2]{0,1:T(2,128)S(1)}, f32[128,2]{0,1:T(2,128)}, u32[]{:S(2)}) copy-start(f32[128,2]{0,1:T(2,128)} %fusion.174) | copy-start | bytes 3076
  123.8 9.9 %copy-start.24 = (f32[128,2]{0,1:T(2,128)S(1)}, f32[128,2]{0,1:T(2,128)}, u32[]{:S(2)}) copy-start(f32[128,2]{0,1:T(2,128)} %fusion.177) | copy-start | bytes 3076
  123.9 37.3 %collective-permute-start.19 = (bf16[2,256,512]{2,1,0:T(8,128)(2,1)}, bf16[2,256,512]{2,1,0:T(8,128)(2,1)}, u32[]{:S(2)}, u32[]{:S(2)}) collective-permute-start(bf16[2,256,512]{2,1,0:T(8,128)(2,1)} %pad_maximum_fusion.7), channel_id=1, source_target_pairs={{0,24},{1,25},{2,26},{3,27},{4,28},{5,29},{6,30},{7,31},{8,0},{9,1... | collective-permute-start | bytes 1572872 | tf_op jit(solution)/shard_map/ppermute | solution.py:306
  145.8 20.0 %copy-start.18 = (f32[2,5,512]{2,0,1:T(2,128)S(1)}, f32[2,5,512]{2,0,1:T(2,128)}, u32[]{:S(2)}) copy-start(f32[2,5,512]{2,0,1:T(2,128)} %copy.82) | copy-start | bytes 61444
  161.1 4.8 %collective-permute-start.24 = (bf16[2,512,512]{2,1,0:T(8,128)(2,1)}, bf16[2,512,512]{2,1,0:T(8,128)(2,1)}, u32[]{:S(2)}, u32[]{:S(2)}) collective-permute-start(bf16[2,512,512]{2,1,0:T(8,128)(2,1)} %collective-permute-done.18.refs_15_.refs_17_), channel_id=1, source_target_pairs={{0,4},{1,5},{2,6},{3,7},{4,0},{5,1},{6,2},{7,3},{8,12},{9,13},{10,... | collective-permute-start | bytes 3145736 | tf_op jit(solution)/shard_map/ppermute | solution.py:306
  161.1 18.0 %collective-permute-start.21 = (bf16[64,4096]{1,0:T(8,128)(2,1)}, bf16[64,4096]{1,0:T(8,128)(2,1)}, u32[]{:S(2)}, u32[]{:S(2)}) collective-permute-start(bf16[64,4096]{1,0:T(8,128)(2,1)} %slice.158), channel_id=1, source_target_pairs={{0,1},{1,0},{2,3},{3,2},{4,5},{5,4},{6,7},{7,6},{8,9},{9,8},{10,11... | collective-permute-start | bytes 1572872 | tf_op jit(solution)/shard_map/ppermute | solution.py:306
  161.7 17.5 %collective-permute-start.22 = (bf16[64,4096]{1,0:T(8,128)(2,1)}, bf16[64,4096]{1,0:T(8,128)(2,1)}, u32[]{:S(2)}, u32[]{:S(2)}) collective-permute-start(bf16[64,4096]{1,0:T(8,128)(2,1)} %slice.159), channel_id=1, source_target_pairs={{0,2},{1,3},{2,0},{3,1},{4,6},{5,7},{6,4},{7,5},{8,10},{9,11},{10,... | collective-permute-start | bytes 1572872 | tf_op jit(solution)/shard_map/ppermute | solution.py:306
  162.2 17.0 %collective-permute-start.23 = (bf16[2,256,512]{2,1,0:T(8,128)(2,1)}, bf16[2,256,512]{2,1,0:T(8,128)(2,1)}, u32[]{:S(2)}, u32[]{:S(2)}) collective-permute-start(bf16[2,256,512]{2,1,0:T(8,128)(2,1)} %pad_maximum_fusion.8), channel_id=1, source_target_pairs={{0,24},{1,25},{2,26},{3,27},{4,28},{5,29},{6,30},{7,31},{8,0},{9,1... | collective-permute-start | bytes 1572872 | tf_op jit(solution)/shard_map/ppermute | solution.py:306
  165.8 13.4 %collective-permute-start.25 = (bf16[2,256,512]{2,1,0:T(8,128)(2,1)}, bf16[2,256,512]{2,1,0:T(8,128)(2,1)S(1)}, u32[]{:S(2)}, u32[]{:S(2)}) collective-permute-start(bf16[2,256,512]{2,1,0:T(8,128)(2,1)} %collective-permute-done.19.refs_19_), channel_id=1, source_target_pairs={{0,4},{1,5},{2,6},{3,7},{4,0},{5,1},{6,2},{7,3},{8,12},{9,13},{10,... | collective-permute-start | bytes 1572872 | tf_op jit(solution)/shard_map/ppermute | solution.py:306
  179.2 2.5 %collective-permute-start.26 = (bf16[2,256,512]{2,1,0:T(8,128)(2,1)}, bf16[2,256,512]{2,1,0:T(8,128)(2,1)}, u32[]{:S(2)}, u32[]{:S(2)}) collective-permute-start(bf16[2,256,512]{2,1,0:T(8,128)(2,1)} %collective-permute-done.23.refs_21_), channel_id=1, source_target_pairs={{0,4},{1,5},{2,6},{3,7},{4,0},{5,1},{6,2},{7,3},{8,12},{9,13},{10,... | collective-permute-start | bytes 1572872 | tf_op jit(solution)/shard_map/ppermute | solution.py:306
  194.1 4.5 %collective-permute-start.27 = (f32[1,32]{1,0:T(1,128)S(1)}, f32[1,32]{1,0:T(1,128)S(1)}, u32[]{:S(2)}, u32[]{:S(2)}) collective-permute-start(f32[1,32]{1,0:T(1,128)S(1)} %bitcast.220), channel_id=1, source_target_pairs={{0,16},{1,17},{2,18},{3,19},{4,20},{5,21},{6,22},{7,23},{8,24},{9,... | collective-permute-start | bytes 392 | tf_op jit(solution)/shard_map/ppermute | solution.py:306
  194.2 5.4 %collective-permute-start.28 = (f32[1,32]{1,0:T(1,128)S(1)}, f32[1,32]{1,0:T(1,128)S(1)}, u32[]{:S(2)}, u32[]{:S(2)}) collective-permute-start(f32[1,32]{1,0:T(1,128)S(1)} %bitcast.221), channel_id=1, source_target_pairs={{0,8},{1,9},{2,10},{3,11},{4,12},{5,13},{6,14},{7,15},{8,16},{9,17... | collective-permute-start | bytes 392 | tf_op jit(solution)/shard_map/ppermute | solution.py:306
  197.0 3.5 %collective-permute-start.29 = (f32[1,32]{1,0:T(1,128)S(1)}, f32[1,32]{1,0:T(1,128)S(1)}, u32[]{:S(2)}, u32[]{:S(2)}) collective-permute-start(f32[1,32]{1,0:T(1,128)S(1)} %bitcast.222), channel_id=1, source_target_pairs={{0,24},{1,25},{2,26},{3,27},{4,28},{5,29},{6,30},{7,31},{8,0},{9,1... | collective-permute-start | bytes 392 | tf_op jit(solution)/shard_map/ppermute | solution.py:306
  200.5 3.5 %collective-permute-start.30 = (f32[1,32]{1,0:T(1,128)S(1)}, f32[1,32]{1,0:T(1,128)S(1)}, u32[]{:S(2)}, u32[]{:S(2)}) collective-permute-start(f32[1,32]{1,0:T(1,128)S(1)} %add_add_fusion.1), channel_id=1, source_target_pairs={{0,1},{1,0},{2,3},{3,2},{4,5},{5,4},{6,7},{7,6},{8,9},{9,8},{10,11... | collective-permute-start | bytes 392 | tf_op jit(solution)/shard_map/ppermute | solution.py:306
  202.0 3.5 %collective-permute-start.31 = (f32[1,32]{1,0:T(1,128)S(1)}, f32[1,32]{1,0:T(1,128)S(1)}, u32[]{:S(2)}, u32[]{:S(2)}) collective-permute-start(f32[1,32]{1,0:T(1,128)S(1)} %add_add_fusion.1), channel_id=1, source_target_pairs={{0,2},{1,3},{2,0},{3,1},{4,6},{5,7},{6,4},{7,5},{8,10},{9,11},{10,... | collective-permute-start | bytes 392 | tf_op jit(solution)/shard_map/ppermute | solution.py:306
  202.5 4.4 %collective-permute-start.32 = (f32[1,32]{1,0:T(1,128)S(1)}, f32[1,32]{1,0:T(1,128)S(1)}, u32[]{:S(2)}, u32[]{:S(2)}) collective-permute-start(f32[1,32]{1,0:T(1,128)S(1)} %add_add_fusion.1), channel_id=1, source_target_pairs={{0,3},{1,2},{2,1},{3,0},{4,7},{5,6},{6,5},{7,4},{8,11},{9,10},{10,... | collective-permute-start | bytes 392 | tf_op jit(solution)/shard_map/ppermute | solution.py:306
  207.0 1.1 collective-permute-start.33
  (15 other events, 76.0 us)
